TPU v7x, 768 devices: a whole 4x8x12 slice. The times are simulated.
768 devices in a mesh: chord: 48 (over y_hi, z, core), span: 16 (over y_lo, x).
Axes of the slice: x: 4, y: 8 (y_hi: 2, y_lo: 4; y = y_hi * 4 + y_lo), z: 12, core: 2. Of those that a mesh axis runs over, the one named last changes fastest.
Arguments:
- velocity: float32 [3, 192, 64, 1024], P(None, 'chord', 'span'), may hold values from -6 to 6
- pressure: float32 [192, 64, 1024], P('chord', 'span'), may hold values from -6 to 6
- viscosity: float32 [192, 64, 1024], P('chord', 'span'), may hold values from 0.02 to 0.15
- send_list: int32 [2304, 2], P('chord'), may hold values from -1 to 15, as said below
- recv_slot: int32 [192, 4], P('chord'), may hold values from 0 to 95, as said below
- marker_block: int32 [98304], P('chord'), may hold values from 0 to 3
- marker_cells: int32 [16, 98304], P(None, 'chord'), may hold values from 0 to 1023, as said below
- marker_layer: int32 [98304], P('chord'), may hold values from 0 to 63, as said below
- marker_frac: float32 [98304], P('chord'), may hold values from 0 to 1
- marker_weights: float32 [16, 98304], P(None, 'chord'), may hold values from 0.15 to 0.5
- marker_target: float32 [3, 98304], P(None, 'chord'), may hold values from -3 to 3
- marker_count: int32 [48], P('chord'), may hold values from 1 to 128, as said below
Outputs:
- velocity_next: float32 [3, 192, 64, 1024], P(None, 'chord', 'span')
- pressure_next: float32 [192, 64, 1024], P('chord', 'span')
Inputs may be any that keep to these rules, and one draw needn't show every extreme that they name: `send_list`: row d times the number of chord indices plus e lists, in 2 slots, the edges that chord index d sends to chord index e, each as 4 * block + side, -1 in empty slots. Every block has one neighbour across each side, the relation is symmetric (across the opposite side), and the pattern is the same on every chord index up to a shift of chord indices. Some pair of chord indices fills all 2 slots. `recv_slot`: entry (block, side) is the source chord index times 2 plus the slot of the edge that forms that side's ghost row; that edge is the listed entry of the source's row for this chord index. `marker_cells`: the 16 support cells of a marker form a 4 x 4 square of its block's plane, listed row by row. `marker_layer`: the marker slots of a chord index come in groups of 128, one group for each span index in order; the lowest support layer of group g's markers lies in layers g * 4 to (g + 1) * 4 - 1. `marker_count`: A marker is live when its position within its group is below its chord index's count.
All inputs are finite; a program needn't handle non-finite values.
Results may differ from a plain program's by a relative error of at most 0.0001.
Values sent between devices are 32-bit elements; how exact they have to be, the bound alone decides.
No kernel may reach another device: no remote copies, remote signals or barrier semaphores. Data moves between devices by JAX's collectives and lax.ppermute only.
A program may use at most 64 MiB of HBM per device.

v0:
```python
import math

import jax
import jax.numpy as jnp
from jax import lax
from jax.sharding import PartitionSpec as P

EDGE = 32
SUPPORT = 4
MS = 2048
ITERS = 8


def with_halo(array, sides, width):
    for axis, dim in sides:
        count, length = (lax.axis_size(axis), array.shape[dim])
        up = [(i, (i + 1) % count) for i in range(count)]
        down = [(j, i) for i, j in up]
        last = lax.slice_in_dim(array, length - width, length, axis=dim)
        leading = lax.slice_in_dim(array, 0, width, axis=dim)
        before = lax.ppermute(last, axis, up)
        after = lax.ppermute(leading, axis, down)
        array = jnp.concatenate([before, array, after], axis=dim)
    return array


def from_behind(array, axis, by):
    count = lax.axis_size(axis)
    return lax.ppermute(array, axis, [(i, (i + by) % count) for i in range(count)])


def edge_rows(cell_field):
    return jnp.stack(
        [
            cell_field[..., :EDGE],
            cell_field[..., EDGE * EDGE - EDGE :],
            cell_field[..., 0::EDGE],
            cell_field[..., EDGE - 1 :: EDGE],
        ],
        axis=-2,
    )


def four_sides(cell_field, ghost_rows):
    column_pos = jnp.arange(EDGE * EDGE, dtype=jnp.int32) % EDGE
    pad_shape = [(0, 0)] * (cell_field.ndim - 1)
    west_side = jnp.concatenate([ghost_rows[..., 0, :], cell_field[..., :-EDGE]], axis=-1)
    east_side = jnp.concatenate([cell_field[..., EDGE:], ghost_rows[..., 1, :]], axis=-1)
    lowered = jnp.pad(cell_field[..., :-1], pad_shape + [(1, 0)])
    raised = jnp.pad(cell_field[..., 1:], pad_shape + [(0, 1)])
    south_side = jnp.where(
        column_pos == 0, jnp.repeat(ghost_rows[..., 2, :], EDGE, axis=-1), lowered
    )
    north_side = jnp.where(
        column_pos == EDGE - 1, jnp.repeat(ghost_rows[..., 3, :], EDGE, axis=-1), raised
    )
    return (west_side, east_side, south_side, north_side)


def span_weights(fraction):
    distance = jnp.stack([1.0 + fraction, fraction, 1.0 - fraction, 2.0 - fraction])
    return 0.25 * (1.0 + jnp.cos(0.5 * math.pi * distance))


def trade(halo_part, edge_strips, send_list, recv_slot):
    padded = with_halo(halo_part, (("span", 2),), 1)
    outgoing = edge_strips[jnp.maximum(send_list, 0)]
    incoming = lax.all_to_all(outgoing, "chord", split_axis=0, concat_axis=0, tiled=True)
    flat_incoming = incoming.reshape((-1,) + incoming.shape[2:])
    return (padded, flat_incoming[recv_slot])


def strips_of(edge_block):
    channels, blocks, layers_here = (edge_block.shape[0], edge_block.shape[1], edge_block.shape[2])
    ordered = jnp.transpose(edge_block, (1, 3, 0, 2, 4))
    return ordered.reshape(blocks * 4, channels, layers_here * EDGE)


def ghost_layout(received, layers_here):
    blocks, channels = (received.shape[0], received.shape[2])
    shaped = received.reshape(blocks, 4, channels, layers_here, EDGE)
    return jnp.transpose(shaped, (2, 0, 3, 1, 4))


def beside_all(cell_field, send_list, recv_slot):
    layers_here = cell_field.shape[2]
    padded, received = trade(cell_field, strips_of(edge_rows(cell_field)), send_list, recv_slot)
    return four_sides(cell_field, ghost_layout(received, layers_here)) + (
        padded[:, :, :-2],
        padded[:, :, 2:],
    )


def local_support(
    fraction, weights, lowest_layer, cells_used, block_ids, first_layer, layers_here, total_layers
):
    span_part = span_weights(fraction)
    support_step = jnp.arange(SUPPORT, dtype=jnp.int32)
    layer_local = (lowest_layer[None, :] + support_step[:, None]) % total_layers - first_layer
    inside = (layer_local >= 0) & (layer_local < layers_here)
    layer_local = jnp.clip(layer_local, 0, layers_here - 1)
    kernel = jnp.where(inside, span_part, 0.0)[:, None, :] * weights[None, :, :]
    point_index = (block_ids[None, None, :] * layers_here + layer_local[:, None, :]) * (
        EDGE * EDGE
    ) + cells_used[None, :, :]
    return (kernel, point_index)


def strip_shift(values, amount):
    return from_behind(values, "span", amount)


def local(
    velocity,
    pressure,
    viscosity,
    send_list,
    recv_slot,
    marker_block,
    marker_cells,
    marker_layer,
    marker_frac,
    marker_weights,
    marker_target,
    marker_count,
):
    layers_here = pressure.shape[1]
    strip_count = lax.axis_size("span")
    strip_index = lax.axis_index("span")
    first_layer = strip_index * layers_here
    total_layers = layers_here * strip_count
    around_cells = beside_all(velocity, send_list, recv_slot)
    laplace = (
        around_cells[0]
        + around_cells[1]
        + around_cells[2]
        + around_cells[3]
        + around_cells[4]
        + around_cells[5]
        - 6.0 * velocity
    )
    tilde_velocity = velocity + viscosity[None] * laplace
    flat_tilde = tilde_velocity.reshape(3, -1)
    group_size = MS // strip_count
    lower_group = (strip_index + strip_count - 1) % strip_count

    def group_support(group_number):

        def take_group(values):
            return lax.dynamic_slice_in_dim(
                values, group_number * group_size, group_size, axis=values.ndim - 1
            )

        found = local_support(
            take_group(marker_frac),
            take_group(marker_weights),
            take_group(marker_layer),
            take_group(marker_cells),
            take_group(marker_block),
            first_layer,
            layers_here,
            total_layers,
        )
        return (take_group, found)

    take_own, (kernel_own, index_own) = group_support(strip_index)
    take_lower, (kernel_lower, index_lower) = group_support(lower_group)
    partial_own = jnp.sum(kernel_own[None] * flat_tilde[:, index_own], axis=(1, 2))
    partial_lower = jnp.sum(kernel_lower[None] * flat_tilde[:, index_lower], axis=(1, 2))
    sampled = partial_own + strip_shift(partial_lower, -1)
    live_mask = jnp.where(
        jnp.arange(group_size, dtype=jnp.int32) < marker_count[0], 1.0, 0.0
    ).astype(jnp.float32)
    force_own = live_mask * (take_own(marker_target) - sampled)
    force_lower = strip_shift(force_own, 1)
    flat_star = flat_tilde.at[:, index_own].add(kernel_own[None] * force_own[:, None, None, :])
    flat_star = flat_star.at[:, index_lower].add(kernel_lower[None] * force_lower[:, None, None, :])
    star_velocity = flat_star.reshape(tilde_velocity.shape)
    star_sides = beside_all(star_velocity, send_list, recv_slot)
    east_minus_west = star_sides[1][0] - star_sides[0][0]
    north_minus_south = star_sides[3][1] - star_sides[2][1]
    above_minus_below = star_sides[5][2] - star_sides[4][2]
    divergence = 0.5 * (east_minus_west + north_minus_south + above_minus_below)
    current = pressure[None]
    for sweep_index in range(ITERS):
        around_cells = beside_all(current, send_list, recv_slot)
        current = (
            around_cells[0]
            + around_cells[1]
            + around_cells[2]
            + around_cells[3]
            + around_cells[4]
            + around_cells[5]
            - divergence
        ) / 6.0
    around_cells = beside_all(current, send_list, recv_slot)
    gradients = jnp.stack(
        [
            around_cells[1][0] - around_cells[0][0],
            around_cells[3][0] - around_cells[2][0],
            around_cells[5][0] - around_cells[4][0],
        ]
    )
    velocity_next = star_velocity - 0.5 * gradients
    return (velocity_next, current[0])


def solution(mesh):
    in_specs = (
        P(None, "chord", "span", None),
        P("chord", "span", None),
        P("chord", "span", None),
        P("chord", None),
        P("chord", None),
        P("chord"),
        P(None, "chord"),
        P("chord"),
        P("chord"),
        P(None, "chord"),
        P(None, "chord"),
        P("chord"),
    )
    out_specs = (P(None, "chord", "span", None), P("chord", "span", None))
    return jax.shard_map(local, mesh=mesh, in_specs=in_specs, out_specs=out_specs, check_vma=False)
```

profile of v0, /device:TPU:1, one launch (start us, length us, event | category | flops | bytes accessed | tf_op | source)
XLA Modules:
  0.0 542.2 jit_solution(1523399709016774317)
XLA Ops:
  1.8 3.9 collective-permute-start
  5.7 6.2 %collective-permute-start.1 = (f32[3,4,1,1024]{3,2,1,0:T(1,128)S(1)}, f32[3,4,1,1024]{3,2,1,0:T(1,128)S(1)}, u32[]{:S(2)}, u32[]{:S(2)}) collective-permute-start(f32[3,4,1,1024]{3,2,1,0:T(1,128)S(1)} %get-tuple-element.23), channel_id=1, source_target_pairs={{1,0},{2,1},{3,2},{4,3},{5,4},{6,5},{7,6},{8,7},{9,8},{10,9},{11,1... | collective-permute-start | bytes 147464 | tf_op jit(solution)/shard_map/ppermute | solution.py:22
  15.8 1.2 gather_fusion.4
  17.0 21.8 %all-to-all-start.1 = ((f32[48,2,1,128]{3,1,2,0:T(2,128)}), f32[48,2,1,128]{3,1,2,0:T(2,128)S(1)}, u32[]{:S(2)}, u32[]{:S(2)}) async-start(f32[48,2,1,128]{3,1,2,0:T(2,128)} %bitcast.40), calls=%async_computation.1 | async-start | bytes 98304 | tf_op jit(solution)/shard_map/all_to_all | solution.py:68
  39.8 1.9 collective-permute-start.4
  41.7 7.3 %collective-permute-start.5 = (f32[1,4,1,1024]{3,2,1,0:T(1,128)S(1)}, f32[1,4,1,1024]{3,2,1,0:T(1,128)S(1)}, u32[]{:S(2)}, u32[]{:S(2)}) collective-permute-start(f32[1,4,1,1024]{3,2,1,0:T(1,128)S(1)} %get-tuple-element.107), channel_id=1, source_target_pairs={{1,0},{2,1},{3,2},{4,3},{5,4},{6,5},{7,6},{8,7},{9,8},{10,9},{11,1... | collective-permute-start | bytes 49160 | tf_op jit(solution)/shard_map/ppermute | solution.py:22
  49.8 2.0 slice.568
  51.8 2.0 slice.569
  65.6 15.5 %all-to-all-start = ((f32[48,2,3,128]{3,1,2,0:T(2,128)}), f32[48,2,3,128]{3,1,2,0:T(2,128)S(1)}, u32[]{:S(2)}, u32[]{:S(2)}) async-start(f32[48,2,3,128]{3,1,2,0:T(2,128)} %copy.124), calls=%async_computation | async-start | bytes 294912 | tf_op jit(solution)/shard_map/all_to_all | solution.py:68
  82.3 15.4 %all-to-all-done = f32[48,2,3,128]{3,1,2,0:T(2,128)S(1)} async-done(((f32[48,2,3,128]{3,1,2,0:T(2,128)}), f32[48,2,3,128]{3,1,2,0:T(2,128)S(1)}, u32[]{:S(2)}, u32[]{:S(2)}) %all-to-all-start) | async-done | bytes 147488 | tf_op jit(solution)/shard_map/all_to_all | solution.py:68
  100.3 4.7 copy.127
  105.0 31.3 %gather_fusion.2 = f32[8192,3]{1,0:T(8,128)} fusion(f32[3,16384]{0,1:T(8,128)} %bitcast.350, s32[8192]{0:T(1024)S(1)} %broadcast_clamp_fusion.1), kind=kCustom, calls=%fused_computation.2 | custom fusion | bytes 229376 | tf_op jit(solution)/shard_map/gather | solution.py:168
  136.3 31.3 %gather_fusion.3 = f32[8192,3]{1,0:T(8,128)} fusion(f32[3,16384]{0,1:T(8,128)} %bitcast.351, s32[8192]{0:T(1024)S(1)} %broadcast_clamp_fusion), kind=kCustom, calls=%fused_computation.3 | custom fusion | bytes 229376 | tf_op jit(solution)/shard_map/gather | solution.py:169
  167.5 3.0 multiply_reduce_fusion
  170.5 1.9 collective-permute-start.2
  172.5 1.3 multiply_reduce_fusion.1
  173.7 2.4 collective-permute-done.2
  176.2 1.9 collective-permute-start.3
  178.2 2.7 broadcast_multiply_fusion.1
  180.9 46.5 %scatter_fusion = f32[3,16384]{0,1:T(8,128)} fusion(f32[3,16384]{0,1:T(8,128)} %bitcast.352, s32[8192]{0:T(1024)S(1)} %bitcast.371, f32[8192,3]{1,0:T(8,128)} %bitcast.356), kind=kCustom, calls=%fused_computation.24 | custom fusion | flops 24576 | bytes 327680 | tf_op jit(solution)/shard_map/scatter-add | solution.py:176
  227.4 2.7 broadcast_multiply_fusion
  230.1 46.5 %scatter_fusion.1 = f32[3,16384]{0,1:T(8,128)} fusion(f32[3,16384]{0,1:T(8,128)} %scatter_fusion, s32[8192]{0:T(1024)S(1)} %bitcast.373, f32[8192,3]{1,0:T(8,128)} %bitcast.355), kind=kCustom, calls=%fused_computation.25 | custom fusion | flops 24576 | bytes 327680 | tf_op jit(solution)/shard_map/scatter-add | solution.py:177
  276.7 5.2 copy.172
  284.9 5.3 all-to-all-start.2
  290.2 7.5 %collective-permute-start.6 = (f32[3,4,1,1024]{3,2,1,0:T(1,128)S(1)}, f32[3,4,1,1024]{3,2,1,0:T(1,128)S(1)}, u32[]{:S(2)}, u32[]{:S(2)}) collective-permute-start(f32[3,4,1,1024]{3,2,1,0:T(1,128)S(1)} %get-tuple-element.14), channel_id=1, source_target_pairs={{1,0},{2,1},{3,2},{4,3},{5,4},{6,5},{7,6},{8,7},{9,8},{10,9},{11,1... | collective-permute-start | bytes 147464 | tf_op jit(solution)/shard_map/ppermute | solution.py:22
  297.7 1.9 collective-permute-start.7
  300.0 6.8 %all-to-all-done.2 = f32[48,2,3,128]{3,1,2,0:T(2,128)S(1)} async-done(((f32[48,2,3,128]{3,1,2,0:T(2,128)}), f32[48,2,3,128]{3,1,2,0:T(2,128)S(1)}, u32[]{:S(2)}, u32[]{:S(2)}) %all-to-all-start.2) | async-done | bytes 147488 | tf_op jit(solution)/shard_map/all_to_all | solution.py:68
  310.0 1.2 gather_fusion.8
  311.2 13.8 %all-to-all-start.3 = ((f32[48,2,1,128]{3,1,2,0:T(2,128)}), f32[48,2,1,128]{3,1,2,0:T(2,128)S(1)}, u32[]{:S(2)}, u32[]{:S(2)}) async-start(f32[48,2,1,128]{3,1,2,0:T(2,128)} %bitcast.65), calls=%async_computation.3 | async-start | bytes 98304 | tf_op jit(solution)/shard_map/all_to_all | solution.py:68
  325.0 1.9 collective-permute-start.8
  326.9 7.3 %collective-permute-start.9 = (f32[1,4,1,1024]{3,2,1,0:T(1,128)S(1)}, f32[1,4,1,1024]{3,2,1,0:T(1,128)S(1)}, u32[]{:S(2)}, u32[]{:S(2)}) collective-permute-start(f32[1,4,1,1024]{3,2,1,0:T(1,128)S(1)} %get-tuple-element.99), channel_id=1, source_target_pairs={{1,0},{2,1},{3,2},{4,3},{5,4},{6,5},{7,6},{8,7},{9,8},{10,9},{11,1... | collective-permute-start | bytes 49160 | tf_op jit(solution)/shard_map/ppermute | solution.py:22
  334.3 5.5 %all-to-all-done.3 = f32[48,2,1,128]{3,1,2,0:T(2,128)S(1)} async-done(((f32[48,2,1,128]{3,1,2,0:T(2,128)}), f32[48,2,1,128]{3,1,2,0:T(2,128)S(1)}, u32[]{:S(2)}, u32[]{:S(2)}) %all-to-all-start.3) | async-done | bytes 49184 | tf_op jit(solution)/shard_map/all_to_all | solution.py:68
  341.9 1.2 gather_fusion.10
  343.1 10.0 %all-to-all-start.4 = ((f32[48,2,1,128]{3,1,2,0:T(2,128)}), f32[48,2,1,128]{3,1,2,0:T(2,128)S(1)}, u32[]{:S(2)}, u32[]{:S(2)}) async-start(f32[48,2,1,128]{3,1,2,0:T(2,128)} %bitcast.78), calls=%async_computation.4 | async-start | bytes 98304 | tf_op jit(solution)/shard_map/all_to_all | solution.py:68
  353.1 1.9 collective-permute-start.10
  355.0 7.8 %collective-permute-start.11 = (f32[1,4,1,1024]{3,2,1,0:T(1,128)S(1)}, f32[1,4,1,1024]{3,2,1,0:T(1,128)S(1)}, u32[]{:S(2)}, u32[]{:S(2)}) collective-permute-start(f32[1,4,1,1024]{3,2,1,0:T(1,128)S(1)} %get-tuple-element.91), channel_id=1, source_target_pairs={{1,0},{2,1},{3,2},{4,3},{5,4},{6,5},{7,6},{8,7},{9,8},{10,9},{11,1... | collective-permute-start | bytes 49160 | tf_op jit(solution)/shard_map/ppermute | solution.py:22
  363.0 4.9 all-to-all-done.4
  370.0 1.2 gather_fusion.12
  371.2 10.3 %all-to-all-start.5 = ((f32[48,2,1,128]{3,1,2,0:T(2,128)}), f32[48,2,1,128]{3,1,2,0:T(2,128)S(1)}, u32[]{:S(2)}, u32[]{:S(2)}) async-start(f32[48,2,1,128]{3,1,2,0:T(2,128)} %bitcast.91), calls=%async_computation.5 | async-start | bytes 98304 | tf_op jit(solution)/shard_map/all_to_all | solution.py:68
  381.5 1.9 collective-permute-start.12
  383.5 7.8 %collective-permute-start.13 = (f32[1,4,1,1024]{3,2,1,0:T(1,128)S(1)}, f32[1,4,1,1024]{3,2,1,0:T(1,128)S(1)}, u32[]{:S(2)}, u32[]{:S(2)}) collective-permute-start(f32[1,4,1,1024]{3,2,1,0:T(1,128)S(1)} %get-tuple-element.83), channel_id=1, source_target_pairs={{1,0},{2,1},{3,2},{4,3},{5,4},{6,5},{7,6},{8,7},{9,8},{10,9},{11,1... | collective-permute-start | bytes 49160 | tf_op jit(solution)/shard_map/ppermute | solution.py:22
  391.4 4.9 all-to-all-done.5
  398.4 1.2 gather_fusion.14
  399.7 10.3 %all-to-all-start.6 = ((f32[48,2,1,128]{3,1,2,0:T(2,128)}), f32[48,2,1,128]{3,1,2,0:T(2,128)S(1)}, u32[]{:S(2)}, u32[]{:S(2)}) async-start(f32[48,2,1,128]{3,1,2,0:T(2,128)} %bitcast.104), calls=%async_computation.6 | async-start | bytes 98304 | tf_op jit(solution)/shard_map/all_to_all | solution.py:68
  410.0 1.9 collective-permute-start.14
  411.9 7.8 %collective-permute-start.15 = (f32[1,4,1,1024]{3,2,1,0:T(1,128)S(1)}, f32[1,4,1,1024]{3,2,1,0:T(1,128)S(1)}, u32[]{:S(2)}, u32[]{:S(2)}) collective-permute-start(f32[1,4,1,1024]{3,2,1,0:T(1,128)S(1)} %get-tuple-element.75), channel_id=1, source_target_pairs={{1,0},{2,1},{3,2},{4,3},{5,4},{6,5},{7,6},{8,7},{9,8},{10,9},{11,1... | collective-permute-start | bytes 49160 | tf_op jit(solution)/shard_map/ppermute | solution.py:22
  419.8 4.9 all-to-all-done.6
  426.9 1.2 gather_fusion.16
  428.1 10.3 %all-to-all-start.7 = ((f32[48,2,1,128]{3,1,2,0:T(2,128)}), f32[48,2,1,128]{3,1,2,0:T(2,128)S(1)}, u32[]{:S(2)}, u32[]{:S(2)}) async-start(f32[48,2,1,128]{3,1,2,0:T(2,128)} %bitcast.117), calls=%async_computation.7 | async-start | bytes 98304 | tf_op jit(solution)/shard_map/all_to_all | solution.py:68
  438.4 1.9 collective-permute-start.16
  440.3 7.8 %collective-permute-start.17 = (f32[1,4,1,1024]{3,2,1,0:T(1,128)S(1)}, f32[1,4,1,1024]{3,2,1,0:T(1,128)S(1)}, u32[]{:S(2)}, u32[]{:S(2)}) collective-permute-start(f32[1,4,1,1024]{3,2,1,0:T(1,128)S(1)} %get-tuple-element.67), channel_id=1, source_target_pairs={{1,0},{2,1},{3,2},{4,3},{5,4},{6,5},{7,6},{8,7},{9,8},{10,9},{11,1... | collective-permute-start | bytes 49160 | tf_op jit(solution)/shard_map/ppermute | solution.py:22
  448.3 4.9 all-to-all-done.7
  456.5 10.3 %all-to-all-start.8 = ((f32[48,2,1,128]{3,1,2,0:T(2,128)}), f32[48,2,1,128]{3,1,2,0:T(2,128)S(1)}, u32[]{:S(2)}, u32[]{:S(2)}) async-start(f32[48,2,1,128]{3,1,2,0:T(2,128)} %bitcast.130), calls=%async_computation.8 | async-start | bytes 98304 | tf_op jit(solution)/shard_map/all_to_all | solution.py:68
  466.8 1.9 collective-permute-start.18
  468.8 7.8 %collective-permute-start.19 = (f32[1,4,1,1024]{3,2,1,0:T(1,128)S(1)}, f32[1,4,1,1024]{3,2,1,0:T(1,128)S(1)}, u32[]{:S(2)}, u32[]{:S(2)}) collective-permute-start(f32[1,4,1,1024]{3,2,1,0:T(1,128)S(1)} %get-tuple-element.59), channel_id=1, source_target_pairs={{1,0},{2,1},{3,2},{4,3},{5,4},{6,5},{7,6},{8,7},{9,8},{10,9},{11,1... | collective-permute-start | bytes 49160 | tf_op jit(solution)/shard_map/ppermute | solution.py:22
  476.7 4.9 all-to-all-done.8
  484.9 10.3 %all-to-all-start.9 = ((f32[48,2,1,128]{3,1,2,0:T(2,128)}), f32[48,2,1,128]{3,1,2,0:T(2,128)S(1)}, u32[]{:S(2)}, u32[]{:S(2)}) async-start(f32[48,2,1,128]{3,1,2,0:T(2,128)} %bitcast.143), calls=%async_computation.9 | async-start | bytes 98304 | tf_op jit(solution)/shard_map/all_to_all | solution.py:68
  495.2 1.9 collective-permute-start.20
  497.2 7.8 %collective-permute-start.21 = (f32[1,4,1,1024]{3,2,1,0:T(1,128)S(1)}, f32[1,4,1,1024]{3,2,1,0:T(1,128)S(1)}, u32[]{:S(2)}, u32[]{:S(2)}) collective-permute-start(f32[1,4,1,1024]{3,2,1,0:T(1,128)S(1)} %get-tuple-element.51), channel_id=1, source_target_pairs={{1,0},{2,1},{3,2},{4,3},{5,4},{6,5},{7,6},{8,7},{9,8},{10,9},{11,1... | collective-permute-start | bytes 49160 | tf_op jit(solution)/shard_map/ppermute | solution.py:22
  505.1 4.9 all-to-all-done.9
  513.4 10.3 %all-to-all-start.10 = ((f32[48,2,1,128]{3,1,2,0:T(2,128)}), f32[48,2,1,128]{3,1,2,0:T(2,128)S(1)}, u32[]{:S(2)}, u32[]{:S(2)}) async-start(f32[48,2,1,128]{3,1,2,0:T(2,128)} %bitcast.156), calls=%async_computation.10 | async-start | bytes 98304 | tf_op jit(solution)/shard_map/all_to_all | solution.py:68
  523.7 7.8 %collective-permute-start.22 = (f32[1,4,1,1024]{3,2,1,0:T(1,128)S(1)}, f32[1,4,1,1024]{3,2,1,0:T(1,128)S(1)}, u32[]{:S(2)}, u32[]{:S(2)}) collective-permute-start(f32[1,4,1,1024]{3,2,1,0:T(1,128)S(1)} %get-tuple-element.42), channel_id=1, source_target_pairs={{1,0},{2,1},{3,2},{4,3},{5,4},{6,5},{7,6},{8,7},{9,8},{10,9},{11,1... | collective-permute-start | bytes 49160 | tf_op jit(solution)/shard_map/ppermute | solution.py:22
  531.5 1.9 collective-permute-start.23
  533.6 6.4 %collective-permute-done.23 = f32[1,4,1,1024]{3,2,1,0:T(1,128)S(1)} collective-permute-done((f32[1,4,1,1024]{3,2,1,0:T(1,128)S(1)}, f32[1,4,1,1024]{3,2,1,0:T(1,128)S(1)}, u32[]{:S(2)}, u32[]{:S(2)}) %collective-permute-start.23) | collective-permute-done | bytes 16416 | tf_op jit(solution)/shard_map/ppermute | solution.py:21
  (270 shorter events, 48.4 us)
Async XLA Ops:
  0.6 62.2 %copy-start = (f32[3,2048]{1,0:T(4,128)S(1)}, f32[3,2048]{1,0:T(4,128)}, u32[]{:S(2)}) copy-start(f32[3,2048]{1,0:T(4,128)} %param.22) | copy-start | bytes 73732
  1.8 98.1 %collective-permute-start = (f32[3,4,1,1024]{3,2,1,0:T(1,128)S(1)}, f32[3,4,1,1024]{3,2,1,0:T(1,128)S(1)}, u32[]{:S(2)}, u32[]{:S(2)}) collective-permute-start(f32[3,4,1,1024]{3,2,1,0:T(1,128)S(1)} %get-tuple-element.22), channel_id=1, source_target_pairs={{0,1},{1,2},{2,3},{3,4},{4,5},{5,6},{6,7},{7,8},{8,9},{9,10},{10,1... | collective-permute-start | bytes 147464 | tf_op jit(solution)/shard_map/ppermute | solution.py:21
  5.7 94.1 %collective-permute-start.1 = (f32[3,4,1,1024]{3,2,1,0:T(1,128)S(1)}, f32[3,4,1,1024]{3,2,1,0:T(1,128)S(1)}, u32[]{:S(2)}, u32[]{:S(2)}) collective-permute-start(f32[3,4,1,1024]{3,2,1,0:T(1,128)S(1)} %get-tuple-element.23), channel_id=1, source_target_pairs={{1,0},{2,1},{3,2},{4,3},{5,4},{6,5},{7,6},{8,7},{9,8},{10,9},{11,1... | collective-permute-start | bytes 147464 | tf_op jit(solution)/shard_map/ppermute | solution.py:22
  17.0 48.6 %all-to-all-start.1 = ((f32[48,2,1,128]{3,1,2,0:T(2,128)}), f32[48,2,1,128]{3,1,2,0:T(2,128)S(1)}, u32[]{:S(2)}, u32[]{:S(2)}) async-start(f32[48,2,1,128]{3,1,2,0:T(2,128)} %bitcast.40), calls=%async_computation.1 | async-start | bytes 98304 | tf_op jit(solution)/shard_map/all_to_all | solution.py:68
  39.8 269.2 %collective-permute-start.4 = (f32[1,4,1,1024]{3,2,1,0:T(1,128)S(1)}, f32[1,4,1,1024]{3,2,1,0:T(1,128)S(1)}, u32[]{:S(2)}, u32[]{:S(2)}) collective-permute-start(f32[1,4,1,1024]{3,2,1,0:T(1,128)S(1)} %get-tuple-element.106), channel_id=1, source_target_pairs={{0,1},{1,2},{2,3},{3,4},{4,5},{5,6},{6,7},{7,8},{8,9},{9,10},{10,1... | collective-permute-start | bytes 49160 | tf_op jit(solution)/shard_map/ppermute | solution.py:21
  41.7 267.3 %collective-permute-start.5 = (f32[1,4,1,1024]{3,2,1,0:T(1,128)S(1)}, f32[1,4,1,1024]{3,2,1,0:T(1,128)S(1)}, u32[]{:S(2)}, u32[]{:S(2)}) collective-permute-start(f32[1,4,1,1024]{3,2,1,0:T(1,128)S(1)} %get-tuple-element.107), channel_id=1, source_target_pairs={{1,0},{2,1},{3,2},{4,3},{5,4},{6,5},{7,6},{8,7},{9,8},{10,9},{11,1... | collective-permute-start | bytes 49160 | tf_op jit(solution)/shard_map/ppermute | solution.py:22
  56.3 43.6 %copy-start.1 = (f32[3,4,4,1024]{3,2,1,0:T(4,128)S(1)}, f32[3,4,4,1024]{3,2,1,0:T(4,128)}, u32[]{:S(2)}) copy-start(f32[3,4,4,1024]{3,2,1,0:T(4,128)} %param.12) | copy-start | bytes 589828
  56.3 43.6 %copy-start.5 = (f32[4,4,1024]{2,1,0:T(4,128)S(1)}, f32[4,4,1024]{2,1,0:T(4,128)}, u32[]{:S(2)}) copy-start(f32[4,4,1024]{2,1,0:T(4,128)} %param.14) | copy-start | bytes 196612
  65.6 32.2 %all-to-all-start = ((f32[48,2,3,128]{3,1,2,0:T(2,128)}), f32[48,2,3,128]{3,1,2,0:T(2,128)S(1)}, u32[]{:S(2)}, u32[]{:S(2)}) async-start(f32[48,2,3,128]{3,1,2,0:T(2,128)} %copy.124), calls=%async_computation | async-start | bytes 294912 | tf_op jit(solution)/shard_map/all_to_all | solution.py:68
  167.5 4.9 copy-start.2
  170.5 5.6 %collective-permute-start.2 = (f32[3,128]{0,1:T(8,128)S(1)}, f32[3,128]{0,1:T(8,128)S(1)}, u32[]{:S(2)}, u32[]{:S(2)}) collective-permute-start(f32[3,128]{0,1:T(8,128)S(1)} %bitcast.398), channel_id=1, source_target_pairs={{0,15},{1,0},{2,1},{3,2},{4,3},{5,4},{6,5},{7,6},{8,7},{9,8},{10,9... | collective-permute-start | bytes 4616 | tf_op jit(solution)/shard_map/ppermute | solution.py:29
  176.2 51.2 %collective-permute-start.3 = (f32[3,128]{0,1:T(8,128)S(1)}, f32[3,128]{0,1:T(8,128)S(1)}, u32[]{:S(2)}, u32[]{:S(2)}) collective-permute-start(f32[3,128]{0,1:T(8,128)S(1)} %fusion.64), channel_id=1, source_target_pairs={{0,1},{1,2},{2,3},{3,4},{4,5},{5,6},{6,7},{7,8},{8,9},{9,10},{10,1... | collective-permute-start | bytes 4616 | tf_op jit(solution)/shard_map/ppermute | solution.py:29
  281.9 27.1 %copy-start.4 = (f32[4,4,1024]{2,1,0:T(4,128)S(1)}, f32[4,4,1024]{2,1,0:T(4,128)}, u32[]{:S(2)}) copy-start(f32[4,4,1024]{2,1,0:T(4,128)} %param.13) | copy-start | bytes 196612
  284.9 22.0 %all-to-all-start.2 = ((f32[48,2,3,128]{3,1,2,0:T(2,128)}), f32[48,2,3,128]{3,1,2,0:T(2,128)S(1)}, u32[]{:S(2)}, u32[]{:S(2)}) async-start(f32[48,2,3,128]{3,1,2,0:T(2,128)} %copy.138), calls=%async_computation.2 | async-start | bytes 294912 | tf_op jit(solution)/shard_map/all_to_all | solution.py:68
  290.2 18.8 %collective-permute-start.6 = (f32[3,4,1,1024]{3,2,1,0:T(1,128)S(1)}, f32[3,4,1,1024]{3,2,1,0:T(1,128)S(1)}, u32[]{:S(2)}, u32[]{:S(2)}) collective-permute-start(f32[3,4,1,1024]{3,2,1,0:T(1,128)S(1)} %get-tuple-element.14), channel_id=1, source_target_pairs={{1,0},{2,1},{3,2},{4,3},{5,4},{6,5},{7,6},{8,7},{9,8},{10,9},{11,1... | collective-permute-start | bytes 147464 | tf_op jit(solution)/shard_map/ppermute | solution.py:22
  297.7 11.3 %collective-permute-start.7 = (f32[3,4,1,1024]{3,2,1,0:T(1,128)S(1)}, f32[3,4,1,1024]{3,2,1,0:T(1,128)S(1)}, u32[]{:S(2)}, u32[]{:S(2)}) collective-permute-start(f32[3,4,1,1024]{3,2,1,0:T(1,128)S(1)} %get-tuple-element.15), channel_id=1, source_target_pairs={{0,1},{1,2},{2,3},{3,4},{4,5},{5,6},{6,7},{7,8},{8,9},{9,10},{10,1... | collective-permute-start | bytes 147464 | tf_op jit(solution)/shard_map/ppermute | solution.py:21
  311.2 28.6 %all-to-all-start.3 = ((f32[48,2,1,128]{3,1,2,0:T(2,128)}), f32[48,2,1,128]{3,1,2,0:T(2,128)S(1)}, u32[]{:S(2)}, u32[]{:S(2)}) async-start(f32[48,2,1,128]{3,1,2,0:T(2,128)} %bitcast.65), calls=%async_computation.3 | async-start | bytes 98304 | tf_op jit(solution)/shard_map/all_to_all | solution.py:68
  325.0 16.1 %collective-permute-start.8 = (f32[1,4,1,1024]{3,2,1,0:T(1,128)S(1)}, f32[1,4,1,1024]{3,2,1,0:T(1,128)S(1)}, u32[]{:S(2)}, u32[]{:S(2)}) collective-permute-start(f32[1,4,1,1024]{3,2,1,0:T(1,128)S(1)} %get-tuple-element.98), channel_id=1, source_target_pairs={{0,1},{1,2},{2,3},{3,4},{4,5},{5,6},{6,7},{7,8},{8,9},{9,10},{10,1... | collective-permute-start | bytes 49160 | tf_op jit(solution)/shard_map/ppermute | solution.py:21
  326.9 14.1 %collective-permute-start.9 = (f32[1,4,1,1024]{3,2,1,0:T(1,128)S(1)}, f32[1,4,1,1024]{3,2,1,0:T(1,128)S(1)}, u32[]{:S(2)}, u32[]{:S(2)}) collective-permute-start(f32[1,4,1,1024]{3,2,1,0:T(1,128)S(1)} %get-tuple-element.99), channel_id=1, source_target_pairs={{1,0},{2,1},{3,2},{4,3},{5,4},{6,5},{7,6},{8,7},{9,8},{10,9},{11,1... | collective-permute-start | bytes 49160 | tf_op jit(solution)/shard_map/ppermute | solution.py:22
  343.1 24.8 %all-to-all-start.4 = ((f32[48,2,1,128]{3,1,2,0:T(2,128)}), f32[48,2,1,128]{3,1,2,0:T(2,128)S(1)}, u32[]{:S(2)}, u32[]{:S(2)}) async-start(f32[48,2,1,128]{3,1,2,0:T(2,128)} %bitcast.78), calls=%async_computation.4 | async-start | bytes 98304 | tf_op jit(solution)/shard_map/all_to_all | solution.py:68
  353.1 16.1 %collective-permute-start.10 = (f32[1,4,1,1024]{3,2,1,0:T(1,128)S(1)}, f32[1,4,1,1024]{3,2,1,0:T(1,128)S(1)}, u32[]{:S(2)}, u32[]{:S(2)}) collective-permute-start(f32[1,4,1,1024]{3,2,1,0:T(1,128)S(1)} %get-tuple-element.90), channel_id=1, source_target_pairs={{0,1},{1,2},{2,3},{3,4},{4,5},{5,6},{6,7},{7,8},{8,9},{9,10},{10,1... | collective-permute-start | bytes 49160 | tf_op jit(solution)/shard_map/ppermute | solution.py:21
  355.0 14.1 %collective-permute-start.11 = (f32[1,4,1,1024]{3,2,1,0:T(1,128)S(1)}, f32[1,4,1,1024]{3,2,1,0:T(1,128)S(1)}, u32[]{:S(2)}, u32[]{:S(2)}) collective-permute-start(f32[1,4,1,1024]{3,2,1,0:T(1,128)S(1)} %get-tuple-element.91), channel_id=1, source_target_pairs={{1,0},{2,1},{3,2},{4,3},{5,4},{6,5},{7,6},{8,7},{9,8},{10,9},{11,1... | collective-permute-start | bytes 49160 | tf_op jit(solution)/shard_map/ppermute | solution.py:22
  371.2 25.1 %all-to-all-start.5 = ((f32[48,2,1,128]{3,1,2,0:T(2,128)}), f32[48,2,1,128]{3,1,2,0:T(2,128)S(1)}, u32[]{:S(2)}, u32[]{:S(2)}) async-start(f32[48,2,1,128]{3,1,2,0:T(2,128)} %bitcast.91), calls=%async_computation.5 | async-start | bytes 98304 | tf_op jit(solution)/shard_map/all_to_all | solution.py:68
  381.5 16.1 %collective-permute-start.12 = (f32[1,4,1,1024]{3,2,1,0:T(1,128)S(1)}, f32[1,4,1,1024]{3,2,1,0:T(1,128)S(1)}, u32[]{:S(2)}, u32[]{:S(2)}) collective-permute-start(f32[1,4,1,1024]{3,2,1,0:T(1,128)S(1)} %get-tuple-element.82), channel_id=1, source_target_pairs={{0,1},{1,2},{2,3},{3,4},{4,5},{5,6},{6,7},{7,8},{8,9},{9,10},{10,1... | collective-permute-start | bytes 49160 | tf_op jit(solution)/shard_map/ppermute | solution.py:21
  383.5 14.1 %collective-permute-start.13 = (f32[1,4,1,1024]{3,2,1,0:T(1,128)S(1)}, f32[1,4,1,1024]{3,2,1,0:T(1,128)S(1)}, u32[]{:S(2)}, u32[]{:S(2)}) collective-permute-start(f32[1,4,1,1024]{3,2,1,0:T(1,128)S(1)} %get-tuple-element.83), channel_id=1, source_target_pairs={{1,0},{2,1},{3,2},{4,3},{5,4},{6,5},{7,6},{8,7},{9,8},{10,9},{11,1... | collective-permute-start | bytes 49160 | tf_op jit(solution)/shard_map/ppermute | solution.py:22
  399.7 25.1 %all-to-all-start.6 = ((f32[48,2,1,128]{3,1,2,0:T(2,128)}), f32[48,2,1,128]{3,1,2,0:T(2,128)S(1)}, u32[]{:S(2)}, u32[]{:S(2)}) async-start(f32[48,2,1,128]{3,1,2,0:T(2,128)} %bitcast.104), calls=%async_computation.6 | async-start | bytes 98304 | tf_op jit(solution)/shard_map/all_to_all | solution.py:68
  410.0 16.1 %collective-permute-start.14 = (f32[1,4,1,1024]{3,2,1,0:T(1,128)S(1)}, f32[1,4,1,1024]{3,2,1,0:T(1,128)S(1)}, u32[]{:S(2)}, u32[]{:S(2)}) collective-permute-start(f32[1,4,1,1024]{3,2,1,0:T(1,128)S(1)} %get-tuple-element.74), channel_id=1, source_target_pairs={{0,1},{1,2},{2,3},{3,4},{4,5},{5,6},{6,7},{7,8},{8,9},{9,10},{10,1... | collective-permute-start | bytes 49160 | tf_op jit(solution)/shard_map/ppermute | solution.py:21
  411.9 14.1 %collective-permute-start.15 = (f32[1,4,1,1024]{3,2,1,0:T(1,128)S(1)}, f32[1,4,1,1024]{3,2,1,0:T(1,128)S(1)}, u32[]{:S(2)}, u32[]{:S(2)}) collective-permute-start(f32[1,4,1,1024]{3,2,1,0:T(1,128)S(1)} %get-tuple-element.75), channel_id=1, source_target_pairs={{1,0},{2,1},{3,2},{4,3},{5,4},{6,5},{7,6},{8,7},{9,8},{10,9},{11,1... | collective-permute-start | bytes 49160 | tf_op jit(solution)/shard_map/ppermute | solution.py:22
  428.1 25.1 %all-to-all-start.7 = ((f32[48,2,1,128]{3,1,2,0:T(2,128)}), f32[48,2,1,128]{3,1,2,0:T(2,128)S(1)}, u32[]{:S(2)}, u32[]{:S(2)}) async-start(f32[48,2,1,128]{3,1,2,0:T(2,128)} %bitcast.117), calls=%async_computation.7 | async-start | bytes 98304 | tf_op jit(solution)/shard_map/all_to_all | solution.py:68
  438.4 16.1 %collective-permute-start.16 = (f32[1,4,1,1024]{3,2,1,0:T(1,128)S(1)}, f32[1,4,1,1024]{3,2,1,0:T(1,128)S(1)}, u32[]{:S(2)}, u32[]{:S(2)}) collective-permute-start(f32[1,4,1,1024]{3,2,1,0:T(1,128)S(1)} %get-tuple-element.66), channel_id=1, source_target_pairs={{0,1},{1,2},{2,3},{3,4},{4,5},{5,6},{6,7},{7,8},{8,9},{9,10},{10,1... | collective-permute-start | bytes 49160 | tf_op jit(solution)/shard_map/ppermute | solution.py:21
  440.3 14.1 %collective-permute-start.17 = (f32[1,4,1,1024]{3,2,1,0:T(1,128)S(1)}, f32[1,4,1,1024]{3,2,1,0:T(1,128)S(1)}, u32[]{:S(2)}, u32[]{:S(2)}) collective-permute-start(f32[1,4,1,1024]{3,2,1,0:T(1,128)S(1)} %get-tuple-element.67), channel_id=1, source_target_pairs={{1,0},{2,1},{3,2},{4,3},{5,4},{6,5},{7,6},{8,7},{9,8},{10,9},{11,1... | collective-permute-start | bytes 49160 | tf_op jit(solution)/shard_map/ppermute | solution.py:22
  456.5 25.1 %all-to-all-start.8 = ((f32[48,2,1,128]{3,1,2,0:T(2,128)}), f32[48,2,1,128]{3,1,2,0:T(2,128)S(1)}, u32[]{:S(2)}, u32[]{:S(2)}) async-start(f32[48,2,1,128]{3,1,2,0:T(2,128)} %bitcast.130), calls=%async_computation.8 | async-start | bytes 98304 | tf_op jit(solution)/shard_map/all_to_all | solution.py:68
  466.8 16.1 %collective-permute-start.18 = (f32[1,4,1,1024]{3,2,1,0:T(1,128)S(1)}, f32[1,4,1,1024]{3,2,1,0:T(1,128)S(1)}, u32[]{:S(2)}, u32[]{:S(2)}) collective-permute-start(f32[1,4,1,1024]{3,2,1,0:T(1,128)S(1)} %get-tuple-element.58), channel_id=1, source_target_pairs={{0,1},{1,2},{2,3},{3,4},{4,5},{5,6},{6,7},{7,8},{8,9},{9,10},{10,1... | collective-permute-start | bytes 49160 | tf_op jit(solution)/shard_map/ppermute | solution.py:21
  468.8 14.1 %collective-permute-start.19 = (f32[1,4,1,1024]{3,2,1,0:T(1,128)S(1)}, f32[1,4,1,1024]{3,2,1,0:T(1,128)S(1)}, u32[]{:S(2)}, u32[]{:S(2)}) collective-permute-start(f32[1,4,1,1024]{3,2,1,0:T(1,128)S(1)} %get-tuple-element.59), channel_id=1, source_target_pairs={{1,0},{2,1},{3,2},{4,3},{5,4},{6,5},{7,6},{8,7},{9,8},{10,9},{11,1... | collective-permute-start | bytes 49160 | tf_op jit(solution)/shard_map/ppermute | solution.py:22
  484.9 25.1 %all-to-all-start.9 = ((f32[48,2,1,128]{3,1,2,0:T(2,128)}), f32[48,2,1,128]{3,1,2,0:T(2,128)S(1)}, u32[]{:S(2)}, u32[]{:S(2)}) async-start(f32[48,2,1,128]{3,1,2,0:T(2,128)} %bitcast.143), calls=%async_computation.9 | async-start | bytes 98304 | tf_op jit(solution)/shard_map/all_to_all | solution.py:68
  495.2 16.1 %collective-permute-start.20 = (f32[1,4,1,1024]{3,2,1,0:T(1,128)S(1)}, f32[1,4,1,1024]{3,2,1,0:T(1,128)S(1)}, u32[]{:S(2)}, u32[]{:S(2)}) collective-permute-start(f32[1,4,1,1024]{3,2,1,0:T(1,128)S(1)} %get-tuple-element.50), channel_id=1, source_target_pairs={{0,1},{1,2},{2,3},{3,4},{4,5},{5,6},{6,7},{7,8},{8,9},{9,10},{10,1... | collective-permute-start | bytes 49160 | tf_op jit(solution)/shard_map/ppermute | solution.py:21
  497.2 14.1 %collective-permute-start.21 = (f32[1,4,1,1024]{3,2,1,0:T(1,128)S(1)}, f32[1,4,1,1024]{3,2,1,0:T(1,128)S(1)}, u32[]{:S(2)}, u32[]{:S(2)}) collective-permute-start(f32[1,4,1,1024]{3,2,1,0:T(1,128)S(1)} %get-tuple-element.51), channel_id=1, source_target_pairs={{1,0},{2,1},{3,2},{4,3},{5,4},{6,5},{7,6},{8,7},{9,8},{10,9},{11,1... | collective-permute-start | bytes 49160 | tf_op jit(solution)/shard_map/ppermute | solution.py:22
  511.5 30.7 %copy-start.3 = (f32[1,4,4,1024]{3,2,1,0:T(4,128)}, f32[1,4,4,1024]{3,2,1,0:T(4,128)S(1)}, u32[]{:S(2)}) copy-start(f32[1,4,4,1024]{3,2,1,0:T(4,128)S(1)} %fusion.11) | copy-start | bytes 196612
  513.4 26.6 %all-to-all-start.10 = ((f32[48,2,1,128]{3,1,2,0:T(2,128)}), f32[48,2,1,128]{3,1,2,0:T(2,128)S(1)}, u32[]{:S(2)}, u32[]{:S(2)}) async-start(f32[48,2,1,128]{3,1,2,0:T(2,128)} %bitcast.156), calls=%async_computation.10 | async-start | bytes 98304 | tf_op jit(solution)/shard_map/all_to_all | solution.py:68
  523.7 9.9 %collective-permute-start.22 = (f32[1,4,1,1024]{3,2,1,0:T(1,128)S(1)}, f32[1,4,1,1024]{3,2,1,0:T(1,128)S(1)}, u32[]{:S(2)}, u32[]{:S(2)}) collective-permute-start(f32[1,4,1,1024]{3,2,1,0:T(1,128)S(1)} %get-tuple-element.42), channel_id=1, source_target_pairs={{1,0},{2,1},{3,2},{4,3},{5,4},{6,5},{7,6},{8,7},{9,8},{10,9},{11,1... | collective-permute-start | bytes 49160 | tf_op jit(solution)/shard_map/ppermute | solution.py:22
  531.5 8.4 %collective-permute-start.23 = (f32[1,4,1,1024]{3,2,1,0:T(1,128)S(1)}, f32[1,4,1,1024]{3,2,1,0:T(1,128)S(1)}, u32[]{:S(2)}, u32[]{:S(2)}) collective-permute-start(f32[1,4,1,1024]{3,2,1,0:T(1,128)S(1)} %get-tuple-element.43), channel_id=1, source_target_pairs={{0,1},{1,2},{2,3},{3,4},{4,5},{5,6},{6,7},{7,8},{8,9},{9,10},{10,1... | collective-permute-start | bytes 49160 | tf_op jit(solution)/shard_map/ppermute | solution.py:21
where the time goes:
time: 545 us; the launch traced here: 542 us
  starting transfers between devices  238 us (44%)
  local copies, waits for them, and re-layouts  126 us (23%)
  other arithmetic  109 us (20%)
  waiting for transfers between devices  66.1 us (12%)
    all_to_all x11, starting transfers between devices, trade(): lax.all_to_all(outgoing, 'chord', split_axis=0, concat_axis=0, tiled=True)  128 us
    ppermute x11, starting transfers between devices, with_halo(): after = lax.ppermute(leading, axis, down)  83.1 us
    all_to_all x11, waiting for transfers between devices, trade(): lax.all_to_all(outgoing, 'chord', split_axis=0, concat_axis=0, tiled=True)  57.3 us
    scatter-add x1, other arithmetic, local(): flat_tilde.at[:, index_own]  46.5 us
    scatter-add x1, other arithmetic, local(): flat_star.at[:, index_lower]  46.5 us
    gather x1, local copies, waits for them, and re-layouts, local(): flat_tilde[:, index_lower]  31.3 us
    gather x1, local copies, waits for them, and re-layouts, local(): flat_tilde[:, index_own]  31.3 us
    ppermute x11, starting transfers between devices, with_halo(): before = lax.ppermute(last, axis, up)  23.2 us
  transfers between devices with their start and end apart: 35, of which 11 were waited for; matrix products, arithmetic and copies ran while one was open for 40% of the time, Pallas kernels for 0%

commit v1 on v0

v1 whole, which is shorter than its diff:
```python
import math

import jax
import jax.numpy as jnp
import ml_dtypes
import numpy as np
from jax import lax
from jax.experimental import pallas as pl
from jax.experimental.pallas import tpu as pltpu
from jax.sharding import PartitionSpec as P

EDGE = 32
CELLS = EDGE * EDGE
NB = 4
SZ = 4
DEPTH = 3
STRIDE = 40
WIDTH = 1536
LANES = 128
SEG = 4 * LANES
F32 = jnp.float32
BF16 = jnp.bfloat16


def place_of(i, k):
    return STRIDE * (i + DEPTH) + k + 4


def edge_cell(side, depth, x):
    return [(depth, x), (EDGE - 1 - depth, x), (x, depth), (x, EDGE - 1 - depth)][side]


def ghost_cell(side, depth, x):
    return [(-1 - depth, x), (EDGE + depth, x), (x, -1 - depth), (x, EDGE + depth)][side]


def pack_matrix(rows, where):
    table = np.zeros((rows, SEG), np.float32)
    for side in range(4):
        for depth in range(DEPTH):
            for x in range(EDGE):
                table[where(*edge_cell(side, depth, x)), side * LANES + depth * EDGE + x] = 1
        for corner in range(4):
            for cell in range(4):
                i, k = cell // 2, cell % 2
                i = i if corner // 2 == 0 else EDGE - 1 - i
                k = k if corner % 2 == 0 else EDGE - 1 - k
                table[where(i, k), side * LANES + 96 + corner * 4 + cell] = 1
    return table.astype(ml_dtypes.bfloat16)


def place_matrix():
    table = np.zeros((SEG, WIDTH), np.float32)
    for side in range(4):
        for depth in range(DEPTH):
            for x in range(EDGE):
                table[side * LANES + depth * EDGE + x, place_of(*ghost_cell(side, depth, x))] = 1
    for vertex in range(4):
        for cell in range(3):
            i, k = cell // 2, cell % 2
            i = -1 - i if vertex // 2 == 0 else EDGE + i
            k = -1 - k if vertex % 2 == 0 else EDGE + k
            table[vertex * LANES + 96 + cell, place_of(i, k)] = 1
    return table.astype(ml_dtypes.bfloat16)


def rim_matrix():
    table = np.zeros((CELLS, LANES), np.float32)
    for side in range(4):
        for x in range(EDGE):
            i, k = edge_cell(side, 0, x)
            table[i * EDGE + k, side * EDGE + x] = 1
    return table.astype(ml_dtypes.bfloat16)


def sheet_mask():
    mask = np.zeros((8, WIDTH), np.float32)
    for i in range(-DEPTH, EDGE + DEPTH):
        for k in range(-DEPTH, EDGE + DEPTH):
            inside_i, inside_k = 0 <= i < EDGE, 0 <= k < EDGE
            if inside_i and not inside_k:
                mask[:4, place_of(i, k)] = 1
            if inside_k and not inside_i:
                mask[4:, place_of(i, k)] = 1
    return mask


def block_mask():
    mask = np.zeros((8, WIDTH), np.float32)
    for i in range(EDGE):
        mask[:, place_of(i, 0) : place_of(i, 0) + EDGE] = 1
    return mask


def vertex_place(vertex):
    return place_of(-1 if vertex // 2 == 0 else EDGE, -1 if vertex % 2 == 0 else EDGE)


def pick(x, table):
    high = x.astype(BF16)
    rest = x - high.astype(F32)
    middle = rest.astype(BF16)
    low = (rest - middle.astype(F32)).astype(BF16)
    parts = jnp.dot(jnp.concatenate([high, middle, low], axis=0), table, preferred_element_type=F32)
    rows = x.shape[0]
    return (parts[:rows] + parts[rows : 2 * rows]) + parts[2 * rows :]


def shifted(x, lanes):
    return pltpu.roll(x, lanes % x.shape[1], axis=1)


def lane_ids(rows):
    return lax.broadcasted_iota(jnp.int32, (rows, LANES), 1)


def remap(x, width, pieces):
    rows = x.shape[0]
    lane = lane_ids(rows)
    out = []
    for tile in range(width // LANES):
        acc = jnp.zeros((rows, LANES), F32)
        base = tile * LANES
        for src, dst in pieces:
            first, last = max(dst, base), min(dst + EDGE, base + LANES)
            while first < last:
                at = src + first - dst
                column = at // LANES
                stop = min(last, first + (column + 1) * LANES - at)
                value = x[:, column * LANES : (column + 1) * LANES]
                turn = (first - base - at % LANES) % LANES
                if turn:
                    value = pltpu.roll(value, turn, axis=1)
                acc = jnp.where((lane >= first - base) & (lane < stop - base), value, acc)
                first = stop
        out.append(acc)
    return jnp.concatenate(out, axis=1)


def expand(x):
    return remap(x, WIDTH, [(EDGE * i, place_of(i, 0)) for i in range(EDGE)])


def compact(x):
    return remap(x, CELLS, [(place_of(i, 0), EDGE * i) for i in range(EDGE)])


def store_table(strips, table_ref, field, fields, first_row):
    lane = lane_ids(NB)
    for layer in range(SZ):
        for side in range(4):
            rows = strips[layer, first_row : first_row + NB, side * LANES : (side + 1) * LANES]
            turned = pltpu.roll(rows, 16, axis=1)
            for slot in range(2):
                low = jnp.broadcast_to(rows[2 * slot : 2 * slot + 1], rows.shape)
                high = jnp.broadcast_to(turned[2 * slot + 1 : 2 * slot + 2], rows.shape)
                value = jnp.where(lane < 96, rows, jnp.where(lane < 112, low, high))
                for block in range(NB):
                    entry = (slot * fields + field) * 16 + block * 4 + side
                    at = slot * SZ + layer
                    table_ref[entry, at : at + 1, :] = value[block : block + 1]


def post(send_ref, table_ref, out_ref, fields, count):
    def one(target, carry):
        first = jnp.maximum(send_ref[2 * target], 0)
        second = jnp.maximum(send_ref[2 * target + 1], 0)
        for field in range(fields):
            out_ref[target * fields + field] = (
                table_ref[field * 16 + first] + table_ref[(fields + field) * 16 + second]
            )
        return carry

    lax.fori_loop(0, count, one, 0, unroll=4)


def first_pack(send_ref, cells_ref, p_ref, rim_ref, pack_ref, out_ref, table_ref, strips_ref):
    count = out_ref.shape[0] // 2
    table_ref[...] = jnp.zeros(table_ref.shape, F32)
    rims = pick(cells_ref[...].reshape(SZ * 16, CELLS), rim_ref[...])
    lane = lane_ids(NB)
    for layer in range(SZ):
        rows = rims[layer * 16 : (layer + 1) * 16]
        for side in range(4):
            value = jnp.zeros((NB, LANES), F32)
            for comp in range(3):
                part = rows[comp * NB : (comp + 1) * NB]
                turn = EDGE * (comp - side) % LANES
                if turn:
                    part = pltpu.roll(part, turn, axis=1)
                value = jnp.where(lane // EDGE == comp, part, value)
            for block in range(NB):
                for slot in range(2):
                    at = slot * SZ + layer
                    table_ref[slot * 32 + block * 4 + side, at : at + 1, :] = value[block : block + 1]
    strips_ref[...] = pick(p_ref[...].reshape(SZ * 8, CELLS), pack_ref[...]).reshape(SZ, 8, SEG)
    store_table(strips_ref, table_ref, 1, 2, 0)
    post(send_ref, table_ref, out_ref, 2, count)


class Hops:
    def __init__(self, me_ref, send_ref, recv_ref, near_ref, count):
        self.me, self.recv, self.near, self.count = me_ref[0], recv_ref, near_ref, count
        for edge in range(16):
            source, slot = recv_ref[edge] // 2, recv_ref[edge] % 2
            back = lax.rem(2 * self.me - source + count, count)
            near_ref[edge] = send_ref[2 * back + slot] // 4
            near_ref[16 + edge] = lax.rem(source - self.me + count, count)

    def rows(self, block, side):
        entry = self.recv[block * 4 + side]
        return entry // 2, entry % 2

    def hop(self, block, offset, side):
        edge = block * 4 + side
        return self.near[edge], offset + self.near[16 + edge]

    def source(self, offset):
        return lax.rem(self.me + offset, self.count)


def near_rows(got_ref, source, slot, field, fields):
    rows = got_ref[source * fields + field]
    return jnp.where(slot == 1, pltpu.roll(rows, SZ, axis=0), rows)


def patch_rows(got_ref, hops, block, offset, corner, field, fields, target, cell):
    rows = near_rows(got_ref, hops.source(offset), block // 2, field, fields)
    lane = 96 + (block % 2) * 16 + corner * 4 + cell
    return pltpu.roll(rows, lax.rem(target - lane + 2 * LANES, LANES), axis=1)


def gather_ghosts(got_ref, hops, ghost_ref, field, fields):
    lane = lane_ids(8)
    for block in range(NB):
        for vertex in range(4):
            strip = near_rows(got_ref, *hops.rows(block, vertex), field, fields)
            i_side, k_side = vertex // 2, 2 + vertex % 2
            far = (1 - vertex // 2) * 2 + 1 - vertex % 2
            for sheet, (side, then) in enumerate(((i_side, k_side), (k_side, i_side))):
                at, offset = hops.hop(block, 0, side)
                at, offset = hops.hop(at, offset, then)
                second = patch_rows(got_ref, hops, at, offset, far, field, fields, 96, 0)
                at, offset = hops.hop(at, offset, side ^ 1)
                beyond = far ^ 2 if sheet == 0 else far ^ 1
                third = patch_rows(got_ref, hops, at, offset, beyond, field, fields, 100, 0)
                value = jnp.where(
                    lane < 96, strip, jnp.where(lane < 100, second, jnp.where(lane == 100, third, 0.0))
                )
                row = sheet * NB + block
                for layer in range(SZ):
                    ghost_ref[layer, row : row + 1, vertex * LANES : (vertex + 1) * LANES] = value[
                        layer : layer + 1
                    ]


def third_cells(ghosts):
    lane = lane_ids(8)
    tiles = [jnp.zeros((8, LANES), F32) for _ in range(WIDTH // LANES)]
    for vertex in range(4):
        tile, at = vertex_place(vertex) // LANES, vertex_place(vertex) % LANES
        value = pltpu.roll(ghosts[:, vertex * LANES : (vertex + 1) * LANES], (at - 100) % LANES, axis=1)
        tiles[tile] = jnp.where(lane == at, value, tiles[tile])
    return jnp.concatenate(tiles, axis=1)


def vertex_masks():
    lane = lax.broadcasted_iota(jnp.int32, (8, WIDTH), 1)
    first = lax.broadcasted_iota(jnp.int32, (8, WIDTH), 0) < NB
    places = [vertex_place(v) for v in range(4)]
    west = first & ((lane == places[0]) | (lane == places[1]))
    east = first & ((lane == places[2]) | (lane == places[3]))
    south = ~first & ((lane == places[0]) | (lane == places[2]))
    north = ~first & ((lane == places[1]) | (lane == places[3]))
    return west, east, south, north


def corrections(ext, third):
    west, east, south, north = vertex_masks()
    return (
        jnp.where(west, third - shifted(ext, -STRIDE), 0.0),
        jnp.where(east, third - shifted(ext, STRIDE), 0.0),
        jnp.where(south, third - shifted(ext, -1), 0.0),
        jnp.where(north, third - shifted(ext, 1), 0.0),
    )


def merge(x, mask):
    return jnp.where(mask, pltpu.roll(x, NB, axis=0), x)


def second_halves(x):
    return jnp.concatenate([x, x], axis=0)


def unpack_pressure(own, got_ref, hops, ghost_ref, place_ref, own_ref, corr_ref, field, fields, up, down):
    gather_ghosts(got_ref, hops, ghost_ref, field, fields)
    placed = pick(ghost_ref[...].reshape(SZ * 8, SEG), place_ref[...])
    for layer in range(SZ):
        ext = own(layer) + placed[layer * 8 : (layer + 1) * 8]
        own_ref[layer] = ext
        corr_ref[layer] = sum(corrections(ext, third_cells(ghost_ref[layer])))
        if layer >= 1:
            up[layer - 1, :, :WIDTH] = ext
        if layer < SZ - 1:
            down[layer, :, :WIDTH] = ext


def first_unpack(
    me_ref, send_ref, recv_ref, got_ref, p_ref, place_ref, own_ref, corr_ref, rim_ref, up_ref, down_ref, ghost_ref, near_ref
):
    count = got_ref.shape[0] // 2
    hops = Hops(me_ref, send_ref, recv_ref, near_ref, count)
    lane = lane_ids(8)
    for block in range(NB):
        strips = [near_rows(got_ref, *hops.rows(block, side), 0, 2) for side in range(4)]
        for comp in range(4):
            value = jnp.zeros((8, LANES), F32)
            if comp < 3:
                for side in range(4):
                    turn = EDGE * (side - comp) % LANES
                    part = pltpu.roll(strips[side], turn, axis=1) if turn else strips[side]
                    value = jnp.where(lane // EDGE == side, part, value)
            row = comp * NB + block
            for layer in range(SZ):
                rim_ref[layer, row : row + 1, :] = value[layer : layer + 1]
    unpack_pressure(
        lambda layer: expand(p_ref[layer]), got_ref, hops, ghost_ref, place_ref, own_ref, corr_ref, 1, 2, up_ref, down_ref
    )
    for layer in range(SZ):
        for half in range(2):
            rows = rim_ref[layer, half * 8 : (half + 1) * 8, :]
            at = WIDTH + half * LANES
            if layer >= 1:
                up_ref[layer - 1, :, at : at + LANES] = rows
            if layer < SZ - 1:
                down_ref[layer, :, at : at + LANES] = rows


def later_unpack(
    me_ref, send_ref, recv_ref, got_ref, p_ref, place_ref, block_ref, own_ref, corr_ref, up_ref, down_ref, ghost_ref, near_ref
):
    count = got_ref.shape[0]
    hops = Hops(me_ref, send_ref, recv_ref, near_ref, count)
    unpack_pressure(
        lambda layer: jnp.where(block_ref[...] > 0.0, p_ref[layer], 0.0),
        got_ref, hops, ghost_ref, place_ref, own_ref, corr_ref, 0, 1, up_ref, down_ref,
    )


def rim_rows(ref, layer):
    return jnp.concatenate([ref[layer, :, WIDTH : WIDTH + LANES], ref[layer, :, WIDTH + LANES :]], axis=0)


def forcing(
    send_ref, count_ref, own_ref, low_ref, high_ref, rim_ref, rim_low_ref, rim_high_ref, spread_ref, pack_ref,
    start_ref, block_ref, corner_ref, phi_ref, weight_ref, target_ref,
    star_ref, out_ref, tilde_ref, plane_ref, table_ref, strips_ref,
):
    markers = start_ref.shape[1]
    group = markers // 2
    layers = SZ + 2 * (SZ - 1)
    cell = lax.broadcasted_iota(jnp.int32, (16, CELLS), 1)

    def cells_at(layer):
        if layer < 0:
            return low_ref[layer + SZ]
        return own_ref[layer] if layer < SZ else high_ref[layer - SZ]

    def rims_at(layer):
        if layer < 0:
            return rim_rows(rim_low_ref, layer + SZ - 1)
        return rim_ref[layer] if layer < SZ else rim_rows(rim_high_ref, layer - SZ)

    for at in range(layers):
        layer = at - (SZ - 1)
        here = cells_at(layer)
        around = jnp.where(cell >= EDGE, shifted(here, EDGE), 0.0)
        around += jnp.where(cell < CELLS - EDGE, shifted(here, -EDGE), 0.0)
        around += jnp.where(cell % EDGE != 0, shifted(here, 1), 0.0)
        around += jnp.where(cell % EDGE != EDGE - 1, shifted(here, -1), 0.0)
        around += pick(rims_at(layer), spread_ref[...])
        around += cells_at(layer - 1) + cells_at(layer + 1)
        eddy = second_halves(second_halves(here[3 * NB :]))
        tilde_ref[at] = here + eddy * (around - 6.0 * here)
    row_i = corner_ref[...] // EDGE
    row_k = corner_ref[...] % EDGE
    along = lax.broadcasted_iota(jnp.int32, (EDGE, markers), 0)
    lines = []
    for a in range(4):
        line = jnp.zeros((EDGE, markers), F32)
        for b in range(4):
            line = jnp.where(along == row_k + b, weight_ref[4 * a + b : 4 * a + b + 1, :], line)
        lines.append(line)

    def fill(i, carry):
        value = jnp.zeros((EDGE, markers), F32)
        for a in range(4):
            value = jnp.where(row_i + a == i, lines[a], value)
        plane_ref[pl.ds(i * EDGE, EDGE), :] = value
        return carry

    lax.fori_loop(0, EDGE, fill, 0)
    start = start_ref[...]

    def span_weight(layer):
        value = jnp.zeros((1, markers), F32)
        for a in range(4):
            value = jnp.where(start + a == layer, phi_ref[a : a + 1, :], value)
        return value

    weights = [span_weight(at - (SZ - 1)) for at in range(layers)]
    dots = jnp.dot(
        tilde_ref[...].reshape(layers * 16, CELLS), plane_ref[...],
        precision=lax.Precision.HIGHEST, preferred_element_type=F32,
    )
    total = jnp.zeros((16, markers), F32)
    for at in range(layers):
        total += weights[at] * dots[at * 16 : (at + 1) * 16]
    mine = (lax.broadcasted_iota(jnp.int32, (16, markers), 0) % NB) == block_ref[...]
    total = jnp.where(mine, total, 0.0)
    place = lax.broadcasted_iota(jnp.int32, (1, markers), 1) % group
    live = place < count_ref[0]
    rows = []
    for comp in range(3):
        sampled = jnp.sum(total[comp * NB : (comp + 1) * NB], axis=0, keepdims=True)
        force = jnp.where(live, target_ref[comp : comp + 1, :] - sampled, 0.0)
        rows.append(jnp.broadcast_to(force, (NB, markers)))
    rows.append(jnp.zeros((NB, markers), F32))
    force = jnp.where(mine, jnp.concatenate(rows, axis=0), 0.0)
    pushes = jnp.concatenate([weights[layer + SZ - 1] * force for layer in range(SZ)], axis=0)
    spread = lax.dot_general(
        pushes, plane_ref[...], (((1,), (1,)), ((), ())),
        precision=lax.Precision.HIGHEST, preferred_element_type=F32,
    )
    star = tilde_ref[SZ - 1 : 2 * SZ - 1].reshape(SZ * 16, CELLS) + spread
    star_ref[...] = star.reshape(SZ, 16, CELLS)
    table_ref[...] = jnp.zeros(table_ref.shape, F32)
    strips_ref[...] = pick(star, pack_ref[...]).reshape(SZ, 16, SEG)
    for comp in range(3):
        store_table(strips_ref, table_ref, comp, 3, comp * NB)
    post(send_ref, table_ref, out_ref, 3, out_ref.shape[0] // 3)


def star_unpack(
    me_ref, send_ref, recv_ref, got_ref, star_ref, place_ref, mask_ref, flat_ref, third_ref, up_ref, down_ref, ghost_ref, near_ref
):
    count = got_ref.shape[0] // 3
    hops = Hops(me_ref, send_ref, recv_ref, near_ref, count)
    for comp in range(3):
        gather_ghosts(got_ref, hops, ghost_ref.at[comp], comp, 3)
    placed = pick(ghost_ref[...].reshape(3 * SZ * 8, SEG), place_ref[...])
    mask = mask_ref[...] > 0.0
    for layer in range(SZ):
        whole = expand(star_ref[layer])
        exts = []
        for comp in range(3):
            at = (comp * SZ + layer) * 8
            exts.append(second_halves(whole[comp * NB : (comp + 1) * NB]) + placed[at : at + 8])
        west, east, _, _ = corrections(exts[0], third_cells(ghost_ref[0, layer]))
        _, _, south, north = corrections(exts[1], third_cells(ghost_ref[1, layer]))
        spread = shifted(exts[0], -STRIDE) - shifted(exts[0], STRIDE)
        spread += shifted(exts[1], -1) - shifted(exts[1], 1)
        spread += (west - east) + (south - north)
        flat = merge(0.5 * spread, mask)
        flat_ref[layer] = flat
        third_ref[layer] = exts[2]
        if layer >= 2:
            up_ref[layer - 2] = flat
        if layer >= 1:
            up_ref[layer + 1] = exts[2]
        if layer < 2:
            down_ref[layer] = flat
        if layer < 3:
            down_ref[layer + 2] = exts[2]


def sweep(source, target, first, last, rhs_ref, corr_ref, mask):
    for at in range(first, last):
        here = source[at]
        around = (shifted(here, STRIDE) + shifted(here, -STRIDE)) + (shifted(here, 1) + shifted(here, -1))
        around += source[at - 1] + source[at + 1]
        around -= rhs_ref[at - 1]
        if corr_ref is not None and DEPTH <= at < DEPTH + SZ:
            around += corr_ref[at - DEPTH]
        target[at] = merge(around * (1.0 / 6.0), mask)


def load_layers(work_ref, own_ref, low_ref, high_ref):
    for layer in range(DEPTH):
        work_ref[layer] = low_ref[layer, :, :WIDTH]
        work_ref[DEPTH + SZ + layer] = high_ref[layer, :, :WIDTH]
    for layer in range(SZ):
        work_ref[DEPTH + layer] = own_ref[layer]


def three_sweeps(work_ref, other_ref, rhs_ref, corr_ref, mask):
    sweep(work_ref, other_ref, 1, 9, rhs_ref, corr_ref, mask)
    sweep(other_ref, work_ref, 2, 8, rhs_ref, None, mask)
    sweep(work_ref, other_ref, 3, 7, rhs_ref, None, mask)


def send_pressure(send_ref, done_ref, pack_ref, p_ref, out_ref, table_ref, strips_ref):
    p_ref[...] = done_ref[DEPTH : DEPTH + SZ]
    table_ref[...] = jnp.zeros(table_ref.shape, F32)
    strips_ref[...] = pick(p_ref[...].reshape(SZ * 8, WIDTH), pack_ref[...]).reshape(SZ, 8, SEG)
    store_table(strips_ref, table_ref, 0, 1, 0)
    post(send_ref, table_ref, out_ref, 1, out_ref.shape[0])


def first_sweeps(
    send_ref, own_ref, corr_ref, low_ref, high_ref, flat_ref, third_ref, star_low_ref, star_high_ref, mask_ref, pack_ref,
    p_ref, rhs_ref, out_ref, work_ref, other_ref, table_ref, strips_ref,
):
    mask = mask_ref[...] > 0.0
    load_layers(work_ref, own_ref, low_ref, high_ref)

    def flat_at(layer):
        if layer < 0:
            return star_low_ref[layer + 2]
        return flat_ref[layer] if layer < SZ else star_high_ref[layer - SZ]

    def third_at(layer):
        if layer < 0:
            return star_low_ref[layer + 5]
        return third_ref[layer] if layer < SZ else star_high_ref[layer - SZ + 2]

    for layer in range(-2, SZ + 2):
        rhs_ref[layer + 2] = flat_at(layer) + 0.5 * (third_at(layer + 1) - third_at(layer - 1))
    three_sweeps(work_ref, other_ref, rhs_ref, corr_ref, mask)
    send_pressure(send_ref, other_ref, pack_ref, p_ref, out_ref, table_ref, strips_ref)


def later_sweeps(
    send_ref, own_ref, corr_ref, low_ref, high_ref, rhs_ref, mask_ref, pack_ref,
    p_ref, out_ref, work_ref, other_ref, table_ref, strips_ref,
):
    load_layers(work_ref, own_ref, low_ref, high_ref)
    three_sweeps(work_ref, other_ref, rhs_ref, corr_ref, mask_ref[...] > 0.0)
    send_pressure(send_ref, other_ref, pack_ref, p_ref, out_ref, table_ref, strips_ref)


def last_sweeps(own_ref, corr_ref, low_ref, high_ref, rhs_ref, mask_ref, star_ref, out_ref, work_ref, other_ref):
    mask = mask_ref[...] > 0.0
    load_layers(work_ref, own_ref, low_ref, high_ref)
    sweep(work_ref, other_ref, 1, 9, rhs_ref, corr_ref, mask)
    sweep(other_ref, work_ref, 2, 8, rhs_ref, None, mask)
    for layer in range(SZ):
        here = work_ref[DEPTH + layer]
        rows = [
            shifted(here, -STRIDE) - shifted(here, STRIDE),
            shifted(here, -1) - shifted(here, 1),
            work_ref[DEPTH + layer + 1] - work_ref[DEPTH + layer - 1],
            here,
        ]
        flat = compact(jnp.concatenate([row[:NB] for row in rows], axis=0))
        star = star_ref[layer]
        row = lax.broadcasted_iota(jnp.int32, (16, CELLS), 0)
        out_ref[layer] = jnp.where(row < 3 * NB, star - 0.5 * flat, flat)


def call(kernel, name, out_shapes, scratch, scalars):
    smem, vmem = pl.BlockSpec(memory_space=pltpu.SMEM), pl.BlockSpec(memory_space=pltpu.VMEM)
    shapes = tuple(jax.ShapeDtypeStruct(shape, F32) for shape in out_shapes)

    def run(*args):
        return pl.pallas_call(
            kernel,
            name=name,
            out_shape=shapes,
            in_specs=[smem if at < scalars else vmem for at in range(len(args))],
            out_specs=tuple(vmem for _ in shapes),
            scratch_shapes=scratch,
            compiler_params=pltpu.CompilerParams(vmem_limit_bytes=24 << 20),
        )(*args)

    return run


def trade(messages, count):
    whole = messages.reshape(count, -1, LANES)
    got = lax.all_to_all(whole, "chord", split_axis=0, concat_axis=0, tiled=True)
    return got.reshape(messages.shape)


def beside(up, down):
    size = lax.axis_size("span")
    low = lax.ppermute(up, "span", [(i, (i + 1) % size) for i in range(size)])
    high = lax.ppermute(down, "span", [(i, (i + size - 1) % size) for i in range(size)])
    return low, high


def local(
    velocity,
    pressure,
    viscosity,
    send_list,
    recv_slot,
    marker_block,
    marker_cells,
    marker_layer,
    marker_frac,
    marker_weights,
    marker_target,
    marker_count,
):
    count, strips = lax.axis_size("chord"), lax.axis_size("span")
    me = lax.axis_index("chord").astype(jnp.int32).reshape(1)
    at = lax.axis_index("span").astype(jnp.int32)
    send, recv = send_list.reshape(-1), recv_slot.reshape(-1)
    rim, spread = jnp.asarray(RIM), jnp.asarray(RIM.T)
    pack_flat, pack_ext = jnp.asarray(PACK_FLAT), jnp.asarray(PACK_EXT)
    place, mask, inside = jnp.asarray(PLACE), jnp.asarray(MASK), jnp.asarray(INSIDE)
    cells = jnp.concatenate([velocity, viscosity[None]], axis=0)
    cells = jnp.transpose(cells, (2, 0, 1, 3)).reshape(SZ, 16, CELLS)
    by_layer = jnp.transpose(pressure, (1, 0, 2))
    flat_p = jnp.concatenate([by_layer, by_layer], axis=1)

    plane, flat = (SZ, 8, WIDTH), (SZ, 16, CELLS)
    tables = lambda fields: pltpu.VMEM((2 * fields * 16, 8, LANES), F32)
    strip_rows = lambda rows: pltpu.VMEM((SZ, rows, SEG), F32)
    near = pltpu.SMEM((32,), jnp.int32)
    layers = pltpu.VMEM((SZ + 2 * DEPTH, 8, WIDTH), F32)

    cells_low, cells_high = beside(cells, cells)
    (messages,) = call(first_pack, "first_pack", [(2 * count, 8, LANES)], [tables(2), strip_rows(8)], 1)(
        send, cells, flat_p, rim, pack_flat
    )
    got = trade(messages, count)
    edge = (DEPTH, 8, WIDTH + 2 * LANES)
    own, corr, rims, up, down = call(
        first_unpack, "first_unpack", [plane, plane, (SZ, 16, LANES), edge, edge], [strip_rows(8), near], 3
    )(me, send, recv, got, flat_p, place)
    low, high = beside(up, down)

    group = marker_block.shape[0] // strips
    below = (at + strips - 1) % strips

    def two_groups(values):
        axis = values.ndim - 1
        parts = [lax.dynamic_slice_in_dim(values, g * group, group, axis=axis) for g in (at, below)]
        return jnp.concatenate(parts, axis=axis)

    first = jnp.concatenate([jnp.full((group,), at * SZ), jnp.full((group,), (below + 1) * SZ)])
    start = two_groups(marker_layer) - first
    fraction = two_groups(marker_frac)
    distance = jnp.stack([1.0 + fraction, fraction, 1.0 - fraction, 2.0 - fraction])
    phi = 0.25 * (1.0 + jnp.cos(0.5 * math.pi * distance))
    star, messages = call(
        forcing, "forcing", [flat, (3 * count, 8, LANES)],
        [
            pltpu.VMEM((SZ + 2 * DEPTH, 16, CELLS), F32),
            pltpu.VMEM((CELLS, 2 * group), F32),
            tables(3),
            strip_rows(16),
        ],
        2,
    )(
        send, marker_count, cells, cells_low, cells_high, rims, low, high, spread, pack_flat,
        start[None], two_groups(marker_block)[None], two_groups(marker_cells[:1]), phi,
        two_groups(marker_weights), two_groups(marker_target),
    )
    got = trade(messages, count)
    edge = (5, 8, WIDTH)
    flat_part, third, up, down = call(
        star_unpack, "star_unpack", [plane, plane, edge, edge], [pltpu.VMEM((3, SZ, 8, SEG), F32), near], 3
    )(me, send, recv, got, star, place, mask)
    star_low, star_high = beside(up, down)

    p, rhs, messages = call(
        first_sweeps, "first_sweeps", [plane, (SZ + 4, 8, WIDTH), (count, 8, LANES)],
        [layers, layers, tables(1), strip_rows(8)], 1,
    )(send, own, corr, low, high, flat_part, third, star_low, star_high, mask, pack_ext)
    edge = (DEPTH, 8, WIDTH)
    for last in (False, True):
        got = trade(messages, count)
        own, corr, up, down = call(
            later_unpack, "later_unpack", [plane, plane, edge, edge], [strip_rows(8), near], 3
        )(me, send, recv, got, p, place, inside)
        low, high = beside(up, down)
        if not last:
            p, messages = call(
                later_sweeps, "later_sweeps", [plane, (count, 8, LANES)], [layers, layers, tables(1), strip_rows(8)], 1
            )(send, own, corr, low, high, rhs, mask, pack_ext)
    (out,) = call(last_sweeps, "last_sweeps", [flat], [layers, layers], 0)(
        own, corr, low, high, rhs, mask, star
    )
    out = jnp.transpose(out.reshape(SZ, 4, NB, CELLS), (1, 2, 0, 3))
    return out[:3], out[3]


RIM = rim_matrix()
PACK_FLAT = pack_matrix(CELLS, lambda i, k: EDGE * i + k)
PACK_EXT = pack_matrix(WIDTH, place_of)
PLACE = place_matrix()
MASK = sheet_mask()
INSIDE = block_mask()


def solution(mesh):
    in_specs = (
        P(None, "chord", "span", None),
        P("chord", "span", None),
        P("chord", "span", None),
        P("chord", None),
        P("chord", None),
        P("chord"),
        P(None, "chord"),
        P("chord"),
        P("chord"),
        P(None, "chord"),
        P(None, "chord"),
        P("chord"),
    )
    out_specs = (P(None, "chord", "span", None), P("chord", "span", None))
    return jax.shard_map(local, mesh=mesh, in_specs=in_specs, out_specs=out_specs, check_vma=False)
```

time: 545 us -> 220 us (0.40)
  starting transfers between devices: 238 us -> 68.6 us
  local copies, waits for them, and re-layouts: 126 us -> 8.08 us
  other arithmetic: 109 us -> 1.25 us
  blocking collectives: 0 us -> 83.9 us
  waiting for transfers between devices: 66.1 us -> 32.4 us
  Pallas kernels: 0 us -> 23.3 us
    all_to_all x11 -> x1, starting transfers between devices: 128 us -> 19 us  [trade(): lax.all_to_all(whole, 'chord', split_axis=0, concat_axis=0, tiled=True)]
    scatter-add x2 -> x0, other arithmetic: 93.1 us -> none  [the longest x1 46.5 us: local(): flat_tilde.at[:, index_own]]
    all_to_all x0 -> x3, blocking collectives: none -> 83.9 us  [trade(): lax.all_to_all(whole, 'chord', split_axis=0, concat_axis=0, tiled=True)]
    gather x28 -> x0, local copies, waits for them, and re-layouts: 82.6 us -> none  [the longest x1 31.3 us: local(): flat_tilde[:, index_lower]]
    ppermute x24 -> x10, starting transfers between devices: 110 us -> 49.6 us  [the longest x5 39.9 us: beside(): lax.ppermute(down, 'span', [(i, (i + size - 1) % size) for i in range(siz...]
    all_to_all x11 -> x1, waiting for transfers between devices: 57.3 us -> 17 us  [trade(): lax.all_to_all(whole, 'chord', split_axis=0, concat_axis=0, tiled=True)]
    pallas_call x0 -> x9, Pallas kernels: none -> 23.3 us  [run(): pl.pallas_call(kernel, name=name, out_shape=shapes, in_specs=[smem if at...]
    slice x55 -> x3, local copies, waits for them, and re-layouts: 18.3 us -> 0.7 us  [the longest x1 0.69 us: local(): return (out[:3], out[3])]
  transfers between devices with their start and end apart: 35 -> 11, of which waited for: 11 -> 9; matrix products, arithmetic and copies ran while one was open for 40% -> 3% of each run, Pallas kernels for 0% -> 2%
where the time goes in v1:
time: 220 us; the launch traced here: 219 us
  blocking collectives  83.9 us (38%)
  starting transfers between devices  68.6 us (31%)
  waiting for transfers between devices  32.4 us (15%)
  Pallas kernels  23.3 us (11%)
  local copies, waits for them, and re-layouts  8.08 us (4%)
    all_to_all x3, blocking collectives, trade(): lax.all_to_all(whole, 'chord', split_axis=0, concat_axis=0, tiled=True)  83.9 us
    ppermute x5, starting transfers between devices, beside(): lax.ppermute(down, 'span', [(i, (i + size - 1) % size) for i in range(siz...  39.9 us
    pallas_call x9, Pallas kernels, run(): pl.pallas_call(kernel, name=name, out_shape=shapes, in_specs=[smem if at...  23.3 us
    all_to_all x1, starting transfers between devices, trade(): lax.all_to_all(whole, 'chord', split_axis=0, concat_axis=0, tiled=True)  19 us
    all_to_all x1, waiting for transfers between devices, trade(): lax.all_to_all(whole, 'chord', split_axis=0, concat_axis=0, tiled=True)  17 us
    ppermute x5, waiting for transfers between devices, beside(): low = lax.ppermute(up, 'span', [(i, (i + 1) % size) for i in range(size)])  9.97 us
    ppermute x5, starting transfers between devices, beside(): low = lax.ppermute(up, 'span', [(i, (i + 1) % size) for i in range(size)])  9.7 us
    ppermute x5, waiting for transfers between devices, beside(): lax.ppermute(down, 'span', [(i, (i + size - 1) % size) for i in range(siz...  5.36 us
  transfers between devices with their start and end apart: 11, of which 9 were waited for; matrix products, arithmetic and copies ran while one was open for 3% of the time, Pallas kernels for 2%

profile of v1, /device:TPU:1, one launch (start us, length us, event | category | flops | bytes accessed | tf_op | source)
XLA Modules:
  0.0 219.1 jit_solution(16097242775861304991)
XLA Ops:
  0.6 0.0 copy-start.2
  0.6 0.0 copy-start.6
  0.7 1.1 pad_maximum_fusion
  1.8 0.2 copy.29.cells_ref.own_ref
  2.0 8.3 %collective-permute-start.3 = (f32[4,16,1024]{2,1,0:T(8,128)S(1)}, f32[4,16,1024]{2,1,0:T(8,128)}, u32[]{:S(2)}, u32[]{:S(2)}) collective-permute-start(f32[4,16,1024]{2,1,0:T(8,128)S(1)} %copy.29.cells_ref.own_ref), channel_id=1, source_target_pairs={{0,15},{1,0},{2,1},{3,2},{4,3},{5,4},{6,5},{7,6},{8,7},{9,8},{10,9... | collective-permute-start | bytes 786440 | tf_op jit(solution)/shard_map/ppermute | solution.py:589
  10.2 1.9 collective-permute-start.2
  12.1 0.8 copy.25
  12.9 0.1 reshape.119.send_ref
  13.0 0.9 copy.32
  14.0 0.0 copy-done.2
  14.0 0.0 copy-done.6
  14.0 0.0 slice-start
  14.0 0.0 copy-start.8
  14.0 0.0 copy-start
  14.0 1.3 first_pack.1
  15.3 0.0 copy-start.3
  15.3 0.7 copy-done.3
  16.0 19.0 %all-to-all-start = ((f32[48,16,128]{2,1,0:T(8,128)}), f32[48,16,128]{2,1,0:T(8,128)S(1)}, u32[]{:S(2)}, u32[]{:S(2)}) async-start(f32[48,16,128]{2,1,0:T(8,128)} %bitcast.24), calls=%async_computation | async-start | bytes 786432 | tf_op jit(solution)/shard_map/all_to_all | solution.py:582
  35.1 0.8 fusion.4
  35.9 0.8 fusion.5
  36.6 0.8 fusion.3
  37.5 0.7 constant_dynamic-slice_fusion.1
  38.2 0.1 fusion.2.phi_ref
  38.3 0.7 constant_dynamic-slice_fusion.3
  39.0 0.0 slice-done
  39.6 0.0 copy-done.8
  39.6 0.1 reshape.120.recv_ref
  39.7 17.0 %all-to-all-done = f32[48,16,128]{2,1,0:T(8,128)S(1)} async-done(((f32[48,16,128]{2,1,0:T(8,128)}), f32[48,16,128]{2,1,0:T(8,128)S(1)}, u32[]{:S(2)}, u32[]{:S(2)}) %all-to-all-start) | async-done | bytes 393248 | tf_op jit(solution)/shard_map/all_to_all | solution.py:582
  56.8 0.0 copy-done
  56.8 2.2 %first_unpack.1 = (f32[4,8,1536]{2,1,0:T(8,128)S(1)}, f32[4,8,1536]{2,1,0:T(8,128)S(1)}, f32[4,16,128]{2,1,0:T(8,128)S(1)}, f32[3,8,1792]{2,1,0:T(8,128)S(1)}, f32[3,8,1792]{2,1,0:T(8,128)S(1)}) custom-call(s32[1]{0:T(128)} %bitcast.me_ref, s32[96]{0:T(128)S(1)} %reshape.119.send_ref, s32[16]{0:T(128)S(1)} %reshape.120.recv_ref, f32[96,8,128]{2,1,0:T(8,128)S(1)} %bitcast.23, ...), custom_call_target="tpu_custom_call" | custom-call | tf_op jit(solution)/shard_map/first_unpack/pallas_call | solution.py:567
  59.0 2.0 collective-permute-start
  61.0 7.4 %collective-permute-start.1 = (f32[3,8,1792]{2,1,0:T(8,128)S(1)}, f32[3,8,1792]{2,1,0:T(8,128)S(1)}, u32[]{:S(2)}, u32[]{:S(2)}) collective-permute-start(f32[3,8,1792]{2,1,0:T(8,128)S(1)} %get-tuple-element.29), channel_id=1, source_target_pairs={{0,15},{1,0},{2,1},{3,2},{4,3},{5,4},{6,5},{7,6},{8,7},{9,8},{10,9... | collective-permute-start | bytes 516104 | tf_op jit(solution)/shard_map/ppermute | solution.py:589
  68.5 0.0 collective-permute-done.3.high_ref
  68.5 0.0 collective-permute-done.2.low_ref
  68.5 2.6 %collective-permute-done.rim_low_ref.low_ref = f32[3,8,1792]{2,1,0:T(8,128)S(1)} collective-permute-done((f32[3,8,1792]{2,1,0:T(8,128)S(1)}, f32[3,8,1792]{2,1,0:T(8,128)S(1)}, u32[]{:S(2)}, u32[]{:S(2)}) %collective-permute-start) | collective-permute-done | bytes 172064 | tf_op jit(solution)/shard_map/ppermute | solution.py:588
  71.1 0.9 collective-permute-done.1.rim_high_ref.high_ref
  71.9 0.0 copy-done.5
  71.9 5.6 %forcing.1 = (f32[4,16,1024]{2,1,0:T(8,128)S(1)}, f32[144,8,128]{2,1,0:T(8,128)S(1)}) custom-call(s32[96]{0:T(128)S(1)} %reshape.119.send_ref, s32[1]{0:T(128)S(6)} %copy.33.count_ref, f32[4,16,1024]{2,1,0:T(8,128)S(1)} %copy.29.cells_ref.own_ref, f32[4,16,1024]{2,1,0:T(8,128)} %collective-permute-done.2.low_ref, ...), custom_call_target="tpu_custom_call" | custom-call | tf_op jit(solution)/shard_map/forcing/pallas_call | solution.py:567
  77.5 0.0 copy-start.1
  77.5 36.0 %all_to_all.20 = f32[48,24,128]{2,1,0:T(8,128)S(1)} all-to-all(f32[48,24,128]{2,1,0:T(8,128)S(1)} %bitcast.25), channel_id=1, replica_groups=mesh['chord'=48,'span'=16] {'chord'}, dimensions={0} | all-to-all | bytes 1179648 | tf_op jit(solution)/shard_map/all_to_all | solution.py:582
  113.5 4.2 %star_unpack.1 = (f32[4,8,1536]{2,1,0:T(8,128)S(1)}, f32[4,8,1536]{2,1,0:T(8,128)S(1)}, f32[5,8,1536]{2,1,0:T(8,128)S(1)}, f32[5,8,1536]{2,1,0:T(8,128)S(1)}) custom-call(s32[1]{0:T(128)} %bitcast.me_ref, s32[96]{0:T(128)S(1)} %reshape.119.send_ref, s32[16]{0:T(128)S(1)} %reshape.120.recv_ref, f32[144,8,128]{2,1,0:T(8,128)S(1)} %bitcast.22, ...), custom_call_target="tpu_custom_call" | custom-call | tf_op jit(solution)/shard_map/star_unpack/pallas_call | solution.py:567
  117.7 1.9 collective-permute-start.4
  119.6 8.2 %collective-permute-start.5 = (f32[5,8,1536]{2,1,0:T(8,128)S(1)}, f32[5,8,1536]{2,1,0:T(8,128)S(1)}, u32[]{:S(2)}, u32[]{:S(2)}) collective-permute-start(f32[5,8,1536]{2,1,0:T(8,128)S(1)} %get-tuple-element.36), channel_id=1, source_target_pairs={{0,15},{1,0},{2,1},{3,2},{4,3},{5,4},{6,5},{7,6},{8,7},{9,8},{10,9... | collective-permute-start | bytes 737288 | tf_op jit(solution)/shard_map/ppermute | solution.py:589
  127.8 3.9 %collective-permute-done.4.star_low_ref = f32[5,8,1536]{2,1,0:T(8,128)S(1)} collective-permute-done((f32[5,8,1536]{2,1,0:T(8,128)S(1)}, f32[5,8,1536]{2,1,0:T(8,128)S(1)}, u32[]{:S(2)}, u32[]{:S(2)}) %collective-permute-start.4) | collective-permute-done | bytes 245792 | tf_op jit(solution)/shard_map/ppermute | solution.py:588
  131.7 0.9 collective-permute-done.5.star_high_ref
  132.6 0.0 copy-done.1
  132.6 2.2 first_sweeps.1
  134.8 25.0 %all_to_all.21.got_ref = f32[48,8,128]{2,1,0:T(8,128)S(1)} all-to-all(f32[48,8,128]{2,1,0:T(8,128)S(1)} %get-tuple-element.37), channel_id=1, replica_groups=mesh['chord'=48,'span'=16] {'chord'}, dimensions={0} | all-to-all | bytes 393216 | tf_op jit(solution)/shard_map/all_to_all | solution.py:582
  159.7 2.1 later_unpack.2
  161.9 1.9 collective-permute-start.6
  163.8 8.0 %collective-permute-start.7 = (f32[3,8,1536]{2,1,0:T(8,128)S(1)}, f32[3,8,1536]{2,1,0:T(8,128)S(1)}, u32[]{:S(2)}, u32[]{:S(2)}) collective-permute-start(f32[3,8,1536]{2,1,0:T(8,128)S(1)} %get-tuple-element.42), channel_id=1, source_target_pairs={{0,15},{1,0},{2,1},{3,2},{4,3},{5,4},{6,5},{7,6},{8,7},{9,8},{10,9... | collective-permute-start | bytes 442376 | tf_op jit(solution)/shard_map/ppermute | solution.py:589
  171.8 1.7 collective-permute-done.6.low_ref
  173.6 1.8 collective-permute-done.7.high_ref
  175.4 2.1 later_sweeps.1
  177.5 22.9 %all_to_all.22.got_ref = f32[48,8,128]{2,1,0:T(8,128)S(1)} all-to-all(f32[48,8,128]{2,1,0:T(8,128)S(1)} %get-tuple-element.44), channel_id=1, replica_groups=mesh['chord'=48,'span'=16] {'chord'}, dimensions={0} | all-to-all | bytes 393216 | tf_op jit(solution)/shard_map/all_to_all | solution.py:582
  200.4 2.1 later_unpack.3
  202.5 1.9 collective-permute-start.8
  204.5 8.0 %collective-permute-start.9 = (f32[3,8,1536]{2,1,0:T(8,128)S(1)}, f32[3,8,1536]{2,1,0:T(8,128)S(1)}, u32[]{:S(2)}, u32[]{:S(2)}) collective-permute-start(f32[3,8,1536]{2,1,0:T(8,128)S(1)} %get-tuple-element.49), channel_id=1, source_target_pairs={{0,15},{1,0},{2,1},{3,2},{4,3},{5,4},{6,5},{7,6},{8,7},{9,8},{10,9... | collective-permute-start | bytes 442376 | tf_op jit(solution)/shard_map/ppermute | solution.py:589
  212.5 1.7 collective-permute-done.8.low_ref
  214.2 1.8 collective-permute-done.9.high_ref
  216.0 1.6 last_sweeps.1
  217.6 0.2 copy.30
  217.8 0.6 slice_bitcast_fusion
  218.5 0.7 slice.12
  (14 shorter events, 0.1 us)
Async XLA Ops:
  0.6 13.3 %copy-start.2 = (bf16[1024,512]{1,0:T(8,128)(2,1)S(1)}, bf16[1024,512]{1,0:T(8,128)(2,1)}, u32[]{:S(2)}) copy-start(bf16[1024,512]{1,0:T(8,128)(2,1)} %constant.57.clone.pack_ref) | copy-start | bytes 3145732
  0.6 13.3 %copy-start.6 = (bf16[1024,128]{1,0:T(8,128)(2,1)S(1)}, bf16[1024,128]{1,0:T(8,128)(2,1)}, u32[]{:S(2)}) copy-start(bf16[1024,128]{1,0:T(8,128)(2,1)} %constant.55.clone.rim_ref) | copy-start | bytes 786436
  2.0 66.5 %collective-permute-start.3 = (f32[4,16,1024]{2,1,0:T(8,128)S(1)}, f32[4,16,1024]{2,1,0:T(8,128)}, u32[]{:S(2)}, u32[]{:S(2)}) collective-permute-start(f32[4,16,1024]{2,1,0:T(8,128)S(1)} %copy.29.cells_ref.own_ref), channel_id=1, source_target_pairs={{0,15},{1,0},{2,1},{3,2},{4,3},{5,4},{6,5},{7,6},{8,7},{9,8},{10,9... | collective-permute-start | bytes 786440 | tf_op jit(solution)/shard_map/ppermute | solution.py:589
  10.2 58.3 %collective-permute-start.2 = (f32[4,16,1024]{2,1,0:T(8,128)S(1)}, f32[4,16,1024]{2,1,0:T(8,128)}, u32[]{:S(2)}, u32[]{:S(2)}) collective-permute-start(f32[4,16,1024]{2,1,0:T(8,128)S(1)} %copy.29.cells_ref.own_ref), channel_id=1, source_target_pairs={{0,1},{1,2},{2,3},{3,4},{4,5},{5,6},{6,7},{7,8},{8,9},{9,10},{10,1... | collective-permute-start | bytes 786440 | tf_op jit(solution)/shard_map/ppermute | solution.py:588
  14.0 25.0 %slice-start = ((s32[16,2048]{1,0:T(8,128)}), s32[1,2048]{1,0:T(1,128)S(1)}, s32[]{:S(2)}) async-start(s32[16,2048]{1,0:T(8,128)} %param.25), calls=%async_computation.4 | async-start | bytes 16384 | tf_op jit(solution)/shard_map/slice | solution.py:660
  14.0 25.6 %copy-start.8 = (s32[4,4]{1,0:T(4,128)S(1)}, s32[4,4]{1,0:T(4,128)}, u32[]{:S(2)}) copy-start(s32[4,4]{1,0:T(4,128)} %param.23) | copy-start | bytes 196
  14.0 42.8 %copy-start = (bf16[512,1536]{1,0:T(8,128)(2,1)S(1)}, bf16[512,1536]{1,0:T(8,128)(2,1)}, u32[]{:S(2)}) copy-start(bf16[512,1536]{1,0:T(8,128)(2,1)} %constant.59.clone.place_ref) | copy-start | bytes 4718596
  15.3 0.7 copy-start.3
  16.0 40.7 %all-to-all-start = ((f32[48,16,128]{2,1,0:T(8,128)}), f32[48,16,128]{2,1,0:T(8,128)S(1)}, u32[]{:S(2)}, u32[]{:S(2)}) async-start(f32[48,16,128]{2,1,0:T(8,128)} %bitcast.24), calls=%async_computation | async-start | bytes 786432 | tf_op jit(solution)/shard_map/all_to_all | solution.py:582
  56.8 15.2 %copy-start.5 = (bf16[128,1024]{1,0:T(8,128)(2,1)S(1)}, bf16[128,1024]{1,0:T(8,128)(2,1)}, u32[]{:S(2)}) copy-start(bf16[128,1024]{1,0:T(8,128)(2,1)} %constant.56.clone.spread_ref) | copy-start | bytes 786436
  59.0 12.1 %collective-permute-start = (f32[3,8,1792]{2,1,0:T(8,128)S(1)}, f32[3,8,1792]{2,1,0:T(8,128)S(1)}, u32[]{:S(2)}, u32[]{:S(2)}) collective-permute-start(f32[3,8,1792]{2,1,0:T(8,128)S(1)} %get-tuple-element.28), channel_id=1, source_target_pairs={{0,1},{1,2},{2,3},{3,4},{4,5},{5,6},{6,7},{7,8},{8,9},{9,10},{10,1... | collective-permute-start | bytes 516104 | tf_op jit(solution)/shard_map/ppermute | solution.py:588
  61.0 10.9 %collective-permute-start.1 = (f32[3,8,1792]{2,1,0:T(8,128)S(1)}, f32[3,8,1792]{2,1,0:T(8,128)S(1)}, u32[]{:S(2)}, u32[]{:S(2)}) collective-permute-start(f32[3,8,1792]{2,1,0:T(8,128)S(1)} %get-tuple-element.29), channel_id=1, source_target_pairs={{0,15},{1,0},{2,1},{3,2},{4,3},{5,4},{6,5},{7,6},{8,7},{9,8},{10,9... | collective-permute-start | bytes 516104 | tf_op jit(solution)/shard_map/ppermute | solution.py:589
  71.9 41.6 %copy-start.4 = (f32[8,1536]{1,0:T(8,128)S(1)}, f32[8,1536]{1,0:T(8,128)}, u32[]{:S(2)}) copy-start(f32[8,1536]{1,0:T(8,128)} %constant.60.clone.mask_ref) | copy-start | bytes 147460
  77.5 55.1 %copy-start.1 = (bf16[1536,512]{1,0:T(8,128)(2,1)S(1)}, bf16[1536,512]{1,0:T(8,128)(2,1)}, u32[]{:S(2)}) copy-start(bf16[1536,512]{1,0:T(8,128)(2,1)} %constant.58.clone.pack_ref) | copy-start | bytes 4718596
  117.7 14.0 %collective-permute-start.4 = (f32[5,8,1536]{2,1,0:T(8,128)S(1)}, f32[5,8,1536]{2,1,0:T(8,128)S(1)}, u32[]{:S(2)}, u32[]{:S(2)}) collective-permute-start(f32[5,8,1536]{2,1,0:T(8,128)S(1)} %get-tuple-element.35), channel_id=1, source_target_pairs={{0,1},{1,2},{2,3},{3,4},{4,5},{5,6},{6,7},{7,8},{8,9},{9,10},{10,1... | collective-permute-start | bytes 737288 | tf_op jit(solution)/shard_map/ppermute | solution.py:588
  119.6 13.0 %collective-permute-start.5 = (f32[5,8,1536]{2,1,0:T(8,128)S(1)}, f32[5,8,1536]{2,1,0:T(8,128)S(1)}, u32[]{:S(2)}, u32[]{:S(2)}) collective-permute-start(f32[5,8,1536]{2,1,0:T(8,128)S(1)} %get-tuple-element.36), channel_id=1, source_target_pairs={{0,15},{1,0},{2,1},{3,2},{4,3},{5,4},{6,5},{7,6},{8,7},{9,8},{10,9... | collective-permute-start | bytes 737288 | tf_op jit(solution)/shard_map/ppermute | solution.py:589
  132.6 27.1 %copy-start.7 = (f32[8,1536]{1,0:T(8,128)S(1)}, f32[8,1536]{1,0:T(8,128)}, u32[]{:S(2)}) copy-start(f32[8,1536]{1,0:T(8,128)} %constant.61.clone.block_ref) | copy-start | bytes 147460
  161.9 11.7 %collective-permute-start.6 = (f32[3,8,1536]{2,1,0:T(8,128)S(1)}, f32[3,8,1536]{2,1,0:T(8,128)S(1)}, u32[]{:S(2)}, u32[]{:S(2)}) collective-permute-start(f32[3,8,1536]{2,1,0:T(8,128)S(1)} %get-tuple-element.41), channel_id=1, source_target_pairs={{0,1},{1,2},{2,3},{3,4},{4,5},{5,6},{6,7},{7,8},{8,9},{9,10},{10,1... | collective-permute-start | bytes 442376 | tf_op jit(solution)/shard_map/ppermute | solution.py:588
  163.8 11.6 %collective-permute-start.7 = (f32[3,8,1536]{2,1,0:T(8,128)S(1)}, f32[3,8,1536]{2,1,0:T(8,128)S(1)}, u32[]{:S(2)}, u32[]{:S(2)}) collective-permute-start(f32[3,8,1536]{2,1,0:T(8,128)S(1)} %get-tuple-element.42), channel_id=1, source_target_pairs={{0,15},{1,0},{2,1},{3,2},{4,3},{5,4},{6,5},{7,6},{8,7},{9,8},{10,9... | collective-permute-start | bytes 442376 | tf_op jit(solution)/shard_map/ppermute | solution.py:589
  202.5 11.7 %collective-permute-start.8 = (f32[3,8,1536]{2,1,0:T(8,128)S(1)}, f32[3,8,1536]{2,1,0:T(8,128)S(1)}, u32[]{:S(2)}, u32[]{:S(2)}) collective-permute-start(f32[3,8,1536]{2,1,0:T(8,128)S(1)} %get-tuple-element.48), channel_id=1, source_target_pairs={{0,1},{1,2},{2,3},{3,4},{4,5},{5,6},{6,7},{7,8},{8,9},{9,10},{10,1... | collective-permute-start | bytes 442376 | tf_op jit(solution)/shard_map/ppermute | solution.py:588
  204.5 11.6 %collective-permute-start.9 = (f32[3,8,1536]{2,1,0:T(8,128)S(1)}, f32[3,8,1536]{2,1,0:T(8,128)S(1)}, u32[]{:S(2)}, u32[]{:S(2)}) collective-permute-start(f32[3,8,1536]{2,1,0:T(8,128)S(1)} %get-tuple-element.49), channel_id=1, source_target_pairs={{0,15},{1,0},{2,1},{3,2},{4,3},{5,4},{6,5},{7,6},{8,7},{9,8},{10,9... | collective-permute-start | bytes 442376 | tf_op jit(solution)/shard_map/ppermute | solution.py:589

commit v2 on v1

v2 whole, which is shorter than its diff:
```python
import math

import jax
import jax.numpy as jnp
import ml_dtypes
import numpy as np
from jax import lax
from jax.experimental import pallas as pl
from jax.experimental.pallas import tpu as pltpu
from jax.sharding import PartitionSpec as P

EDGE = 32
CELLS = EDGE * EDGE
NB = 4
SZ = 4
DEPTH = 3
STRIDE = 40
WIDTH = 1536
LANES = 128
SEG = 4 * LANES
F32 = jnp.float32
BF16 = jnp.bfloat16


def place_of(i, k):
    return STRIDE * (i + DEPTH) + k + 4


def edge_cell(side, depth, x):
    return [(depth, x), (EDGE - 1 - depth, x), (x, depth), (x, EDGE - 1 - depth)][side]


def ghost_cell(side, depth, x):
    return [(-1 - depth, x), (EDGE + depth, x), (x, -1 - depth), (x, EDGE + depth)][side]


def pack_matrix(rows, where):
    table = np.zeros((rows, SEG), np.float32)
    for side in range(4):
        for depth in range(DEPTH):
            for x in range(EDGE):
                table[where(*edge_cell(side, depth, x)), side * LANES + depth * EDGE + x] = 1
        for corner in range(4):
            for cell in range(4):
                i, k = cell // 2, cell % 2
                i = i if corner // 2 == 0 else EDGE - 1 - i
                k = k if corner % 2 == 0 else EDGE - 1 - k
                table[where(i, k), side * LANES + 96 + corner * 4 + cell] = 1
    return table.astype(ml_dtypes.bfloat16)


def place_matrix():
    table = np.zeros((SEG, WIDTH), np.float32)
    for side in range(4):
        for depth in range(DEPTH):
            for x in range(EDGE):
                table[side * LANES + depth * EDGE + x, place_of(*ghost_cell(side, depth, x))] = 1
    for vertex in range(4):
        for cell in range(3):
            i, k = cell // 2, cell % 2
            i = -1 - i if vertex // 2 == 0 else EDGE + i
            k = -1 - k if vertex % 2 == 0 else EDGE + k
            table[vertex * LANES + 96 + cell, place_of(i, k)] = 1
    return table.astype(ml_dtypes.bfloat16)


def spread_matrix():
    table = np.zeros((SEG, WIDTH), np.float32)
    for side in range(4):
        for depth in range(2):
            for x in range(EDGE):
                table[side * LANES + depth * EDGE + x, place_of(*ghost_cell(side, depth, x))] = 1
        for x in range(EDGE):
            table[side * LANES + 2 * EDGE + x, place_of(*edge_cell(side, 0, x))] = 0.5 if side % 2 else -0.5
    for vertex in range(4):
        lane = vertex * LANES + 96
        i, k = vertex_cell(vertex)
        in_i, in_k = (1, 1) if vertex == 0 else (1, -1) if vertex == 1 else (-1, 1) if vertex == 2 else (-1, -1)
        table[lane, place_of(i, k)] = 1
        table[lane + 1, place_of(i, k + in_k)] = -0.5 * in_k
        table[lane + 2, place_of(i - in_i, k + in_k)] = -0.5 * in_k
        table[lane + 3, place_of(i + in_i, k)] = -0.5 * in_i
        table[lane + 4, place_of(i + in_i, k - in_k)] = -0.5 * in_i
        table[lane + 5, place_of(i, k)] = 0.5 * in_i
        table[lane + 6, place_of(i, k)] = 0.5 * in_k
    return table.astype(ml_dtypes.bfloat16)


def rim_matrix():
    table = np.zeros((CELLS, LANES), np.float32)
    for side in range(4):
        for x in range(EDGE):
            i, k = edge_cell(side, 0, x)
            table[i * EDGE + k, side * EDGE + x] = 1
    return table.astype(ml_dtypes.bfloat16)


def sheet_mask():
    mask = np.zeros((8, WIDTH), np.float32)
    for i in range(-DEPTH, EDGE + DEPTH):
        for k in range(-DEPTH, EDGE + DEPTH):
            inside_i, inside_k = 0 <= i < EDGE, 0 <= k < EDGE
            if inside_i and not inside_k:
                mask[:4, place_of(i, k)] = 1
            if inside_k and not inside_i:
                mask[4:, place_of(i, k)] = 1
    return mask


def block_mask():
    mask = np.zeros((8, WIDTH), np.float32)
    for i in range(EDGE):
        mask[:, place_of(i, 0) : place_of(i, 0) + EDGE] = 1
    return mask


def vertex_cell(vertex):
    return -1 if vertex // 2 == 0 else EDGE, -1 if vertex % 2 == 0 else EDGE


def vertex_place(vertex):
    return place_of(*vertex_cell(vertex))


def pick(x, table):
    high = x.astype(BF16)
    rest = x - high.astype(F32)
    middle = rest.astype(BF16)
    low = (rest - middle.astype(F32)).astype(BF16)
    parts = jnp.dot(jnp.concatenate([high, middle, low], axis=0), table, preferred_element_type=F32)
    rows = x.shape[0]
    return (parts[:rows] + parts[rows : 2 * rows]) + parts[2 * rows :]


def shifted(x, lanes):
    return pltpu.roll(x, lanes % x.shape[1], axis=1)


def lane_ids(rows):
    return lax.broadcasted_iota(jnp.int32, (rows, LANES), 1)


def remap(x, width, pieces):
    rows = x.shape[0]
    lane = lane_ids(rows)
    out = []
    for tile in range(width // LANES):
        acc = jnp.zeros((rows, LANES), F32)
        base = tile * LANES
        for src, dst in pieces:
            first, last = max(dst, base), min(dst + EDGE, base + LANES)
            while first < last:
                at = src + first - dst
                column = at // LANES
                stop = min(last, first + (column + 1) * LANES - at)
                value = x[:, column * LANES : (column + 1) * LANES]
                turn = (first - base - at % LANES) % LANES
                if turn:
                    value = pltpu.roll(value, turn, axis=1)
                acc = jnp.where((lane >= first - base) & (lane < stop - base), value, acc)
                first = stop
        out.append(acc)
    return jnp.concatenate(out, axis=1)


def expand(x):
    return remap(x, WIDTH, [(EDGE * i, place_of(i, 0)) for i in range(EDGE)])


def compact(x):
    return remap(x, CELLS, [(place_of(i, 0), EDGE * i) for i in range(EDGE)])


def store_table(rows_of, table_ref, field, fields):
    lane = lane_ids(NB)
    for layer in range(SZ):
        for side in range(4):
            rows = rows_of(layer, side)
            turned = pltpu.roll(rows, 16, axis=1)
            for slot in range(2):
                low = jnp.broadcast_to(rows[2 * slot : 2 * slot + 1], rows.shape)
                high = jnp.broadcast_to(turned[2 * slot + 1 : 2 * slot + 2], rows.shape)
                value = jnp.where(lane < 96, rows, jnp.where(lane < 112, low, high))
                for block in range(NB):
                    entry = (slot * fields + field) * 16 + block * 4 + side
                    at = slot * SZ + layer
                    table_ref[entry, at : at + 1, :] = value[block : block + 1]


def segments(strips, row):
    return lambda layer, side: strips[layer, row : row + NB, side * LANES : (side + 1) * LANES]


def post(send_ref, table_ref, out_ref, fields, count):
    def one(target, carry):
        first = jnp.maximum(send_ref[0, target], 0)
        second = jnp.maximum(send_ref[1, target], 0)
        for field in range(fields):
            out_ref[target * fields + field] = (
                table_ref[field * 16 + first] + table_ref[(fields + field) * 16 + second]
            )
        return carry

    lax.fori_loop(0, count, one, 0, unroll=4)


def first_pack(
    send_any, velocity_any, p_any, rim_any, pack_any, out_ref,
    send_ref, velocity_ref, p_ref, rim_ref, pack_ref, table_ref, done_ref,
):
    copies = [
        pltpu.make_async_copy(source, target, done_ref.at[at])
        for at, (source, target) in enumerate(
            (
                (velocity_any, velocity_ref), (rim_any, rim_ref), (p_any, p_ref), (pack_any, pack_ref), (send_any, send_ref),
            )
        )
    ]
    for copy in copies:
        copy.start()
    table_ref[...] = jnp.zeros(table_ref.shape, F32)
    lane = lane_ids(SZ)
    copies[0].wait()
    copies[1].wait()
    rims = pick(velocity_ref[...].reshape(3 * NB * SZ, CELLS), rim_ref[...])
    for block in range(NB):
        for side in range(4):
            value = jnp.zeros((SZ, LANES), F32)
            for comp in range(3):
                first = (comp * NB + block) * SZ
                part = rims[first : first + SZ]
                turn = EDGE * (comp - side) % LANES
                if turn:
                    part = pltpu.roll(part, turn, axis=1)
                value = jnp.where(lane // EDGE == comp, part, value)
            for slot in range(2):
                table_ref[slot * 32 + block * 4 + side, slot * SZ : (slot + 1) * SZ, :] = value
    copies[2].wait()
    copies[3].wait()
    strips = pick(p_ref[...].reshape(NB * SZ, CELLS), pack_ref[...])
    for side in range(4):
        parts = [strips[block * SZ : (block + 1) * SZ, side * LANES : (side + 1) * LANES] for block in range(NB)]
        for slot in range(2):
            patch = jnp.where(lane < 112, parts[2 * slot], pltpu.roll(parts[2 * slot + 1], 16, axis=1))
            for block in range(NB):
                value = jnp.where(lane < 96, parts[block], patch)
                table_ref[slot * 32 + 16 + block * 4 + side, slot * SZ : (slot + 1) * SZ, :] = value
    copies[4].wait()
    post(send_ref, table_ref, out_ref, 2, out_ref.shape[0] // 2)


def routes(me_ref, send_ref, recv_ref, out_ref, near_ref):
    me, count = me_ref[0], send_ref.shape[1]
    for edge in range(16):
        block, side = edge // 4, edge % 4
        entry = recv_ref[block, side]
        source, slot = entry // 2, entry % 2
        out_ref[2 * edge], out_ref[2 * edge + 1] = source, slot
        back = lax.rem(2 * me - source + count, count)
        near_ref[edge] = send_ref[slot, back] // 4
        near_ref[16 + edge] = lax.rem(source - me + count, count)
    for block in range(NB):
        for vertex in range(4):
            i_side, k_side = vertex // 2, 2 + vertex % 2
            for sheet, (side, then) in enumerate(((i_side, k_side), (k_side, i_side))):
                at, offset = block, 0
                for step, across in enumerate((side, then, side ^ 1)):
                    edge = at * 4 + across
                    at, offset = near_ref[edge], offset + near_ref[16 + edge]
                    place = route_at(block, vertex, sheet, step)
                    out_ref[place] = lax.rem(me + offset, count)
                    out_ref[place + 1] = at // 2
                    out_ref[place + 2] = 96 + (at % 2) * 16


def route_at(block, vertex, sheet, step):
    return 32 + (((block * 4 + vertex) * 2 + sheet) * 3 + step) * 3


ROUTES = 32 + 32 * 9


def near_rows(got_ref, source, slot, field, fields):
    rows = got_ref[source * fields + field]
    return jnp.where(slot == 1, pltpu.roll(rows, SZ, axis=0), rows)


def strip_rows_of(got_ref, route_ref, block, side, field, fields):
    edge = block * 4 + side
    return near_rows(got_ref, route_ref[2 * edge], route_ref[2 * edge + 1], field, fields)


def patch_rows(got_ref, route_ref, place, corner, field, fields, target, cell):
    rows = near_rows(got_ref, route_ref[place], route_ref[place + 1], field, fields)
    turn = target - (corner * 4 + cell) + 2 * LANES - route_ref[place + 2]
    return pltpu.roll(rows, lax.rem(turn, LANES), axis=1)


def gather_ghosts(got_ref, route_ref, ghost_ref, field, fields):
    lane = lane_ids(8)
    for block in range(NB):
        for vertex in range(4):
            strip = strip_rows_of(got_ref, route_ref, block, vertex, field, fields)
            far = (1 - vertex // 2) * 2 + 1 - vertex % 2
            for sheet in range(2):
                twice, thrice = (route_at(block, vertex, sheet, step) for step in (1, 2))
                second = patch_rows(got_ref, route_ref, twice, far, field, fields, 96, 0)
                beyond = far ^ 2 if sheet == 0 else far ^ 1
                third = patch_rows(got_ref, route_ref, thrice, beyond, field, fields, 100, 0)
                value = jnp.where(
                    lane < 96, strip, jnp.where(lane < 100, second, jnp.where(lane == 100, third, 0.0))
                )
                row = sheet * NB + block
                for layer in range(SZ):
                    ghost_ref[layer, row : row + 1, vertex * LANES : (vertex + 1) * LANES] = value[
                        layer : layer + 1
                    ]


def third_cells(ghosts):
    lane = lane_ids(8)
    tiles = [jnp.zeros((8, LANES), F32) for _ in range(WIDTH // LANES)]
    for vertex in range(4):
        tile, at = vertex_place(vertex) // LANES, vertex_place(vertex) % LANES
        value = pltpu.roll(ghosts[:, vertex * LANES : (vertex + 1) * LANES], (at - 100) % LANES, axis=1)
        tiles[tile] = jnp.where(lane == at, value, tiles[tile])
    return jnp.concatenate(tiles, axis=1)


def vertex_masks():
    lane = lax.broadcasted_iota(jnp.int32, (8, WIDTH), 1)
    first = lax.broadcasted_iota(jnp.int32, (8, WIDTH), 0) < NB
    places = [vertex_place(v) for v in range(4)]
    west = first & ((lane == places[0]) | (lane == places[1]))
    east = first & ((lane == places[2]) | (lane == places[3]))
    south = ~first & ((lane == places[0]) | (lane == places[2]))
    north = ~first & ((lane == places[1]) | (lane == places[3]))
    return west, east, south, north


def corrections(ext, third):
    west, east, south, north = vertex_masks()
    return (
        jnp.where(west, third - shifted(ext, -STRIDE), 0.0),
        jnp.where(east, third - shifted(ext, STRIDE), 0.0),
        jnp.where(south, third - shifted(ext, -1), 0.0),
        jnp.where(north, third - shifted(ext, 1), 0.0),
    )


def fold(ext):
    lane, last = lane_ids(NB), ext[:NB, WIDTH - LANES :]
    for vertex in range(4):
        tile, at = vertex_place(vertex) // LANES * LANES, vertex_place(vertex) % LANES
        value = pltpu.roll(ext[NB:, tile : tile + LANES], (112 + vertex - at) % LANES, axis=1)
        last = jnp.where(lane == 112 + vertex, value, last)
    return jnp.concatenate([ext[:NB, : WIDTH - LANES], last], axis=1)


def unfold(rows):
    lane, last = lane_ids(NB), rows[:, WIDTH - LANES : WIDTH]
    tiles = [rows[:, at : at + LANES] for at in range(0, WIDTH, LANES)]
    for vertex in range(4):
        tile, at = vertex_place(vertex) // LANES, vertex_place(vertex) % LANES
        value = pltpu.roll(last, (at - 112 - vertex) % LANES, axis=1)
        tiles[tile] = jnp.where(lane == at, value, tiles[tile])
    return jnp.concatenate([rows[:, :WIDTH], jnp.concatenate(tiles, axis=1)], axis=0)


def merge(x, mask):
    return jnp.where(mask, pltpu.roll(x, NB, axis=0), x)


def second_halves(x):
    return jnp.concatenate([x, x], axis=0)


def unpack_pressure(own, got_ref, route_ref, ghost_ref, place_ref, own_ref, corr_ref, field, fields, up, down):
    gather_ghosts(got_ref, route_ref, ghost_ref, field, fields)
    placed = pick(ghost_ref[...].reshape(SZ * 8, SEG), place_ref[...])
    for layer in range(SZ):
        ext = own(layer) + placed[layer * 8 : (layer + 1) * 8]
        own_ref[layer] = ext
        corr_ref[layer] = sum(corrections(ext, third_cells(ghost_ref[layer])))
        if layer >= 1:
            up[layer - 1, :, :WIDTH] = fold(ext)
        if layer < SZ - 1:
            down[layer, :, :WIDTH] = fold(ext)


def first_unpack(
    route_ref, got_ref, p_ref, place_ref, own_ref, corr_ref, rim_ref, up_ref, down_ref, ghost_ref, block_ref
):
    lane = lane_ids(8)
    for block in range(NB):
        strips = [strip_rows_of(got_ref, route_ref, block, side, 0, 2) for side in range(4)]
        for comp in range(4):
            value = jnp.zeros((8, LANES), F32)
            if comp < 3:
                for side in range(4):
                    turn = EDGE * (side - comp) % LANES
                    part = pltpu.roll(strips[side], turn, axis=1) if turn else strips[side]
                    value = jnp.where(lane // EDGE == side, part, value)
            row = comp * NB + block
            for layer in range(SZ):
                rim_ref[layer, row : row + 1, :] = value[layer : layer + 1]
    for block in range(NB):
        rows = expand(p_ref[block])
        for sheet in range(2):
            block_ref[:, sheet * NB + block, :] = rows
    unpack_pressure(
        lambda layer: block_ref[layer], got_ref, route_ref, ghost_ref, place_ref, own_ref, corr_ref, 1, 2, up_ref, down_ref
    )
    for layer in range(SZ):
        for comp in range(3):
            rows = rim_ref[layer, comp * NB : (comp + 1) * NB, :]
            at = WIDTH + comp * LANES
            if layer >= 1:
                up_ref[layer - 1, :, at : at + LANES] = rows
            if layer < SZ - 1:
                down_ref[layer, :, at : at + LANES] = rows


def later_unpack(
    route_ref, got_ref, p_ref, place_ref, block_ref, own_ref, corr_ref, up_ref, down_ref, ghost_ref
):
    unpack_pressure(
        lambda layer: jnp.where(block_ref[...] > 0.0, p_ref[layer], 0.0),
        got_ref, route_ref, ghost_ref, place_ref, own_ref, corr_ref, 0, 1, up_ref, down_ref,
    )


def rim_rows(ref, layer):
    rows = [ref[layer, :, at : at + LANES] for at in range(WIDTH, WIDTH + 3 * LANES, LANES)]
    return jnp.concatenate(rows + [jnp.zeros((NB, LANES), F32)], axis=0)


def weigh(
    at_ref, block_ref, cells_ref, layer_ref, fraction_ref, weight_ref, target_ref, plane_ref, span_ref, aim_ref
):
    group = plane_ref.shape[1] // 2
    along = lax.broadcasted_iota(jnp.int32, (EDGE, group), 0)
    for which in range(2):
        lanes = pl.ds(pl.multiple_of(at_ref[which] * group, group), group)
        here = slice(which * group, (which + 1) * group)
        corner = cells_ref[0:1, lanes]
        row_i, row_k = corner // EDGE, corner % EDGE
        weight = weight_ref[:, lanes]
        lines = []
        for a in range(4):
            line = jnp.zeros((EDGE, group), F32)
            for b in range(4):
                line = jnp.where(along == row_k + b, weight[4 * a + b : 4 * a + b + 1], line)
            lines.append(line)
        for i in range(EDGE):
            value = jnp.zeros((EDGE, group), F32)
            for a in range(4):
                value = jnp.where(row_i + a == i, lines[a], value)
            plane_ref[i * EDGE : (i + 1) * EDGE, here] = value
        start = layer_ref[:, lanes] - (at_ref[which] + which) * SZ
        fraction = fraction_ref[:, lanes]
        phi = [0.25 * (1.0 + jnp.cos(0.5 * math.pi * distance)) for distance in
               (1.0 + fraction, fraction, 1.0 - fraction, 2.0 - fraction)]
        for at in range(SZ + 2 * DEPTH):
            value = jnp.zeros((1, group), F32)
            for a in range(4):
                value = jnp.where(start + a == at - DEPTH, phi[a], value)
            span_ref[at : at + 1, here] = value
        aim_ref[0:3, here] = target_ref[:, lanes]
        aim_ref[3:4, here] = block_ref[:, lanes].astype(F32)


def diffused(cells_at, rims, spread, layer):
    cell = lax.broadcasted_iota(jnp.int32, (16, CELLS), 1)
    here = cells_at(layer)
    around = jnp.where(cell >= EDGE, shifted(here, EDGE), 0.0)
    around += jnp.where(cell < CELLS - EDGE, shifted(here, -EDGE), 0.0)
    around += jnp.where(cell % EDGE != 0, shifted(here, 1), 0.0)
    around += jnp.where(cell % EDGE != EDGE - 1, shifted(here, -1), 0.0)
    around += pick(rims, spread)
    around += cells_at(layer - 1) + cells_at(layer + 1)
    eddy = second_halves(second_halves(here[3 * NB :]))
    return here + eddy * (around - 6.0 * here)


def span_row(span_ref, layer):
    return span_ref[layer + DEPTH : layer + DEPTH + 1, :]


def layers_of(own_ref, low_ref, high_ref):
    def at(layer):
        if layer < 0:
            return low_ref[layer + SZ]
        return own_ref[layer] if layer < SZ else high_ref[layer - SZ]

    return at


def samples(tilde_ref, plane_ref, weights):
    dots = jnp.dot(
        tilde_ref[...].reshape(len(weights) * 16, CELLS), plane_ref[...],
        precision=lax.Precision.HIGHEST, preferred_element_type=F32,
    )
    return sum(weight * dots[at * 16 : (at + 1) * 16] for at, weight in enumerate(weights))


def own_layers(
    own_ref, low_ref, high_ref, rim_ref, spread_ref, plane_ref, span_ref, tilde_ref, total_ref
):
    cells_at = layers_of(own_ref, low_ref, high_ref)
    for layer in range(SZ):
        tilde_ref[layer] = diffused(cells_at, rim_ref[layer], spread_ref[...], layer)
    total_ref[...] = samples(tilde_ref, plane_ref, [span_row(span_ref, layer) for layer in range(SZ)])


def forcing(
    send_ref, count_ref, own_ref, low_ref, high_ref, tilde_ref, total_ref, rim_low_ref, rim_high_ref, spread_ref,
    pack_ref, plane_ref, span_ref, aim_ref,
    star_ref, out_ref, beside_ref, table_ref, strips_ref,
):
    markers = plane_ref.shape[1]
    group = markers // 2
    cells_at = layers_of(own_ref, low_ref, high_ref)
    halo = [-3, -2, -1, SZ, SZ + 1, SZ + 2]
    for at, layer in enumerate(halo):
        rims = rim_rows(rim_low_ref, layer + SZ - 1) if layer < 0 else rim_rows(rim_high_ref, layer - SZ)
        beside_ref[at] = diffused(cells_at, rims, spread_ref[...], layer)
    total = total_ref[...] + samples(beside_ref, plane_ref, [span_row(span_ref, layer) for layer in halo])
    mine = (lax.broadcasted_iota(jnp.int32, (16, markers), 0) % NB).astype(F32) == aim_ref[3:4, :]
    total = jnp.where(mine, total, 0.0)
    place = lax.broadcasted_iota(jnp.int32, (1, markers), 1) % group
    live = place < count_ref[0]
    rows = []
    for comp in range(3):
        sampled = jnp.sum(total[comp * NB : (comp + 1) * NB], axis=0, keepdims=True)
        force = jnp.where(live, aim_ref[comp : comp + 1, :] - sampled, 0.0)
        rows.append(jnp.broadcast_to(force, (NB, markers)))
    rows.append(jnp.zeros((NB, markers), F32))
    force = jnp.where(mine, jnp.concatenate(rows, axis=0), 0.0)
    pushes = jnp.concatenate([span_row(span_ref, layer) * force for layer in range(SZ)], axis=0)
    spread = lax.dot_general(
        pushes, plane_ref[...], (((1,), (1,)), ((), ())),
        precision=lax.Precision.HIGHEST, preferred_element_type=F32,
    )
    star = tilde_ref[...].reshape(SZ * 16, CELLS) + spread
    planes = []
    cell = lax.broadcasted_iota(jnp.int32, (NB, CELLS), 1)
    for layer in range(SZ):
        rows = star[layer * 16 : (layer + 1) * 16]
        first, second = rows[:NB], rows[NB : 2 * NB]
        inner = jnp.where(cell < CELLS - EDGE, shifted(first, -EDGE), 0.0)
        inner -= jnp.where(cell >= EDGE, shifted(first, EDGE), 0.0)
        inner += jnp.where(cell % EDGE != EDGE - 1, shifted(second, -1), 0.0)
        inner -= jnp.where(cell % EDGE != 0, shifted(second, 1), 0.0)
        planes.append(jnp.concatenate([rows[: 3 * NB], 0.5 * inner], axis=0))
        star_ref[layer] = planes[layer]
    table_ref[...] = jnp.zeros(table_ref.shape, F32)
    strips_ref[...] = pick(jnp.concatenate(planes, axis=0), pack_ref[...]).reshape(SZ, 16, SEG)
    lane = lane_ids(NB)
    comps = [segments(strips_ref, comp * NB) for comp in range(4)]

    def corners(values):
        out = values[0]
        for at in range(1, 4):
            out = jnp.where(lane % 4 == at, values[at], out)
        return out

    def flat_rows(layer, side):
        first, second, inner = (comps[comp](layer, side) for comp in (0, 1, 3))
        edge = pltpu.roll(first if side < 2 else second, 2 * EDGE, axis=1)
        turned = pltpu.roll(first, 1, axis=1)
        patch = corners([inner, turned, turned, pltpu.roll(second, 3, axis=1)])
        return jnp.where(lane < 2 * EDGE, inner, jnp.where(lane < 96, edge, patch))

    def third_rows(layer, side):
        third = comps[2](layer, side)
        patch = jnp.where(lane % 4 == 1, pltpu.roll(comps[1](layer, side), LANES - 1, axis=1), third)
        return jnp.where(lane < 96, third, patch)

    store_table(flat_rows, table_ref, 0, 2)
    store_table(third_rows, table_ref, 1, 2)
    post(send_ref, table_ref, out_ref, 2, out_ref.shape[0] // 2)


def gather_star(got_ref, route_ref, flat_ghost_ref, third_ghost_ref):
    lane = lane_ids(8)
    for block in range(NB):
        for vertex in range(4):
            strip = strip_rows_of(got_ref, route_ref, block, vertex, 0, 2)
            third_strip = strip_rows_of(got_ref, route_ref, block, vertex, 1, 2)
            far = (1 - vertex // 2) * 2 + 1 - vertex % 2
            for sheet in range(2):

                def cell(step, corner, field, index, target):
                    place = route_at(block, vertex, sheet, step)
                    return patch_rows(got_ref, route_ref, place, corner, field, 2, target, index)

                beside = cell(0, far ^ (1 if sheet == 0 else 2), 0, 3 if sheet == 0 else 1, 102 - sheet)
                value = jnp.where(lane < 96, strip, 0.0)
                value = jnp.where(lane == 96, cell(1, far, 0, 0, 96), value)
                across = cell(1, far, 0, 3 if sheet == 0 else 1, 97 + 2 * sheet)
                value = jnp.where(lane == 97 + 2 * sheet, across, value)
                if sheet == 0:
                    deeper = cell(1, far, 1, 1, 98)
                else:
                    deeper = cell(1, far, 0, 2, 100)
                value = jnp.where(lane == 98 + 2 * sheet, deeper, value)
                third = jnp.where(lane == 96, cell(1, far, 1, 0, 96), 0.0)
                third = jnp.where(lane < 96, third_strip, third)
                beyond = far ^ 2 if sheet == 0 else far ^ 1
                last = cell(2, beyond, 0, 1 if sheet == 0 else 3, 101 + sheet)
                value = jnp.where(lane == 101 + sheet, last, value)
                value = jnp.where(lane == 102 - sheet, beside, value)
                row, at = sheet * NB + block, slice(vertex * LANES, (vertex + 1) * LANES)
                for layer in range(SZ):
                    flat_ghost_ref[layer, row : row + 1, at] = value[layer : layer + 1]
                    third_ghost_ref[layer, row : row + 1, at] = third[layer : layer + 1]


def star_unpack(
    route_ref, got_ref, star_ref, spread_ref, place_ref, mask_ref,
    flat_ref, third_ref, up_ref, down_ref, flat_ghost_ref, third_ghost_ref,
):
    gather_star(got_ref, route_ref, flat_ghost_ref, third_ghost_ref)
    flat_placed = pick(flat_ghost_ref[...].reshape(SZ * 8, SEG), spread_ref[...])
    third_placed = pick(third_ghost_ref[...].reshape(SZ * 8, SEG), place_ref[...])
    mask = mask_ref[...] > 0.0
    lane = lax.broadcasted_iota(jnp.int32, (NB, WIDTH), 1)
    row, column = lane // STRIDE - DEPTH, lane % STRIDE - 4
    flats, thirds = [], []
    for layer in range(SZ):
        whole = expand(star_ref[layer])
        first, second = whole[:NB], whole[NB : 2 * NB]
        flat = whole[3 * NB :]
        flat += jnp.where(row == EDGE, -0.5 * shifted(first, STRIDE), 0.0)
        flat += jnp.where(row == -1, 0.5 * shifted(first, -STRIDE), 0.0)
        flat += jnp.where(column == EDGE, -0.5 * shifted(second, 1), 0.0)
        flat += jnp.where(column == -1, 0.5 * shifted(second, -1), 0.0)
        at = layer * 8
        flats.append(merge(second_halves(flat) + flat_placed[at : at + 8], mask))
        thirds.append(second_halves(whole[2 * NB : 3 * NB]) + third_placed[at : at + 8])
        flat_ref[layer] = flats[layer]
        third_ref[layer] = thirds[layer]
    up_ref[0] = (flats[2] + 0.5 * (thirds[3] - thirds[1]))[:NB]
    up_ref[1] = (flats[3] - 0.5 * thirds[2])[:NB]
    up_ref[2] = fold(thirds[3])
    down_ref[0] = fold(thirds[0])
    down_ref[1] = (flats[0] + 0.5 * thirds[1])[:NB]
    down_ref[2] = (flats[1] + 0.5 * (thirds[2] - thirds[0]))[:NB]


def sweep(source, target, first, last, rhs_ref, corr_ref, mask):
    for at in range(first, last):
        here = source[at]
        around = (shifted(here, STRIDE) + shifted(here, -STRIDE)) + (shifted(here, 1) + shifted(here, -1))
        around += source[at - 1] + source[at + 1]
        around -= rhs_ref[at - 1]
        if corr_ref is not None and DEPTH <= at < DEPTH + SZ:
            around += corr_ref[at - DEPTH]
        target[at] = merge(around * (1.0 / 6.0), mask)


def load_layers(work_ref, own_ref, low_ref, high_ref):
    for layer in range(DEPTH):
        work_ref[layer] = unfold(low_ref[layer])
        work_ref[DEPTH + SZ + layer] = unfold(high_ref[layer])
    for layer in range(SZ):
        work_ref[DEPTH + layer] = own_ref[layer]


def three_sweeps(work_ref, other_ref, rhs_ref, corr_ref, mask):
    sweep(work_ref, other_ref, 1, 9, rhs_ref, corr_ref, mask)
    sweep(other_ref, work_ref, 2, 8, rhs_ref, None, mask)
    sweep(work_ref, other_ref, 3, 7, rhs_ref, None, mask)


def send_pressure(send_ref, done_ref, pack_ref, p_ref, out_ref, table_ref, strips_ref):
    p_ref[...] = done_ref[DEPTH : DEPTH + SZ]
    table_ref[...] = jnp.zeros(table_ref.shape, F32)
    strips_ref[...] = pick(p_ref[...].reshape(SZ * 8, WIDTH), pack_ref[...]).reshape(SZ, 8, SEG)
    store_table(segments(strips_ref, 0), table_ref, 0, 1)
    post(send_ref, table_ref, out_ref, 1, out_ref.shape[0])


def first_sweeps(
    send_ref, own_ref, corr_ref, low_ref, high_ref, flat_ref, third_ref, star_low_ref, star_high_ref, mask_ref, pack_ref,
    p_ref, rhs_ref, out_ref, work_ref, other_ref, table_ref, strips_ref,
):
    mask = mask_ref[...] > 0.0
    load_layers(work_ref, own_ref, low_ref, high_ref)

    thirds = [unfold(star_low_ref[2])] + [third_ref[layer] for layer in range(SZ)] + [unfold(star_high_ref[0])]
    for layer in range(SZ):
        rhs_ref[layer + 2] = flat_ref[layer] + 0.5 * (thirds[layer + 2] - thirds[layer])
    rhs_ref[0] = second_halves(star_low_ref[0])
    rhs_ref[1] = second_halves(star_low_ref[1]) + 0.5 * thirds[1]
    rhs_ref[SZ + 2] = second_halves(star_high_ref[1]) - 0.5 * thirds[SZ]
    rhs_ref[SZ + 3] = second_halves(star_high_ref[2])
    three_sweeps(work_ref, other_ref, rhs_ref, corr_ref, mask)
    send_pressure(send_ref, other_ref, pack_ref, p_ref, out_ref, table_ref, strips_ref)


def later_sweeps(
    send_ref, own_ref, corr_ref, low_ref, high_ref, rhs_ref, mask_ref, pack_ref,
    p_ref, out_ref, work_ref, other_ref, table_ref, strips_ref,
):
    load_layers(work_ref, own_ref, low_ref, high_ref)
    three_sweeps(work_ref, other_ref, rhs_ref, corr_ref, mask_ref[...] > 0.0)
    send_pressure(send_ref, other_ref, pack_ref, p_ref, out_ref, table_ref, strips_ref)


def last_sweeps(
    own_ref, corr_ref, low_ref, high_ref, rhs_ref, mask_ref, star_ref, velocity_ref, p_ref, work_ref, other_ref
):
    mask = mask_ref[...] > 0.0
    load_layers(work_ref, own_ref, low_ref, high_ref)
    sweep(work_ref, other_ref, 1, 9, rhs_ref, corr_ref, mask)
    sweep(other_ref, work_ref, 2, 8, rhs_ref, None, mask)
    for layer in range(SZ):
        here = work_ref[DEPTH + layer]
        rows = [
            shifted(here, -STRIDE) - shifted(here, STRIDE),
            shifted(here, -1) - shifted(here, 1),
            work_ref[DEPTH + layer + 1] - work_ref[DEPTH + layer - 1],
            here,
        ]
        flat = compact(jnp.concatenate([row[:NB] for row in rows], axis=0))
        velocity_ref[:, layer, :] = (star_ref[layer] - 0.5 * flat)[: 3 * NB]
        p_ref[:, layer, :] = flat[3 * NB :]


def call(kernel, name, out_shapes, scratch, scalars):
    smem, vmem = pl.BlockSpec(memory_space=pltpu.SMEM), pl.BlockSpec(memory_space=pltpu.VMEM)
    shapes = tuple(jax.ShapeDtypeStruct(shape, F32) for shape in out_shapes)

    def run(*args):
        return pl.pallas_call(
            kernel,
            name=name,
            out_shape=shapes,
            in_specs=[smem if at < scalars else vmem for at in range(len(args))],
            out_specs=tuple(vmem for _ in shapes),
            scratch_shapes=scratch,
            compiler_params=pltpu.CompilerParams(vmem_limit_bytes=24 << 20),
        )(*args)

    return run


def trade(messages, count):
    whole = messages.reshape(count, -1, LANES)
    got = lax.all_to_all(whole, "chord", split_axis=0, concat_axis=0, tiled=True)
    return got.reshape(messages.shape)


def beside(up, down):
    size = lax.axis_size("span")
    low = lax.ppermute(up, "span", [(i, (i + 1) % size) for i in range(size)])
    high = lax.ppermute(down, "span", [(i, (i + size - 1) % size) for i in range(size)])
    return low, high


def local(
    velocity,
    pressure,
    viscosity,
    send_list,
    recv_slot,
    marker_block,
    marker_cells,
    marker_layer,
    marker_frac,
    marker_weights,
    marker_target,
    marker_count,
):
    count, strips = lax.axis_size("chord"), lax.axis_size("span")
    me = lax.axis_index("chord").astype(jnp.int32).reshape(1)
    at = lax.axis_index("span").astype(jnp.int32)
    send = send_list.T
    rim, spread = jnp.asarray(RIM), jnp.asarray(RIM.T)
    pack_flat, pack_ext = jnp.asarray(PACK_FLAT), jnp.asarray(PACK_EXT)
    spread_flat = jnp.asarray(SPREAD)
    place, mask, inside = jnp.asarray(PLACE), jnp.asarray(MASK), jnp.asarray(INSIDE)

    plane, flat = (SZ, 8, WIDTH), (SZ, 16, CELLS)
    tables = lambda fields: pltpu.VMEM((2 * fields * 16, 8, LANES), F32)
    strip_rows = lambda rows: pltpu.VMEM((SZ, rows, SEG), F32)
    layers = pltpu.VMEM((SZ + 2 * DEPTH, 8, WIDTH), F32)

    anywhere = pl.BlockSpec(memory_space=pl.ANY)
    messages = pl.pallas_call(
        first_pack,
        name="first_pack",
        out_shape=jax.ShapeDtypeStruct((2 * count, 8, LANES), F32),
        in_specs=[anywhere] * 5,
        out_specs=pl.BlockSpec(memory_space=pltpu.VMEM),
        scratch_shapes=[
            pltpu.SMEM((2, count), jnp.int32),
            pltpu.VMEM((3 * NB, SZ, CELLS), F32),
            pltpu.VMEM((NB, SZ, CELLS), F32),
            pltpu.VMEM((CELLS, LANES), BF16),
            pltpu.VMEM((CELLS, SEG), BF16),
            tables(2),
            pltpu.SemaphoreType.DMA((5,)),
        ],
        compiler_params=pltpu.CompilerParams(vmem_limit_bytes=60 << 20),
    )(send, velocity.reshape(3 * NB, SZ, CELLS), pressure, rim, pack_flat)
    got = trade(messages, count)
    me, _ = lax.optimization_barrier((me, messages))
    route = pl.pallas_call(
        routes,
        name="routes",
        out_shape=jax.ShapeDtypeStruct((ROUTES,), jnp.int32),
        in_specs=[pl.BlockSpec(memory_space=pltpu.SMEM)] * 3,
        out_specs=pl.BlockSpec(memory_space=pltpu.SMEM),
        scratch_shapes=[pltpu.SMEM((32,), jnp.int32)],
    )(me, send, recv_slot)
    later, eddy, route = lax.optimization_barrier((velocity, viscosity, route))
    cells = jnp.concatenate([later, eddy[None]], axis=0)
    cells = jnp.transpose(cells, (2, 0, 1, 3)).reshape(SZ, 16, CELLS)
    cells_low, cells_high = beside(cells, cells)

    group = marker_block.shape[0] // strips
    groups = jnp.stack([at, (at + strips - 1) % strips])
    weights, spans, aims = call(weigh, "weigh", [(CELLS, 2 * group), (16, 2 * group), (4, 2 * group)], [], 1)(
        groups, marker_block[None], marker_cells, marker_layer[None], marker_frac[None], marker_weights, marker_target
    )

    edge = (DEPTH, NB, WIDTH + 3 * LANES)
    own, corr, rims, up, down = call(
        first_unpack, "first_unpack", [plane, plane, (SZ, 16, LANES), edge, edge], [strip_rows(8), pltpu.VMEM(plane, F32)], 1
    )(route, got, pressure, place)
    low, high = beside(up, down)
    tilde, total = call(own_layers, "own_layers", [flat, (16, 2 * group)], [], 0)(
        cells, cells_low, cells_high, rims, spread, weights, spans
    )
    star, messages = call(
        forcing, "forcing", [flat, (2 * count, 8, LANES)],
        [pltpu.VMEM((6, 16, CELLS), F32), tables(2), strip_rows(16)], 2,
    )(
        send, marker_count, cells, cells_low, cells_high, tilde, total, low, high, spread,
        pack_flat, weights, spans, aims,
    )
    got = trade(messages, count)
    edge = (DEPTH, NB, WIDTH)
    flat_part, third, up, down = call(
        star_unpack, "star_unpack", [plane, plane, edge, edge], [strip_rows(8), strip_rows(8)], 1
    )(route, got, star, spread_flat, place, mask)
    star_low, star_high = beside(up, down)

    p, rhs, messages = call(
        first_sweeps, "first_sweeps", [plane, (SZ + 4, 8, WIDTH), (count, 8, LANES)],
        [layers, layers, tables(1), strip_rows(8)], 1,
    )(send, own, corr, low, high, flat_part, third, star_low, star_high, mask, pack_ext)
    for last in (False, True):
        got = trade(messages, count)
        own, corr, up, down = call(
            later_unpack, "later_unpack", [plane, plane, edge, edge], [strip_rows(8)], 1
        )(route, got, p, place, inside)
        low, high = beside(up, down)
        if not last:
            p, messages = call(
                later_sweeps, "later_sweeps", [plane, (count, 8, LANES)], [layers, layers, tables(1), strip_rows(8)], 1
            )(send, own, corr, low, high, rhs, mask, pack_ext)
    velocity_next, pressure_next = call(
        last_sweeps, "last_sweeps", [(3 * NB, SZ, CELLS), (NB, SZ, CELLS)], [layers, layers], 0
    )(own, corr, low, high, rhs, mask, star)
    return velocity_next.reshape(velocity.shape), pressure_next


RIM = rim_matrix()
PACK_FLAT = pack_matrix(CELLS, lambda i, k: EDGE * i + k)
PACK_EXT = pack_matrix(WIDTH, place_of)
PLACE = place_matrix()
SPREAD = spread_matrix()
MASK = sheet_mask()
INSIDE = block_mask()


def solution(mesh):
    in_specs = (
        P(None, "chord", "span", None),
        P("chord", "span", None),
        P("chord", "span", None),
        P("chord", None),
        P("chord", None),
        P("chord"),
        P(None, "chord"),
        P("chord"),
        P("chord"),
        P(None, "chord"),
        P(None, "chord"),
        P("chord"),
    )
    out_specs = (P(None, "chord", "span", None), P("chord", "span", None))
    return jax.shard_map(local, mesh=mesh, in_specs=in_specs, out_specs=out_specs, check_vma=False)
```

time: 220 us -> 190 us (0.86)
  waiting for transfers between devices: 32.4 us -> 16.9 us
  local copies, waits for them, and re-layouts: 8.08 us -> 0.95 us
  blocking collectives: 83.9 us -> 77.5 us
    ppermute x5, waiting for transfers between devices: 9.97 us -> 0.71 us  [beside(): low = lax.ppermute(up, 'span', [(i, (i + 1) % size) for i in range(size)])]
    all_to_all x3, blocking collectives: 83.9 us -> 77.5 us  [trade(): lax.all_to_all(whole, 'chord', split_axis=0, concat_axis=0, tiled=True)]
    pallas_call x0 -> x2, Pallas kernels: none -> 5.49 us  [the longest x1 3.01 us: local(): pl.pallas_call(first_pack, name='first_pack', out_shape=jax.ShapeDtypeStr...]
    all_to_all x1, waiting for transfers between devices: 17 us -> 11.6 us  [trade(): lax.all_to_all(whole, 'chord', split_axis=0, concat_axis=0, tiled=True)]
    ppermute x5, starting transfers between devices: 39.9 us -> 34.8 us  [beside(): lax.ppermute(down, 'span', [(i, (i + size - 1) % size) for i in range(siz...]
    pallas_call x9 -> x10, Pallas kernels: 23.3 us -> 19.1 us  [run(): pl.pallas_call(kernel, name=name, out_shape=shapes, in_specs=[smem if at...]
    dynamic_slice x6 -> x0, local copies, waits for them, and re-layouts: 3.77 us -> none  [two_groups(): lax.dynamic_slice_in_dim(values, g * group, group, axis=axis)]
    all_to_all x1, starting transfers between devices: 19 us -> 22.3 us  [trade(): lax.all_to_all(whole, 'chord', split_axis=0, concat_axis=0, tiled=True)]
  transfers between devices with their start and end apart: 11 -> 11, of which waited for: 9 -> 7; matrix products, arithmetic and copies ran while one was open for 3% -> 0% of each run, Pallas kernels for 2% -> 3%
where the time goes in v2:
time: 190 us
  blocking collectives  77.5 us (41%)
  starting transfers between devices  67.9 us (36%)
  Pallas kernels  24.6 us (13%)
  waiting for transfers between devices  16.9 us (9%)
    all_to_all x3, blocking collectives, trade(): lax.all_to_all(whole, 'chord', split_axis=0, concat_axis=0, tiled=True)  77.5 us
    ppermute x5, starting transfers between devices, beside(): lax.ppermute(down, 'span', [(i, (i + size - 1) % size) for i in range(siz...  34.8 us
    all_to_all x1, starting transfers between devices, trade(): lax.all_to_all(whole, 'chord', split_axis=0, concat_axis=0, tiled=True)  22.3 us
    pallas_call x10, Pallas kernels, run(): pl.pallas_call(kernel, name=name, out_shape=shapes, in_specs=[smem if at...  19.1 us
    all_to_all x1, waiting for transfers between devices, trade(): lax.all_to_all(whole, 'chord', split_axis=0, concat_axis=0, tiled=True)  11.6 us
    ppermute x5, starting transfers between devices, beside(): low = lax.ppermute(up, 'span', [(i, (i + 1) % size) for i in range(size)])  10.9 us
    ppermute x5, waiting for transfers between devices, beside(): lax.ppermute(down, 'span', [(i, (i + size - 1) % size) for i in range(siz...  4.63 us
  transfers between devices with their start and end apart: 11, of which 7 were waited for; matrix products, arithmetic and copies ran while one was open for 0% of the time, Pallas kernels for 3%

profile of v2, /device:TPU:1, one launch (start us, length us, event | category | flops | bytes accessed | tf_op | source)
XLA Modules:
  0.0 189.8 jit_solution(2739731414468540099)
XLA Ops:
  0.6 0.0 copy-start.17
  0.6 0.0 copy-start.18
  0.6 0.0 copy-start
  0.7 0.0 copy-start.6
  0.7 3.0 %first_pack.1 = f32[96,8,128]{2,1,0:T(8,128)} custom-call(s32[2,48]{1,0:T(2,128)} %bitcast.20, f32[12,4,1024]{2,1,0:T(4,128)} %bitcast.30, f32[4,4,1024]{2,1,0:T(4,128)} %p_ref.1, bf16[1024,128]{1,0:T(8,128)(2,1)} %constant.40.clone.rim_any, bf16[1024,512]{1,0:T(8,128)(2,1)} %constant.42.clone.pack_any.pack_ref), custom_call_target="tpu_custom_call" | custom-call | tf_op jit(solution)/shard_map/first_pack/pallas_call | solution.py:792
  3.7 22.3 %all-to-all-start = ((f32[48,16,128]{2,1,0:T(8,128)}), f32[48,16,128]{2,1,0:T(8,128)S(1)}, u32[]{:S(2)}, u32[]{:S(2)}) async-start(f32[48,16,128]{2,1,0:T(8,128)} %bitcast.28), calls=%async_computation | async-start | bytes 786432 | tf_op jit(solution)/shard_map/all_to_all | solution.py:752
  26.0 0.0 copy-start.8
  26.0 0.0 copy-start.9
  26.0 0.0 copy-start.12
  26.0 0.0 copy-start.14
  26.0 0.0 copy-start.15
  26.0 0.0 copy-start.16
  26.0 2.5 %routes.1.route_ref = s32[320]{0:T(512)} custom-call(s32[1]{0:T(128)} %bitcast.me_ref, s32[2,48]{1,0:T(2,128)} %bitcast.21, s32[4,4]{1,0:T(4,128)} %recv_ref.1), custom_call_target="tpu_custom_call" | custom-call | tf_op jit(solution)/shard_map/routes/pallas_call | solution.py:811
  28.5 0.0 copy-done.17
  28.5 0.1 pad_maximum_fusion
  28.6 0.0 copy-start.4
  28.6 0.2 copy.23.own_ref
  28.8 4.7 %collective-permute-start.3 = (f32[4,16,1024]{2,1,0:T(8,128)S(1)}, f32[4,16,1024]{2,1,0:T(8,128)S(1)}, u32[]{:S(2)}, u32[]{:S(2)}) collective-permute-start(f32[4,16,1024]{2,1,0:T(8,128)S(1)} %copy.23.own_ref), channel_id=1, source_target_pairs={{0,15},{1,0},{2,1},{3,2},{4,3},{5,4},{6,5},{7,6},{8,7},{9,8},{10,9... | collective-permute-start | bytes 786440 | tf_op jit(solution)/shard_map/ppermute | solution.py:759
  33.5 1.9 %collective-permute-start.2 = (f32[4,16,1024]{2,1,0:T(8,128)S(1)}, f32[4,16,1024]{2,1,0:T(8,128)S(1)}, u32[]{:S(2)}, u32[]{:S(2)}) collective-permute-start(f32[4,16,1024]{2,1,0:T(8,128)S(1)} %copy.23.own_ref), channel_id=1, source_target_pairs={{0,1},{1,2},{2,3},{3,4},{4,5},{5,6},{6,7},{7,8},{8,9},{9,10},{10,1... | collective-permute-start | bytes 786440 | tf_op jit(solution)/shard_map/ppermute | solution.py:758
  36.1 11.6 %all-to-all-done = f32[48,16,128]{2,1,0:T(8,128)S(1)} async-done(((f32[48,16,128]{2,1,0:T(8,128)}), f32[48,16,128]{2,1,0:T(8,128)S(1)}, u32[]{:S(2)}, u32[]{:S(2)}) %all-to-all-start) | async-done | bytes 393248 | tf_op jit(solution)/shard_map/all_to_all | solution.py:752
  47.7 0.0 copy-done
  47.7 0.7 copy-done.10
  48.4 1.3 first_unpack.1
  49.8 0.0 copy-start.2
  49.8 0.0 copy-start.13
  49.8 3.2 %collective-permute-start = (f32[3,4,1920]{2,1,0:T(4,128)S(1)}, f32[3,4,1920]{2,1,0:T(4,128)S(1)}, u32[]{:S(2)}, u32[]{:S(2)}) collective-permute-start(f32[3,4,1920]{2,1,0:T(4,128)S(1)} %get-tuple-element.41), channel_id=1, source_target_pairs={{0,1},{1,2},{2,3},{3,4},{4,5},{5,6},{6,7},{7,8},{8,9},{9,10},{10,1... | collective-permute-start | bytes 276488 | tf_op jit(solution)/shard_map/ppermute | solution.py:758
  53.0 6.1 %collective-permute-start.1 = (f32[3,4,1920]{2,1,0:T(4,128)S(1)}, f32[3,4,1920]{2,1,0:T(4,128)S(1)}, u32[]{:S(2)}, u32[]{:S(2)}) collective-permute-start(f32[3,4,1920]{2,1,0:T(4,128)S(1)} %get-tuple-element.42), channel_id=1, source_target_pairs={{0,15},{1,0},{2,1},{3,2},{4,3},{5,4},{6,5},{7,6},{8,7},{9,8},{10,9... | collective-permute-start | bytes 276488 | tf_op jit(solution)/shard_map/ppermute | solution.py:759
  59.1 0.1 pad_add_fusion.at_ref
  59.2 0.0 copy-done.9
  59.2 0.0 copy-done.14
  59.3 0.9 weigh.1
  60.2 0.0 collective-permute-done.3.high_ref
  60.2 0.0 collective-permute-done.2.low_ref
  60.2 0.0 copy-done.4
  60.2 1.0 own_layers.1
  61.2 0.0 collective-permute-done.rim_low_ref.low_ref
  61.3 0.0 collective-permute-done.1.rim_high_ref.high_ref
  61.3 0.0 copy-start.3
  61.3 0.0 copy-start.5
  61.3 4.2 %forcing.1 = (f32[4,16,1024]{2,1,0:T(8,128)S(1)}, f32[96,8,128]{2,1,0:T(8,128)S(1)}) custom-call(s32[2,48]{1,0:T(2,128)S(1)} %bitcast.22, s32[1]{0:T(128)S(6)} %copy.24.count_ref, f32[4,16,1024]{2,1,0:T(8,128)S(1)} %copy.23.own_ref, f32[4,16,1024]{2,1,0:T(8,128)S(1)} %collective-permute-done.2.low_ref, f32[4,16,1024]{2,1,0:T(8,128)S(1)} %collective-permute-done.3.high_ref, ...), custom_call_target="tpu_custom_call" | custom-call | tf_op jit(solution)/shard_map/forcing/pallas_call | solution.py:737
  65.5 29.4 %all_to_all.20 = f32[48,16,128]{2,1,0:T(8,128)S(1)} all-to-all(f32[48,16,128]{2,1,0:T(8,128)S(1)} %bitcast.19), channel_id=1, replica_groups=mesh['chord'=48,'span'=16] {'chord'}, dimensions={0} | all-to-all | bytes 786432 | tf_op jit(solution)/shard_map/all_to_all | solution.py:752
  94.9 2.0 %star_unpack.1 = (f32[4,8,1536]{2,1,0:T(8,128)S(1)}, f32[4,8,1536]{2,1,0:T(8,128)S(1)}, f32[3,4,1536]{2,1,0:T(4,128)S(1)}, f32[3,4,1536]{2,1,0:T(4,128)S(1)}) custom-call(s32[320]{0:T(512)S(1)} %copy-done.10, f32[96,8,128]{2,1,0:T(8,128)S(1)} %bitcast.18, f32[4,16,1024]{2,1,0:T(8,128)S(1)} %get-tuple-element.52.star_ref, bf16[512,1536]{1,0:T(8,128)(2,1)S(1)} %copy-done.3, ...), custom_call_target="tpu_custom_call" | custom-call | tf_op jit(solution)/shard_map/star_unpack/pallas_call | solution.py:737
  97.0 1.9 %collective-permute-start.4 = (f32[3,4,1536]{2,1,0:T(4,128)S(1)}, f32[3,4,1536]{2,1,0:T(4,128)S(1)}, u32[]{:S(2)}, u32[]{:S(2)}) collective-permute-start(f32[3,4,1536]{2,1,0:T(4,128)S(1)} %get-tuple-element.55), channel_id=1, source_target_pairs={{0,1},{1,2},{2,3},{3,4},{4,5},{5,6},{6,7},{7,8},{8,9},{9,10},{10,1... | collective-permute-start | bytes 221192 | tf_op jit(solution)/shard_map/ppermute | solution.py:758
  98.9 0.0 copy-start.7
  98.9 0.0 copy-start.11
  98.9 8.0 %collective-permute-start.5 = (f32[3,4,1536]{2,1,0:T(4,128)S(1)}, f32[3,4,1536]{2,1,0:T(4,128)S(1)}, u32[]{:S(2)}, u32[]{:S(2)}) collective-permute-start(f32[3,4,1536]{2,1,0:T(4,128)S(1)} %get-tuple-element.56), channel_id=1, source_target_pairs={{0,15},{1,0},{2,1},{3,2},{4,3},{5,4},{6,5},{7,6},{8,7},{9,8},{10,9... | collective-permute-start | bytes 221192 | tf_op jit(solution)/shard_map/ppermute | solution.py:759
  107.0 0.4 collective-permute-done.4.star_low_ref
  107.4 1.0 collective-permute-done.5.star_high_ref
  108.4 2.3 %first_sweeps.1 = (f32[4,8,1536]{2,1,0:T(8,128)S(1)}, f32[8,8,1536]{2,1,0:T(8,128)S(1)}, f32[48,8,128]{2,1,0:T(8,128)S(1)}) custom-call(s32[2,48]{1,0:T(2,128)S(1)} %bitcast.23, f32[4,8,1536]{2,1,0:T(8,128)S(1)} %get-tuple-element.39.own_ref, f32[4,8,1536]{2,1,0:T(8,128)S(1)} %get-tuple-element.40.corr_ref, ...), custom_call_target="tpu_custom_call" | custom-call | tf_op jit(solution)/shard_map/first_sweeps/pallas_call | solution.py:737
  110.7 25.0 %all_to_all.21.got_ref = f32[48,8,128]{2,1,0:T(8,128)S(1)} all-to-all(f32[48,8,128]{2,1,0:T(8,128)S(1)} %get-tuple-element.57), channel_id=1, replica_groups=mesh['chord'=48,'span'=16] {'chord'}, dimensions={0} | all-to-all | bytes 393216 | tf_op jit(solution)/shard_map/all_to_all | solution.py:752
  135.7 0.0 copy-done.7
  135.7 1.3 later_unpack.2
  137.0 1.9 %collective-permute-start.6 = (f32[3,4,1536]{2,1,0:T(4,128)S(1)}, f32[3,4,1536]{2,1,0:T(4,128)S(1)}, u32[]{:S(2)}, u32[]{:S(2)}) collective-permute-start(f32[3,4,1536]{2,1,0:T(4,128)S(1)} %get-tuple-element.61), channel_id=1, source_target_pairs={{0,1},{1,2},{2,3},{3,4},{4,5},{5,6},{6,7},{7,8},{8,9},{9,10},{10,1... | collective-permute-start | bytes 221192 | tf_op jit(solution)/shard_map/ppermute | solution.py:758
  139.0 8.0 %collective-permute-start.7 = (f32[3,4,1536]{2,1,0:T(4,128)S(1)}, f32[3,4,1536]{2,1,0:T(4,128)S(1)}, u32[]{:S(2)}, u32[]{:S(2)}) collective-permute-start(f32[3,4,1536]{2,1,0:T(4,128)S(1)} %get-tuple-element.62), channel_id=1, source_target_pairs={{0,15},{1,0},{2,1},{3,2},{4,3},{5,4},{6,5},{7,6},{8,7},{9,8},{10,9... | collective-permute-start | bytes 221192 | tf_op jit(solution)/shard_map/ppermute | solution.py:759
  146.9 0.2 collective-permute-done.6.low_ref
  147.1 1.8 collective-permute-done.7.high_ref
  148.9 2.3 %later_sweeps.1 = (f32[4,8,1536]{2,1,0:T(8,128)S(1)}, f32[48,8,128]{2,1,0:T(8,128)S(1)}) custom-call(s32[2,48]{1,0:T(2,128)S(1)} %bitcast.24, f32[4,8,1536]{2,1,0:T(8,128)S(1)} %get-tuple-element.59.own_ref, f32[4,8,1536]{2,1,0:T(8,128)S(1)} %get-tuple-element.60.corr_ref, f32[3,4,1536]{2,1,0:T(4,128)S(1)} %collective-permute-done.6.low_ref, ...), custom_call_target="tpu_custom_call" | custom-call | tf_op jit(solution)/shard_map/later_sweeps/pallas_call | solution.py:737
  151.2 23.1 %all_to_all.22.got_ref = f32[48,8,128]{2,1,0:T(8,128)S(1)} all-to-all(f32[48,8,128]{2,1,0:T(8,128)S(1)} %get-tuple-element.64), channel_id=1, replica_groups=mesh['chord'=48,'span'=16] {'chord'}, dimensions={0} | all-to-all | bytes 393216 | tf_op jit(solution)/shard_map/all_to_all | solution.py:752
  174.2 1.3 later_unpack.3
  175.6 1.9 %collective-permute-start.8 = (f32[3,4,1536]{2,1,0:T(4,128)S(1)}, f32[3,4,1536]{2,1,0:T(4,128)S(1)}, u32[]{:S(2)}, u32[]{:S(2)}) collective-permute-start(f32[3,4,1536]{2,1,0:T(4,128)S(1)} %get-tuple-element.68), channel_id=1, source_target_pairs={{0,1},{1,2},{2,3},{3,4},{4,5},{5,6},{6,7},{7,8},{8,9},{9,10},{10,1... | collective-permute-start | bytes 221192 | tf_op jit(solution)/shard_map/ppermute | solution.py:758
  177.5 7.9 %collective-permute-start.9 = (f32[3,4,1536]{2,1,0:T(4,128)S(1)}, f32[3,4,1536]{2,1,0:T(4,128)S(1)}, u32[]{:S(2)}, u32[]{:S(2)}) collective-permute-start(f32[3,4,1536]{2,1,0:T(4,128)S(1)} %get-tuple-element.69), channel_id=1, source_target_pairs={{0,15},{1,0},{2,1},{3,2},{4,3},{5,4},{6,5},{7,6},{8,7},{9,8},{10,9... | collective-permute-start | bytes 221192 | tf_op jit(solution)/shard_map/ppermute | solution.py:759
  185.4 0.2 collective-permute-done.8.low_ref
  185.6 1.8 collective-permute-done.9.high_ref
  187.4 2.3 %last_sweeps.1 = (f32[12,4,1024]{2,1,0:T(4,128)}, f32[4,4,1024]{2,1,0:T(4,128)}) custom-call(f32[4,8,1536]{2,1,0:T(8,128)S(1)} %get-tuple-element.66.own_ref, f32[4,8,1536]{2,1,0:T(8,128)S(1)} %get-tuple-element.67.corr_ref, f32[3,4,1536]{2,1,0:T(4,128)S(1)} %collective-permute-done.8.low_ref, f32[3,4,1536]{2,1,0:T(4,128)S(1)} %collective-permute-done.9.high_ref, ...), custom_call_target="tpu_custom_call" | custom-call | tf_op jit(solution)/shard_map/last_sweeps/pallas_call | solution.py:737
  (14 shorter events, 0.0 us)
Async XLA Ops:
  0.6 27.9 %copy-start.17 = (f32[3,4,4,1024]{3,2,1,0:T(4,128)S(1)}, f32[3,4,4,1024]{3,2,1,0:T(4,128)}, u32[]{:S(2)}) copy-start(f32[3,4,4,1024]{3,2,1,0:T(4,128)} %param.20) | copy-start | bytes 589828
  0.6 27.9 %copy-start.18 = (f32[4,4,1024]{2,1,0:T(4,128)S(1)}, f32[4,4,1024]{2,1,0:T(4,128)}, u32[]{:S(2)}) copy-start(f32[4,4,1024]{2,1,0:T(4,128)} %param.22) | copy-start | bytes 196612
  0.6 47.1 %copy-start = (bf16[512,1536]{1,0:T(8,128)(2,1)S(1)}, bf16[512,1536]{1,0:T(8,128)(2,1)}, u32[]{:S(2)}) copy-start(bf16[512,1536]{1,0:T(8,128)(2,1)} %constant.45.clone.place_ref) | copy-start | bytes 4718596
  0.7 47.1 %copy-start.6 = (f32[4,4,1024]{2,1,0:T(4,128)S(1)}, f32[4,4,1024]{2,1,0:T(4,128)}, u32[]{:S(2)}) copy-start(f32[4,4,1024]{2,1,0:T(4,128)} %p_ref.1) | copy-start | bytes 196612
  3.7 44.0 %all-to-all-start = ((f32[48,16,128]{2,1,0:T(8,128)}), f32[48,16,128]{2,1,0:T(8,128)S(1)}, u32[]{:S(2)}, u32[]{:S(2)}) async-start(f32[48,16,128]{2,1,0:T(8,128)} %bitcast.28), calls=%async_computation | async-start | bytes 786432 | tf_op jit(solution)/shard_map/all_to_all | solution.py:752
  26.0 33.3 %copy-start.8 = (s32[16,2048]{1,0:T(8,128)S(1)}, s32[16,2048]{1,0:T(8,128)}, u32[]{:S(2)}) copy-start(s32[16,2048]{1,0:T(8,128)} %cells_ref.1) | copy-start | bytes 393220
  26.0 33.2 %copy-start.9 = (f32[16,2048]{1,0:T(8,128)S(1)}, f32[16,2048]{1,0:T(8,128)}, u32[]{:S(2)}) copy-start(f32[16,2048]{1,0:T(8,128)} %weight_ref.1) | copy-start | bytes 393220
  26.0 33.2 %copy-start.12 = (f32[3,2048]{1,0:T(4,128)S(1)}, f32[3,2048]{1,0:T(4,128)}, u32[]{:S(2)}) copy-start(f32[3,2048]{1,0:T(4,128)} %target_ref.1) | copy-start | bytes 73732
  26.0 33.2 %copy-start.14 = (s32[2048]{0:T(1024)S(1)}, s32[2048]{0:T(1024)}, u32[]{:S(2)}) copy-start(s32[2048]{0:T(1024)} %param.25) | copy-start | bytes 24580
  26.0 33.2 %copy-start.15 = (s32[2048]{0:T(1024)S(1)}, s32[2048]{0:T(1024)}, u32[]{:S(2)}) copy-start(s32[2048]{0:T(1024)} %param.27) | copy-start | bytes 24580
  26.0 33.2 %copy-start.16 = (f32[2048]{0:T(1024)S(1)}, f32[2048]{0:T(1024)}, u32[]{:S(2)}) copy-start(f32[2048]{0:T(1024)} %param.28) | copy-start | bytes 24580
  28.6 31.6 %copy-start.4 = (bf16[128,1024]{1,0:T(8,128)(2,1)S(1)}, bf16[128,1024]{1,0:T(8,128)(2,1)}, u32[]{:S(2)}) copy-start(bf16[128,1024]{1,0:T(8,128)(2,1)} %constant.41.clone.spread_ref) | copy-start | bytes 786436
  28.8 31.4 %collective-permute-start.3 = (f32[4,16,1024]{2,1,0:T(8,128)S(1)}, f32[4,16,1024]{2,1,0:T(8,128)S(1)}, u32[]{:S(2)}, u32[]{:S(2)}) collective-permute-start(f32[4,16,1024]{2,1,0:T(8,128)S(1)} %copy.23.own_ref), channel_id=1, source_target_pairs={{0,15},{1,0},{2,1},{3,2},{4,3},{5,4},{6,5},{7,6},{8,7},{9,8},{10,9... | collective-permute-start | bytes 786440 | tf_op jit(solution)/shard_map/ppermute | solution.py:759
  33.5 26.6 %collective-permute-start.2 = (f32[4,16,1024]{2,1,0:T(8,128)S(1)}, f32[4,16,1024]{2,1,0:T(8,128)S(1)}, u32[]{:S(2)}, u32[]{:S(2)}) collective-permute-start(f32[4,16,1024]{2,1,0:T(8,128)S(1)} %copy.23.own_ref), channel_id=1, source_target_pairs={{0,1},{1,2},{2,3},{3,4},{4,5},{5,6},{6,7},{7,8},{8,9},{9,10},{10,1... | collective-permute-start | bytes 786440 | tf_op jit(solution)/shard_map/ppermute | solution.py:758
  47.7 0.7 copy-start.10
  49.8 11.5 %copy-start.2 = (bf16[1024,512]{1,0:T(8,128)(2,1)S(1)}, bf16[1024,512]{1,0:T(8,128)(2,1)}, u32[]{:S(2)}) copy-start(bf16[1024,512]{1,0:T(8,128)(2,1)} %constant.42.clone.pack_any.pack_ref) | copy-start | bytes 3145732
  49.8 11.5 %copy-start.13 = (s32[48,2]{0,1:T(2,128)S(1)}, s32[48,2]{0,1:T(2,128)}, u32[]{:S(2)}) copy-start(s32[48,2]{0,1:T(2,128)} %param.23) | copy-start | bytes 1156
  49.8 11.4 %collective-permute-start = (f32[3,4,1920]{2,1,0:T(4,128)S(1)}, f32[3,4,1920]{2,1,0:T(4,128)S(1)}, u32[]{:S(2)}, u32[]{:S(2)}) collective-permute-start(f32[3,4,1920]{2,1,0:T(4,128)S(1)} %get-tuple-element.41), channel_id=1, source_target_pairs={{0,1},{1,2},{2,3},{3,4},{4,5},{5,6},{6,7},{7,8},{8,9},{9,10},{10,1... | collective-permute-start | bytes 276488 | tf_op jit(solution)/shard_map/ppermute | solution.py:758
  53.0 8.3 %collective-permute-start.1 = (f32[3,4,1920]{2,1,0:T(4,128)S(1)}, f32[3,4,1920]{2,1,0:T(4,128)S(1)}, u32[]{:S(2)}, u32[]{:S(2)}) collective-permute-start(f32[3,4,1920]{2,1,0:T(4,128)S(1)} %get-tuple-element.42), channel_id=1, source_target_pairs={{0,15},{1,0},{2,1},{3,2},{4,3},{5,4},{6,5},{7,6},{8,7},{9,8},{10,9... | collective-permute-start | bytes 276488 | tf_op jit(solution)/shard_map/ppermute | solution.py:759
  61.3 33.6 %copy-start.3 = (bf16[512,1536]{1,0:T(8,128)(2,1)S(1)}, bf16[512,1536]{1,0:T(8,128)(2,1)}, u32[]{:S(2)}) copy-start(bf16[512,1536]{1,0:T(8,128)(2,1)} %constant.44.clone.spread_ref) | copy-start | bytes 4718596
  61.3 33.6 %copy-start.5 = (f32[8,1536]{1,0:T(8,128)S(1)}, f32[8,1536]{1,0:T(8,128)}, u32[]{:S(2)}) copy-start(f32[8,1536]{1,0:T(8,128)} %constant.46.clone.mask_ref) | copy-start | bytes 147460
  94.9 13.4 %copy-start.1 = (bf16[1536,512]{1,0:T(8,128)(2,1)S(1)}, bf16[1536,512]{1,0:T(8,128)(2,1)}, u32[]{:S(2)}) copy-start(bf16[1536,512]{1,0:T(8,128)(2,1)} %constant.43.clone.pack_ref) | copy-start | bytes 4718596
  97.0 10.4 %collective-permute-start.4 = (f32[3,4,1536]{2,1,0:T(4,128)S(1)}, f32[3,4,1536]{2,1,0:T(4,128)S(1)}, u32[]{:S(2)}, u32[]{:S(2)}) collective-permute-start(f32[3,4,1536]{2,1,0:T(4,128)S(1)} %get-tuple-element.55), channel_id=1, source_target_pairs={{0,1},{1,2},{2,3},{3,4},{4,5},{5,6},{6,7},{7,8},{8,9},{9,10},{10,1... | collective-permute-start | bytes 221192 | tf_op jit(solution)/shard_map/ppermute | solution.py:758
  98.9 36.8 %copy-start.7 = (f32[8,1536]{1,0:T(8,128)S(1)}, f32[8,1536]{1,0:T(8,128)}, u32[]{:S(2)}) copy-start(f32[8,1536]{1,0:T(8,128)} %constant.47.clone.block_ref) | copy-start | bytes 147460
  98.9 36.8 %copy-start.11 = (s32[320]{0:T(512)S(1)}, s32[320]{0:T(512)}, u32[]{:S(2)}) copy-start(s32[320]{0:T(512)} %routes.1.route_ref) | copy-start | bytes 3844
  98.9 9.4 %collective-permute-start.5 = (f32[3,4,1536]{2,1,0:T(4,128)S(1)}, f32[3,4,1536]{2,1,0:T(4,128)S(1)}, u32[]{:S(2)}, u32[]{:S(2)}) collective-permute-start(f32[3,4,1536]{2,1,0:T(4,128)S(1)} %get-tuple-element.56), channel_id=1, source_target_pairs={{0,15},{1,0},{2,1},{3,2},{4,3},{5,4},{6,5},{7,6},{8,7},{9,8},{10,9... | collective-permute-start | bytes 221192 | tf_op jit(solution)/shard_map/ppermute | solution.py:759
  137.0 10.1 %collective-permute-start.6 = (f32[3,4,1536]{2,1,0:T(4,128)S(1)}, f32[3,4,1536]{2,1,0:T(4,128)S(1)}, u32[]{:S(2)}, u32[]{:S(2)}) collective-permute-start(f32[3,4,1536]{2,1,0:T(4,128)S(1)} %get-tuple-element.61), channel_id=1, source_target_pairs={{0,1},{1,2},{2,3},{3,4},{4,5},{5,6},{6,7},{7,8},{8,9},{9,10},{10,1... | collective-permute-start | bytes 221192 | tf_op jit(solution)/shard_map/ppermute | solution.py:758
  139.0 9.9 %collective-permute-start.7 = (f32[3,4,1536]{2,1,0:T(4,128)S(1)}, f32[3,4,1536]{2,1,0:T(4,128)S(1)}, u32[]{:S(2)}, u32[]{:S(2)}) collective-permute-start(f32[3,4,1536]{2,1,0:T(4,128)S(1)} %get-tuple-element.62), channel_id=1, source_target_pairs={{0,15},{1,0},{2,1},{3,2},{4,3},{5,4},{6,5},{7,6},{8,7},{9,8},{10,9... | collective-permute-start | bytes 221192 | tf_op jit(solution)/shard_map/ppermute | solution.py:759
  175.6 10.0 %collective-permute-start.8 = (f32[3,4,1536]{2,1,0:T(4,128)S(1)}, f32[3,4,1536]{2,1,0:T(4,128)S(1)}, u32[]{:S(2)}, u32[]{:S(2)}) collective-permute-start(f32[3,4,1536]{2,1,0:T(4,128)S(1)} %get-tuple-element.68), channel_id=1, source_target_pairs={{0,1},{1,2},{2,3},{3,4},{4,5},{5,6},{6,7},{7,8},{8,9},{9,10},{10,1... | collective-permute-start | bytes 221192 | tf_op jit(solution)/shard_map/ppermute | solution.py:758
  177.5 9.9 %collective-permute-start.9 = (f32[3,4,1536]{2,1,0:T(4,128)S(1)}, f32[3,4,1536]{2,1,0:T(4,128)S(1)}, u32[]{:S(2)}, u32[]{:S(2)}) collective-permute-start(f32[3,4,1536]{2,1,0:T(4,128)S(1)} %get-tuple-element.69), channel_id=1, source_target_pairs={{0,15},{1,0},{2,1},{3,2},{4,3},{5,4},{6,5},{7,6},{8,7},{9,8},{10,9... | collective-permute-start | bytes 221192 | tf_op jit(solution)/shard_map/ppermute | solution.py:759

commit v3 on v2

v3 whole, which is shorter than its diff:
```python
import math

import jax
import jax.numpy as jnp
import ml_dtypes
import numpy as np
from jax import lax
from jax.experimental import pallas as pl
from jax.experimental.pallas import tpu as pltpu
from jax.sharding import PartitionSpec as P

EDGE = 32
CELLS = EDGE * EDGE
NB = 4
SZ = 4
REACH = 3
DEPTH = 4
STRIDE = 40
WIDTH = 1664
LANES = 128
SEG = 4 * LANES
PATCH = ((0, 0), (0, 1), (1, 0), (0, 2), (1, 1), (2, 0))
F32 = jnp.float32
BF16 = jnp.bfloat16


def place_of(i, k):
    return STRIDE * (i + DEPTH) + k + 4


def edge_cell(side, depth, x):
    return [(depth, x), (EDGE - 1 - depth, x), (x, depth), (x, EDGE - 1 - depth)][side]


def ghost_cell(side, depth, x):
    return [(-1 - depth, x), (EDGE + depth, x), (x, -1 - depth), (x, EDGE + depth)][side]


def corner_cell(corner, i, k):
    return i if corner // 2 == 0 else EDGE - 1 - i, k if corner % 2 == 0 else EDGE - 1 - k


def vertex_cell(vertex, i=0, k=0):
    return -1 - i if vertex // 2 == 0 else EDGE + i, -1 - k if vertex % 2 == 0 else EDGE + k


def pack_matrix(rows, where):
    table = np.zeros((rows, SEG + LANES), np.float32)
    for side in range(4):
        for depth in range(DEPTH):
            for x in range(EDGE):
                table[where(*edge_cell(side, depth, x)), side * LANES + depth * EDGE + x] = 1
    for corner in range(4):
        for at, cell in enumerate(PATCH):
            table[where(*corner_cell(corner, *cell)), SEG + corner * 8 + at] = 1
    return table.astype(ml_dtypes.bfloat16)


def pack_rhs_matrix():
    table = np.zeros((CELLS, SEG), np.float32)
    for side in range(4):
        for depth in range(DEPTH - 1):
            for x in range(EDGE):
                i, k = edge_cell(side, depth, x)
                table[EDGE * i + k, side * LANES + depth * EDGE + x] = 1
        for corner in range(4):
            for at in range(4):
                i, k = corner_cell(corner, at // 2, at % 2)
                table[EDGE * i + k, side * LANES + 96 + corner * 4 + at] = 1
    return table.astype(ml_dtypes.bfloat16)


def place_matrix():
    table = np.zeros((SEG + LANES, WIDTH), np.float32)
    for side in range(4):
        for depth in range(DEPTH):
            for x in range(EDGE):
                table[side * LANES + depth * EDGE + x, place_of(*ghost_cell(side, depth, x))] = 1
    for vertex in range(4):
        for at, cell in enumerate(PATCH):
            table[SEG + vertex * 16 + at, place_of(*vertex_cell(vertex, *cell))] = 1
    return table.astype(ml_dtypes.bfloat16)


def place_rhs_matrix():
    table = np.zeros((SEG, WIDTH), np.float32)
    for side in range(4):
        for depth in range(DEPTH - 1):
            for x in range(EDGE):
                table[side * LANES + depth * EDGE + x, place_of(*ghost_cell(side, depth, x))] = 1
    for vertex in range(4):
        for at in range(3):
            table[vertex * LANES + 96 + at, place_of(*vertex_cell(vertex, at // 2, at % 2))] = 1
    return table.astype(ml_dtypes.bfloat16)


def across_matrix():
    table = np.zeros((LANES, CELLS), np.float32)
    for side in range(4):
        for x in range(EDGE):
            i, k = edge_cell(side, 0, x)
            table[side * EDGE + x, i * EDGE + k] = 0.5 if side % 2 else -0.5
    return table.astype(ml_dtypes.bfloat16)


def fan_codes():
    codes = np.zeros((8, WIDTH), np.float32)
    for vertex in range(4):
        to_i, to_k = 1 + (1 - vertex // 2), 3 + (1 - vertex % 2)
        codes[:NB, place_of(*vertex_cell(vertex))] = to_i
        codes[:NB, place_of(*vertex_cell(vertex, 0, 1))] = to_i + 4
        codes[NB:, place_of(*vertex_cell(vertex))] = to_k
        codes[NB:, place_of(*vertex_cell(vertex, 1, 0))] = to_k + 4
    return codes


def rim_matrix():
    table = np.zeros((CELLS, LANES), np.float32)
    for side in range(4):
        for x in range(EDGE):
            i, k = edge_cell(side, 0, x)
            table[i * EDGE + k, side * EDGE + x] = 1
    return table.astype(ml_dtypes.bfloat16)


def sheet_mask():
    mask = np.zeros((8, WIDTH), np.float32)
    for i in range(-DEPTH, EDGE + DEPTH):
        for k in range(-DEPTH, EDGE + DEPTH):
            inside_i, inside_k = 0 <= i < EDGE, 0 <= k < EDGE
            if inside_i and not inside_k:
                mask[:4, place_of(i, k)] = 1
            if inside_k and not inside_i:
                mask[4:, place_of(i, k)] = 1
    return mask


def block_mask():
    mask = np.zeros((8, WIDTH), np.float32)
    for i in range(EDGE):
        mask[:, place_of(i, 0) : place_of(i, 0) + EDGE] = 1
    return mask


def vertex_place(vertex):
    return place_of(*vertex_cell(vertex))


def pick(x, table):
    high = x.astype(BF16)
    rest = x - high.astype(F32)
    middle = rest.astype(BF16)
    low = (rest - middle.astype(F32)).astype(BF16)
    parts = jnp.dot(jnp.concatenate([high, middle, low], axis=0), table, preferred_element_type=F32)
    rows = x.shape[0]
    return (parts[:rows] + parts[rows : 2 * rows]) + parts[2 * rows :]


def shifted(x, lanes):
    return pltpu.roll(x, lanes % x.shape[1], axis=1)


def lane_ids(rows):
    return lax.broadcasted_iota(jnp.int32, (rows, LANES), 1)


def remap(x, width, pieces):
    rows = x.shape[0]
    lane = lane_ids(rows)
    out = []
    for tile in range(width // LANES):
        acc = jnp.zeros((rows, LANES), F32)
        base = tile * LANES
        for src, dst in pieces:
            first, last = max(dst, base), min(dst + EDGE, base + LANES)
            while first < last:
                at = src + first - dst
                column = at // LANES
                stop = min(last, first + (column + 1) * LANES - at)
                value = x[:, column * LANES : (column + 1) * LANES]
                turn = (first - base - at % LANES) % LANES
                if turn:
                    value = pltpu.roll(value, turn, axis=1)
                acc = jnp.where((lane >= first - base) & (lane < stop - base), value, acc)
                first = stop
        out.append(acc)
    return jnp.concatenate(out, axis=1)


def expand(x):
    return remap(x, WIDTH, [(EDGE * i, place_of(i, 0)) for i in range(EDGE)])


def compact(x):
    return remap(x, CELLS, [(place_of(i, 0), EDGE * i) for i in range(EDGE)])


def post(send_ref, out_ref, count, parts):
    units = len(parts)

    def one(target, carry):
        edges = [jnp.maximum(send_ref[slot, target], 0) for slot in range(2)]
        for unit, (table, slot, offset) in enumerate(parts):
            out_ref[target * units + unit] = table[offset if slot is None else offset + edges[slot]]
        return carry

    lax.fori_loop(0, count, one, 0, unroll=4)


def store_strips(strips, table_ref, corner_ref):
    lane = lane_ids(SZ)
    corners = jnp.zeros((SZ, LANES), F32)
    for block in range(NB):
        rows = strips[block * SZ : (block + 1) * SZ]
        for side in range(4):
            table_ref[block * 4 + side] = rows[:, side * LANES : (side + 1) * LANES]
        patch = rows[:, SEG:]
        patch = pltpu.roll(patch, EDGE * block, axis=1) if block else patch
        corners = jnp.where(lane // EDGE == block, patch, corners)
    corner_ref[0] = corners


def store_rhs_strips(strips, table_ref):
    lane = lane_ids(SZ)
    for side in range(4):
        parts = [strips[block * SZ : (block + 1) * SZ, side * LANES : (side + 1) * LANES] for block in range(NB)]
        for slot in range(2):
            patch = jnp.where(lane < 112, parts[2 * slot], pltpu.roll(parts[2 * slot + 1], 16, axis=1))
            for block in range(NB):
                table_ref[slot * 16 + block * 4 + side] = jnp.where(lane < 96, parts[block], patch)


def first_pack(
    send_any, velocity_any, p_any, rim_any, out_ref, send_ref, velocity_ref, p_ref, rim_ref, table_ref, done_ref
):
    pairs = ((velocity_any, velocity_ref), (rim_any, rim_ref), (p_any, p_ref), (send_any, send_ref))
    copies = [pltpu.make_async_copy(*pair, done_ref.at[at]) for at, pair in enumerate(pairs)]
    for copy in copies:
        copy.start()
    lane = lane_ids(SZ)
    for copy in copies:
        copy.wait()
    rows = [velocity_ref[...].reshape(3 * NB * SZ, CELLS), p_ref[...].reshape(NB * SZ, CELLS)]
    rims = pick(jnp.concatenate(rows, axis=0), rim_ref[...])
    for block in range(NB):
        for side in range(4):
            value = jnp.zeros((SZ, LANES), F32)
            for comp in range(4):
                first = (comp * NB + block) * SZ
                part = rims[first : first + SZ]
                turn = EDGE * (comp - side) % LANES
                if turn:
                    part = pltpu.roll(part, turn, axis=1)
                value = jnp.where(lane // EDGE == comp, part, value)
            table_ref[block * 4 + side] = value
    post(send_ref, out_ref, out_ref.shape[0] // 2, [(table_ref, 0, 0), (table_ref, 1, 0)])


def routes(me_ref, send_ref, recv_ref, out_ref, near_ref):
    me, count = me_ref[0], send_ref.shape[1]
    for edge in range(16):
        block, side = edge // 4, edge % 4
        entry = recv_ref[block, side]
        source, slot = entry // 2, entry % 2
        out_ref[2 * edge], out_ref[2 * edge + 1] = source, slot
        back = lax.rem(2 * me - source + count, count)
        near_ref[edge] = send_ref[slot, back] // 4
        near_ref[16 + edge] = lax.rem(source - me + count, count)
    for block in range(NB):
        for vertex in range(4):
            i_side, k_side = vertex // 2, 2 + vertex % 2
            for sheet, (side, then) in enumerate(((i_side, k_side), (k_side, i_side))):
                at, offset = block, 0
                for step, across in enumerate((side, then, side ^ 1, then ^ 1)):
                    edge = at * 4 + across
                    at, offset = near_ref[edge], offset + near_ref[16 + edge]
                    place = route_at(block, vertex, sheet, step)
                    out_ref[place] = lax.rem(me + offset, count)
                    out_ref[place + 1] = at


def route_at(block, vertex, sheet, step):
    return 32 + (((block * 4 + vertex) * 2 + sheet) * 4 + step) * 2


ROUTES = 32 + 32 * 8


def strip_of(got_ref, route_ref, block, side, unit, units):
    edge = block * 4 + side
    return got_ref[route_ref[2 * edge] * units + unit + route_ref[2 * edge + 1]]


def turned(rows, target, lane):
    return pltpu.roll(rows, lax.rem(target + LANES - lane, LANES), axis=1)


def gather_ghosts(got_ref, route_ref, ghost_ref, fan_ref, units, old_ref):
    lane = lane_ids(SZ)
    for block in range(NB):
        for side in range(4):
            strip = strip_of(got_ref, route_ref, block, side, 0, units)
            for sheet in range(2):
                ghost_ref[:, sheet * NB + block, side * LANES : (side + 1) * LANES] = strip
        for sheet in range(2):
            row = sheet * NB + block
            value = jnp.zeros((SZ, LANES), F32) if old_ref is None else old_ref[:, row, :]
            for vertex in range(4):
                far = (1 - vertex // 2) * 2 + 1 - vertex % 2
                beyond = far ^ 2 if sheet == 0 else far ^ 1
                first = vertex * 16

                def cells(step, corner, target, low, high, value):
                    place = route_at(block, vertex, sheet, step)
                    rows = got_ref[route_ref[place] * units + 2]
                    rows = turned(rows, target, route_ref[place + 1] * EDGE + corner * 8)
                    return jnp.where((lane >= low) & (lane < high), rows, value)

                value = cells(1, far, first, first, first + 6, value)
                value = cells(2, beyond, first + 6, first + 6, first + 9, value)
                value = cells(3, vertex, first + 9, first + 9, first + 10, value)
                if old_ref is None:
                    place = route_at(block, vertex, sheet, 2)
                    at = route_ref[place + 1]
                    rows = got_ref[route_ref[place] * units + 3 + at // 2]
                    rows = turned(rows, first + 10, 96 + (at % 2) * 16 + beyond * 4)
                    value = jnp.where(lane == first + 10, rows, value)
            ghost_ref[:, row, SEG:] = value
            fan_ref[:, row, :] = value


def gather_rhs(got_ref, route_ref, ghost_ref, units):
    lane = lane_ids(SZ)
    for block in range(NB):
        for vertex in range(4):
            strip = strip_of(got_ref, route_ref, block, vertex, 3, units)
            far = (1 - vertex // 2) * 2 + 1 - vertex % 2
            for sheet in range(2):
                place = route_at(block, vertex, sheet, 1)
                at = route_ref[place + 1]
                rows = got_ref[route_ref[place] * units + 3 + at // 2]
                rows = turned(rows, 96, (96 + (at % 2) * 16 + far * 4))
                value = jnp.where(lane < 96, strip, jnp.where(lane < 99, rows, 0.0))
                ghost_ref[:, sheet * NB + block, vertex * LANES : (vertex + 1) * LANES] = value


def moved(tiles, value, lane_from, place):
    tile, at = place // LANES, place % LANES
    turn = (at - lane_from) % LANES
    value = pltpu.roll(value, turn, axis=1) if turn else value
    tiles[tile] = jnp.where(lane_ids(value.shape[0]) == at, value, tiles[tile])


def tiles_of(x):
    return [x[:, at : at + LANES] for at in range(0, WIDTH, LANES)]


def fold(ext):
    last = [ext[:NB, WIDTH - LANES : WIDTH]]
    for vertex in range(4):
        place = vertex_place(vertex)
        tile = place // LANES * LANES
        moved(last, ext[NB:, tile : tile + LANES], place % LANES, 112 + vertex)
    return jnp.concatenate([ext[:NB, : WIDTH - LANES], last[0]], axis=1)


def unfold(rows):
    tiles = tiles_of(rows)
    last = tiles[-1]
    for vertex in range(4):
        moved(tiles, last, 112 + vertex, vertex_place(vertex))
    return jnp.concatenate([rows[:, :WIDTH], jnp.concatenate(tiles, axis=1)], axis=0)


def both_sheets(rows, corners):
    tiles = tiles_of(rows)
    if corners:
        segment = rows[:, WIDTH + LANES : WIDTH + 2 * LANES]
        for vertex in range(4):
            for at in range(3):
                moved(tiles, segment, vertex * 16 + at, place_of(*vertex_cell(vertex, *PATCH[at])))
    return jnp.concatenate([rows[:, :WIDTH], jnp.concatenate(tiles, axis=1)], axis=0)


def corner_tiles():
    cells = [vertex_cell(vertex, *cell) for vertex in range(4) for cell in PATCH[:3]]
    return sorted({place_of(*cell) // LANES for cell in cells})


def third_cells(fan):
    tiles = {tile: jnp.zeros((8, LANES), F32) for tile in corner_tiles()}
    for vertex in range(4):
        moved(tiles, fan, vertex * 16 + 6, vertex_place(vertex))
        moved(tiles, fan, vertex * 16 + 7, place_of(*vertex_cell(vertex, 0, 1)))
        moved(tiles, fan, vertex * 16 + 8, place_of(*vertex_cell(vertex, 1, 0)))
    return tiles


def third_sums(fan):
    total = (fan + shifted(fan, -1)) + (shifted(fan, -2) - shifted(fan, -3))
    tiles = {tile: jnp.zeros((8, LANES), F32) for tile in corner_tiles()}
    for vertex in range(4):
        moved(tiles, total, vertex * 16 + 7, vertex_place(vertex))
    return tiles


def merge(x, mask):
    return jnp.where(mask, pltpu.roll(x, NB, axis=0), x)


def second_halves(x):
    return jnp.concatenate([x, x], axis=0)


def first_unpack(route_ref, got_ref, p_ref, rim_ref, up_ref, down_ref):
    lane = lane_ids(SZ)
    for block in range(NB):
        strips = [strip_of(got_ref, route_ref, block, side, 0, 2) for side in range(4)]
        for comp in range(4):
            value = jnp.zeros((SZ, LANES), F32)
            for side in range(4):
                turn = EDGE * (side - comp) % LANES
                part = pltpu.roll(strips[side], turn, axis=1) if turn else strips[side]
                value = jnp.where(lane // EDGE == side, part, value)
            rim_ref[:, comp * NB + block, :] = value
    for layer in range(REACH):
        for comp in range(3):
            at = (layer * 3 + comp) * LANES
            up_ref[:, at : at + LANES] = rim_ref[layer + 1, comp * NB : (comp + 1) * NB, :]
            down_ref[:, at : at + LANES] = rim_ref[layer, comp * NB : (comp + 1) * NB, :]
    up_ref[:, RIMS:] = p_ref[:, SZ - 1, :]
    down_ref[:, RIMS:] = p_ref[:, 0, :]


RIMS = 3 * REACH * LANES


def send_planes(ext, fan, layer, up_ref, down_ref):
    for ref in (up_ref, down_ref):
        ref[layer, :, :WIDTH] = ext[:NB]
        ref[layer, :, WIDTH : WIDTH + LANES] = fan[:NB]
        ref[layer, :, WIDTH + LANES :] = fan[NB:]


def middle_unpack(
    route_ref, got_ref, p_ref, rhs_ref, place_ref, place_rhs_ref,
    own_ref, fan_ref, div_ref, up_ref, down_ref, ghost_ref, rhs_ghost_ref, block_ref,
):
    gather_ghosts(got_ref, route_ref, ghost_ref, fan_ref, 5, None)
    gather_rhs(got_ref, route_ref, rhs_ghost_ref, 5)
    placed = pick(ghost_ref[...].reshape(SZ * 8, SEG + LANES), place_ref[...])
    placed_rhs = pick(rhs_ghost_ref[...].reshape(SZ * 8, SEG), place_rhs_ref[...])
    for which, ref in enumerate((p_ref, rhs_ref)):
        whole = expand(ref[...].reshape(NB * SZ, CELLS))
        for block in range(NB):
            for sheet in range(2):
                block_ref[which, :, sheet * NB + block, :] = whole[block * SZ : (block + 1) * SZ]
    for layer in range(SZ):
        ext = block_ref[0, layer] + placed[layer * 8 : (layer + 1) * 8]
        own_ref[layer] = ext
        send_planes(ext, fan_ref[layer], layer, up_ref, down_ref)
        ext = block_ref[1, layer] + placed_rhs[layer * 8 : (layer + 1) * 8]
        div_ref[layer] = ext
        if layer >= 1:
            up_ref[SZ + layer - 1, :, :WIDTH] = fold(ext)
        if layer < SZ - 1:
            down_ref[SZ + layer, :, :WIDTH] = fold(ext)


def last_unpack(
    route_ref, got_ref, p_ref, old_ref, place_ref, block_ref, own_ref, fan_ref, up_ref, down_ref, ghost_ref
):
    gather_ghosts(got_ref, route_ref, ghost_ref, fan_ref, 3, old_ref)
    placed = pick(ghost_ref[...].reshape(SZ * 8, SEG + LANES), place_ref[...])
    for layer in range(SZ):
        ext = jnp.where(block_ref[...] > 0.0, p_ref[layer], 0.0) + placed[layer * 8 : (layer + 1) * 8]
        own_ref[layer] = ext
        send_planes(ext, fan_ref[layer], layer, up_ref, down_ref)


def rim_rows(ref, layer):
    rows = [ref[:, (3 * layer + comp) * LANES : (3 * layer + comp + 1) * LANES] for comp in range(3)]
    return jnp.concatenate(rows + [jnp.zeros((NB, LANES), F32)], axis=0)


def halves(x):
    high = x.astype(BF16)
    return high, (x - high.astype(F32)).astype(BF16)


def product(x, high, low, contract):
    rows = x.shape[0]
    dims = (((1,), (contract,)), ((), ()))
    parts = halves(x)
    both = lax.dot_general(jnp.concatenate(parts, axis=0), high, dims, preferred_element_type=F32)
    return (both[:rows] + both[rows:]) + lax.dot_general(parts[0], low, dims, preferred_element_type=F32)


def weigh(
    at_ref, block_ref, cells_ref, layer_ref, fraction_ref, weight_ref, target_ref, high_ref, low_ref, span_ref, aim_ref
):
    group = high_ref.shape[1] // 2
    along = lax.broadcasted_iota(jnp.int32, (EDGE, group), 0)
    for which in range(2):
        lanes = pl.ds(pl.multiple_of(at_ref[which] * group, group), group)
        here = slice(which * group, (which + 1) * group)
        corner = cells_ref[0:1, lanes]
        row_i, row_k = corner // EDGE, corner % EDGE
        weight = weight_ref[:, lanes]
        lines = []
        for a in range(4):
            line = jnp.zeros((EDGE, group), F32)
            for b in range(4):
                line = jnp.where(along == row_k + b, weight[4 * a + b : 4 * a + b + 1], line)
            lines.append(line)
        for i in range(EDGE):
            value = jnp.zeros((EDGE, group), F32)
            for a in range(4):
                value = jnp.where(row_i + a == i, lines[a], value)
            high, low = halves(value)
            high_ref[i * EDGE : (i + 1) * EDGE, here] = high
            low_ref[i * EDGE : (i + 1) * EDGE, here] = low
        start = layer_ref[:, lanes] - (at_ref[which] + which) * SZ
        fraction = fraction_ref[:, lanes]
        phi = [0.25 * (1.0 + jnp.cos(0.5 * math.pi * distance)) for distance in
               (1.0 + fraction, fraction, 1.0 - fraction, 2.0 - fraction)]
        for at in range(SZ + 2 * REACH):
            value = jnp.zeros((1, group), F32)
            for a in range(4):
                value = jnp.where(start + a == at - REACH, phi[a], value)
            span_ref[at : at + 1, here] = value
        aim_ref[0:3, here] = target_ref[:, lanes]
        aim_ref[3:4, here] = block_ref[:, lanes].astype(F32)


def diffused(cells_at, rims, spread, layer):
    cell = lax.broadcasted_iota(jnp.int32, (16, CELLS), 1)
    here = cells_at(layer)
    around = jnp.where(cell >= EDGE, shifted(here, EDGE), 0.0)
    around += jnp.where(cell < CELLS - EDGE, shifted(here, -EDGE), 0.0)
    around += jnp.where(cell % EDGE != 0, shifted(here, 1), 0.0)
    around += jnp.where(cell % EDGE != EDGE - 1, shifted(here, -1), 0.0)
    around += pick(rims, spread)
    around += cells_at(layer - 1) + cells_at(layer + 1)
    eddy = second_halves(second_halves(here[3 * NB :]))
    return here + eddy * (around - 6.0 * here)


def span_row(span_ref, layer):
    return span_ref[layer + REACH : layer + REACH + 1, :]


def layers_of(own_ref, low_ref, high_ref):
    def at(layer):
        if layer < 0:
            return low_ref[layer + SZ]
        return own_ref[layer] if layer < SZ else high_ref[layer - SZ]

    return at


def samples(tilde_ref, plane_high_ref, plane_low_ref, weights):
    dots = product(tilde_ref[...].reshape(len(weights) * 16, CELLS), plane_high_ref[...], plane_low_ref[...], 0)
    return sum(weight * dots[at * 16 : (at + 1) * 16] for at, weight in enumerate(weights))


def own_layers(
    own_ref, low_ref, high_ref, rim_ref, spread_ref, plane_high_ref, plane_low_ref, span_ref, tilde_ref, total_ref
):
    cells_at = layers_of(own_ref, low_ref, high_ref)
    for layer in range(SZ):
        tilde_ref[layer] = diffused(cells_at, rim_ref[layer], spread_ref[...], layer)
    total_ref[...] = samples(tilde_ref, plane_high_ref, plane_low_ref, [span_row(span_ref, layer) for layer in range(SZ)])


def forcing(
    send_ref, count_ref, own_ref, low_ref, high_ref, tilde_ref, total_ref, rim_low_ref, rim_high_ref, spread_ref,
    edge_ref, plane_high_ref, plane_low_ref, span_ref, aim_ref, star_ref, out_ref, up_ref, down_ref, beside_ref, table_ref,
):
    markers = plane_high_ref.shape[1]
    group = markers // 2
    cells_at = layers_of(own_ref, low_ref, high_ref)
    halo = [-3, -2, -1, SZ, SZ + 1, SZ + 2]
    for at, layer in enumerate(halo):
        rims = rim_rows(rim_low_ref, layer + SZ - 1) if layer < 0 else rim_rows(rim_high_ref, layer - SZ)
        beside_ref[at] = diffused(cells_at, rims, spread_ref[...], layer)
    total = total_ref[...] + samples(beside_ref, plane_high_ref, plane_low_ref, [span_row(span_ref, layer) for layer in halo])
    mine = (lax.broadcasted_iota(jnp.int32, (16, markers), 0) % NB).astype(F32) == aim_ref[3:4, :]
    total = jnp.where(mine, total, 0.0)
    place = lax.broadcasted_iota(jnp.int32, (1, markers), 1) % group
    live = place < count_ref[0]
    rows = []
    for comp in range(3):
        sampled = jnp.sum(total[comp * NB : (comp + 1) * NB], axis=0, keepdims=True)
        force = jnp.where(live, aim_ref[comp : comp + 1, :] - sampled, 0.0)
        rows.append(jnp.broadcast_to(force, (NB, markers)))
    rows.append(jnp.zeros((NB, markers), F32))
    force = jnp.where(mine, jnp.concatenate(rows, axis=0), 0.0)
    pushes = jnp.concatenate([span_row(span_ref, layer) * force for layer in range(SZ)], axis=0)
    spread = product(pushes, plane_high_ref[...], plane_low_ref[...], 1)
    star = tilde_ref[...].reshape(SZ * 16, CELLS) + spread
    star_ref[...] = star.reshape(SZ, 16, CELLS)
    up_ref[...] = star_ref[SZ - 1, 2 * NB : 3 * NB, :]
    down_ref[...] = star_ref[0, 2 * NB : 3 * NB, :]
    rims = pick(star, edge_ref[...])
    lane = lane_ids(NB)
    for side in range(4):
        value = jnp.zeros((NB, LANES), F32)
        for layer in range(SZ):
            row = layer * 16 + side // 2 * NB
            part = rims[row : row + NB]
            turn = EDGE * (layer - side) % LANES
            if turn:
                part = pltpu.roll(part, turn, axis=1)
            value = jnp.where(lane // EDGE == layer, part, value)
        for block in range(NB):
            table_ref[block * 4 + side] = value[block : block + 1]

    def one(target, carry):
        for slot in range(2):
            out_ref[target, slot : slot + 1, :] = table_ref[jnp.maximum(send_ref[slot, target], 0)]
        return carry

    lax.fori_loop(0, out_ref.shape[0], one, 0, unroll=4)


def half_step(star_ref, p_ref, low_ref, high_ref, rim_ref, spread_ref, out_ref):
    cell = lax.broadcasted_iota(jnp.int32, (NB, CELLS), 1)
    left, right = cell >= EDGE, cell < CELLS - EDGE
    front, back = cell % EDGE != 0, cell % EDGE != EDGE - 1
    rims = pick(jnp.concatenate([rim_ref[layer, 3 * NB :, :] for layer in range(SZ)], axis=0), spread_ref[...])

    def pressure_at(layer):
        if layer < 0:
            return low_ref[:, RIMS:]
        return p_ref[:, layer, :] if layer < SZ else high_ref[:, RIMS:]

    planes = [pressure_at(layer) for layer in range(-1, SZ + 1)]
    for layer in range(SZ):
        rows = star_ref[layer]
        first, second = rows[:NB], rows[NB : 2 * NB]
        flat = jnp.where(right, shifted(first, -EDGE), 0.0) - jnp.where(left, shifted(first, EDGE), 0.0)
        flat += jnp.where(back, shifted(second, -1), 0.0) - jnp.where(front, shifted(second, 1), 0.0)
        if layer < SZ - 1:
            flat += star_ref[layer + 1, 2 * NB : 3 * NB, :]
        if layer > 0:
            flat -= star_ref[layer - 1, 2 * NB : 3 * NB, :]
        out_ref[layer, :NB] = 0.5 * flat
        here = planes[layer + 1]
        around = jnp.where(left, shifted(here, EDGE), 0.0) + jnp.where(right, shifted(here, -EDGE), 0.0)
        around += jnp.where(front, shifted(here, 1), 0.0) + jnp.where(back, shifted(here, -1), 0.0)
        around += rims[layer * NB : (layer + 1) * NB] + (planes[layer] + planes[layer + 2])
        out_ref[layer, NB:] = around


def first_step(
    route_ref, send_ref, got_ref, star_ref, pressure_ref, p_low_ref, p_high_ref, rim_ref, spread_ref,
    low_ref, high_ref, across_ref, pack_ref, pack_rhs_ref,
    p_ref, rhs_ref, out_ref, half_ref, near_ref, table_ref, corner_ref, rhs_table_ref,
):
    half_step(star_ref, pressure_ref, p_low_ref, p_high_ref, rim_ref, spread_ref, half_ref)
    lane = lane_ids(NB)
    for side in range(4):
        for block in range(NB):
            edge = block * 4 + side
            rows = got_ref[route_ref[2 * edge]]
            near_ref[side, block : block + 1, :] = jnp.where(route_ref[2 * edge + 1] == 1, rows[1:2], rows[0:1])
    beyond = []
    for layer in range(SZ):
        value = jnp.zeros((NB, LANES), F32)
        for side in range(4):
            turn = EDGE * (side - layer) % LANES
            part = pltpu.roll(near_ref[side], turn, axis=1) if turn else near_ref[side]
            value = jnp.where(lane // EDGE == side, part, value)
        beyond.append(value)
    across = pick(jnp.concatenate(beyond, axis=0), across_ref[...])
    for layer in range(SZ):
        rhs = half_ref[layer, :NB, :] + across[layer * NB : (layer + 1) * NB]
        if layer == 0:
            rhs -= 0.5 * low_ref[...]
        if layer == SZ - 1:
            rhs += 0.5 * high_ref[...]
        rhs_ref[:, layer, :] = rhs
        p_ref[:, layer, :] = (half_ref[layer, NB:, :] - rhs) * (1.0 / 6.0)
    store_strips(pick(p_ref[...].reshape(NB * SZ, CELLS), pack_ref[...]), table_ref, corner_ref)
    store_rhs_strips(pick(rhs_ref[...].reshape(NB * SZ, CELLS), pack_rhs_ref[...]), rhs_table_ref)
    post(
        send_ref, out_ref, out_ref.shape[0] // 5,
        [(table_ref, 0, 0), (table_ref, 1, 0), (corner_ref, None, 0), (rhs_table_ref, 0, 0), (rhs_table_ref, 1, 16)],
    )


def sweep(source, target, step, rhs_ref, mask, codes, thirds):
    layers = SZ + 2 * DEPTH
    for at in range(step, layers - step):
        here = source[at]
        sides = [shifted(here, STRIDE), shifted(here, -STRIDE), shifted(here, 1), shifted(here, -1)]
        if at - DEPTH in thirds:
            for side in range(4):
                tiles = tiles_of(sides[side])
                for tile, cells in thirds[at - DEPTH].items():
                    code = codes[tile]
                    found = code == side + 1
                    if step == 1:
                        found = found | (code == side + 5)
                    tiles[tile] = jnp.where(found, cells, tiles[tile])
                sides[side] = jnp.concatenate(tiles, axis=1)
        around = (sides[0] + sides[1]) + (sides[2] + sides[3])
        around += source[at - 1] + source[at + 1]
        around -= rhs_ref[at - 1]
        target[at] = merge(around * (1.0 / 6.0), mask)


def load_layers(work_ref, own_ref, low_ref, high_ref):
    for layer in range(SZ):
        work_ref[layer] = both_sheets(low_ref[layer], layer >= 2)
        work_ref[DEPTH + layer] = own_ref[layer]
        work_ref[DEPTH + SZ + layer] = both_sheets(high_ref[layer], layer < 2)


def beside_segments(ref, layer):
    return jnp.concatenate([ref[layer, :, WIDTH : WIDTH + LANES], ref[layer, :, WIDTH + LANES :]], axis=0)


def sweeps(work_ref, other_ref, own_ref, fan_ref, low_ref, high_ref, rhs_ref, mask, codes, steps):
    load_layers(work_ref, own_ref, low_ref, high_ref)
    codes = tiles_of(codes)
    thirds = {layer: third_cells(fan_ref[layer]) for layer in range(SZ)}
    thirds[-1] = third_cells(beside_segments(low_ref, SZ - 1))
    thirds[SZ] = third_cells(beside_segments(high_ref, 0))
    later = {}
    for layer in range(SZ):
        later[layer] = {}
        for tile, total in third_sums(fan_ref[layer]).items():
            around = total + own_ref[layer, :, tile * LANES : (tile + 1) * LANES]
            later[layer][tile] = (around + (thirds[layer - 1][tile] + thirds[layer + 1][tile])) * (1.0 / 6.0)
    refs = (work_ref, other_ref)
    for step in range(1, steps + 1):
        given = thirds if step == 1 else later if step == 2 else {}
        sweep(refs[(step + 1) % 2], refs[step % 2], step, rhs_ref, mask, codes, given)
    return refs[steps % 2]


def middle_sweeps(
    send_ref, own_ref, fan_ref, low_ref, high_ref, div_ref, mask_ref, codes_ref, pack_ref,
    p_ref, rhs_ref, out_ref, work_ref, other_ref, rows_ref, table_ref, corner_ref,
):
    for layer in range(REACH):
        rhs_ref[layer] = unfold(low_ref[SZ + layer])
        rhs_ref[REACH + SZ + layer] = unfold(high_ref[SZ + layer])
    for layer in range(SZ):
        rhs_ref[REACH + layer] = div_ref[layer]
    done = sweeps(
        work_ref, other_ref, own_ref, fan_ref, low_ref, high_ref, rhs_ref, mask_ref[...] > 0.0, codes_ref[...], 4
    )
    for layer in range(SZ):
        here = done[DEPTH + layer]
        p_ref[layer] = here
        rows_ref[:, layer, :] = here[:NB]
    store_strips(pick(rows_ref[...].reshape(NB * SZ, WIDTH), pack_ref[...]), table_ref, corner_ref)
    post(
        send_ref, out_ref, out_ref.shape[0] // 3, [(table_ref, 0, 0), (table_ref, 1, 0), (corner_ref, None, 0)]
    )


def last_sweeps(
    own_ref, fan_ref, low_ref, high_ref, rhs_ref, mask_ref, codes_ref, star_ref, velocity_ref, p_ref, work_ref, other_ref
):
    done = sweeps(
        work_ref, other_ref, own_ref, fan_ref, low_ref, high_ref, rhs_ref, mask_ref[...] > 0.0, codes_ref[...], 3
    )
    for layer in range(SZ):
        here = done[DEPTH + layer]
        rows = [
            shifted(here, -STRIDE) - shifted(here, STRIDE),
            shifted(here, -1) - shifted(here, 1),
            done[DEPTH + layer + 1] - done[DEPTH + layer - 1],
            here,
        ]
        flat = compact(jnp.concatenate([row[:NB] for row in rows], axis=0))
        velocity_ref[:, layer, :] = (star_ref[layer] - 0.5 * flat)[: 3 * NB]
        p_ref[:, layer, :] = flat[3 * NB :]


def call(kernel, name, out_shapes, scratch, scalars, types=None):
    smem, vmem = pl.BlockSpec(memory_space=pltpu.SMEM), pl.BlockSpec(memory_space=pltpu.VMEM)
    types = types or (F32,) * len(out_shapes)
    shapes = tuple(jax.ShapeDtypeStruct(shape, held) for shape, held in zip(out_shapes, types))

    def run(*args):
        return pl.pallas_call(
            kernel,
            name=name,
            out_shape=shapes,
            in_specs=[smem if at < scalars else vmem for at in range(len(args))],
            out_specs=tuple(vmem for _ in shapes),
            scratch_shapes=scratch,
            compiler_params=pltpu.CompilerParams(vmem_limit_bytes=24 << 20),
        )(*args)

    return run


def trade(messages, count):
    whole = messages.reshape((count, -1) + messages.shape[1:])
    got = lax.all_to_all(whole, "chord", split_axis=0, concat_axis=0, tiled=True)
    return got.reshape(messages.shape)


def beside(up, down):
    size = lax.axis_size("span")
    low = lax.ppermute(up, "span", [(i, (i + 1) % size) for i in range(size)])
    high = lax.ppermute(down, "span", [(i, (i + size - 1) % size) for i in range(size)])
    return low, high


def local(
    velocity,
    pressure,
    viscosity,
    send_list,
    recv_slot,
    marker_block,
    marker_cells,
    marker_layer,
    marker_frac,
    marker_weights,
    marker_target,
    marker_count,
):
    count, strips = lax.axis_size("chord"), lax.axis_size("span")
    me = lax.axis_index("chord").astype(jnp.int32).reshape(1)
    at = lax.axis_index("span").astype(jnp.int32)
    send = send_list.T
    rim, spread, across = jnp.asarray(RIM), jnp.asarray(RIM.T), jnp.asarray(ACROSS)
    pack_flat, pack_rhs, pack_ext = jnp.asarray(PACK_FLAT), jnp.asarray(PACK_RHS), jnp.asarray(PACK_EXT)
    place, place_rhs, codes = jnp.asarray(PLACE), jnp.asarray(PLACE_RHS), jnp.asarray(CODES)
    mask, inside = jnp.asarray(MASK), jnp.asarray(INSIDE)

    plane, flat, rows = (SZ, 8, WIDTH), (SZ, 16, CELLS), (NB, SZ, CELLS)
    fans = (SZ, 8, LANES)
    vmem = lambda *shape: pltpu.VMEM(shape, F32)
    table, layers = vmem(16, SZ, LANES), vmem(SZ + 2 * DEPTH, 8, WIDTH)

    anywhere = pl.BlockSpec(memory_space=pl.ANY)
    messages = pl.pallas_call(
        first_pack,
        name="first_pack",
        out_shape=jax.ShapeDtypeStruct((2 * count, SZ, LANES), F32),
        in_specs=[anywhere] * 4,
        out_specs=pl.BlockSpec(memory_space=pltpu.VMEM),
        scratch_shapes=[
            pltpu.SMEM((2, count), jnp.int32),
            vmem(3 * NB, SZ, CELLS),
            vmem(NB, SZ, CELLS),
            pltpu.VMEM((CELLS, LANES), BF16),
            table,
            pltpu.SemaphoreType.DMA((4,)),
        ],
        compiler_params=pltpu.CompilerParams(vmem_limit_bytes=60 << 20),
    )(send, velocity.reshape(3 * NB, SZ, CELLS), pressure, rim)
    got = trade(messages, count)
    me, _ = lax.optimization_barrier((me, messages))
    route = pl.pallas_call(
        routes,
        name="routes",
        out_shape=jax.ShapeDtypeStruct((ROUTES,), jnp.int32),
        in_specs=[pl.BlockSpec(memory_space=pltpu.SMEM)] * 3,
        out_specs=pl.BlockSpec(memory_space=pltpu.SMEM),
        scratch_shapes=[pltpu.SMEM((32,), jnp.int32)],
    )(me, send, recv_slot)
    later, eddy, route = lax.optimization_barrier((velocity, viscosity, route))
    cells = jnp.concatenate([later, eddy[None]], axis=0)
    cells = jnp.transpose(cells, (2, 0, 1, 3)).reshape(SZ, 16, CELLS)
    cells_low, cells_high = beside(cells, cells)

    group = marker_block.shape[0] // strips
    groups = jnp.stack([at, (at + strips - 1) % strips])
    held = (CELLS, 2 * group)
    weights_high, weights_low, spans, aims = call(
        weigh, "weigh", [held, held, (16, 2 * group), (4, 2 * group)], [], 1, (BF16, BF16, F32, F32)
    )(
        groups, marker_block[None], marker_cells, marker_layer[None], marker_frac[None], marker_weights, marker_target
    )

    edge = (NB, RIMS + CELLS)
    rims, up, down = call(first_unpack, "first_unpack", [(SZ, 16, LANES), edge, edge], [], 1)(route, got, pressure)
    low, high = beside(up, down)
    tilde, total = call(own_layers, "own_layers", [flat, (16, 2 * group)], [], 0)(
        cells, cells_low, cells_high, rims, spread, weights_high, weights_low, spans
    )
    star, messages, up, down = call(
        forcing, "forcing", [flat, (count, 2, LANES), (NB, CELLS), (NB, CELLS)], [vmem(6, 16, CELLS), vmem(16, 1, LANES)], 2
    )(
        send, marker_count, cells, cells_low, cells_high, tilde, total, low, high, spread, rim, weights_high, weights_low, spans, aims
    )
    got = trade(messages, count)
    up, down, got = lax.optimization_barrier((up, down, got))
    star_low, star_high = beside(up, down)

    p, div, messages = call(
        first_step, "first_step", [rows, rows, (5 * count, SZ, LANES)],
        [vmem(SZ, 8, CELLS), vmem(4, NB, LANES), table, vmem(1, SZ, LANES), vmem(32, SZ, LANES)], 2,
    )(
        route, send, got, star, pressure, low, high, rims, spread, star_low, star_high, across, pack_flat, pack_rhs
    )
    got = trade(messages, count)
    edge = (SZ + REACH, NB, WIDTH + 2 * LANES)
    own, fan, div, up, down = call(
        middle_unpack, "middle_unpack", [plane, fans, plane, edge, edge],
        [vmem(SZ, 8, SEG + LANES), vmem(SZ, 8, SEG), vmem(2, SZ, 8, WIDTH)], 1,
    )(route, got, p, div, place, place_rhs)
    low, high = beside(up, down)
    p, rhs, messages = call(
        middle_sweeps, "middle_sweeps", [plane, (SZ + 2 * REACH, 8, WIDTH), (3 * count, SZ, LANES)],
        [layers, layers, vmem(NB, SZ, WIDTH), table, vmem(1, SZ, LANES)], 1,
    )(send, own, fan, low, high, div, mask, codes, pack_ext)
    got = trade(messages, count)
    edge = (SZ, NB, WIDTH + 2 * LANES)
    own, fan, up, down = call(
        last_unpack, "last_unpack", [plane, fans, edge, edge], [vmem(SZ, 8, SEG + LANES)], 1
    )(route, got, p, fan, place, inside)
    low, high = beside(up, down)
    velocity_next, pressure_next = call(
        last_sweeps, "last_sweeps", [(3 * NB, SZ, CELLS), rows], [layers, layers], 0
    )(own, fan, low, high, rhs, mask, codes, star)
    return velocity_next.reshape(velocity.shape), pressure_next


RIM = rim_matrix()
ACROSS = across_matrix()
PACK_FLAT = pack_matrix(CELLS, lambda i, k: EDGE * i + k)
PACK_RHS = pack_rhs_matrix()
PACK_EXT = pack_matrix(WIDTH, place_of)
PLACE = place_matrix()
PLACE_RHS = place_rhs_matrix()
CODES = fan_codes()
MASK = sheet_mask()
INSIDE = block_mask()


def solution(mesh):
    in_specs = (
        P(None, "chord", "span", None),
        P("chord", "span", None),
        P("chord", "span", None),
        P("chord", None),
        P("chord", None),
        P("chord"),
        P(None, "chord"),
        P("chord"),
        P("chord"),
        P(None, "chord"),
        P(None, "chord"),
        P("chord"),
    )
    out_specs = (P(None, "chord", "span", None), P("chord", "span", None))
    return jax.shard_map(local, mesh=mesh, in_specs=in_specs, out_specs=out_specs, check_vma=False)
```

time: 190 us -> 188 us (0.989)
  Pallas kernels: 24.6 us -> 21.7 us
  waiting for transfers between devices: 16.9 us -> 14.6 us
  blocking collectives: 77.5 us -> 79.4 us
    all_to_all x1, waiting for transfers between devices: 11.6 us -> 7.16 us  [trade(): lax.all_to_all(whole, 'chord', split_axis=0, concat_axis=0, tiled=True)]
    ppermute x5, waiting for transfers between devices: 0.71 us -> 4.83 us  [beside(): low = lax.ppermute(up, 'span', [(i, (i + 1) % size) for i in range(size)])]
    ppermute x5, waiting for transfers between devices: 4.63 us -> 2.56 us  [beside(): lax.ppermute(down, 'span', [(i, (i + size - 1) % size) for i in range(siz...]
    pallas_call x10 -> x9, Pallas kernels: 19.1 us -> 17.2 us  [run(): pl.pallas_call(kernel, name=name, out_shape=shapes, in_specs=[smem if at...]
    all_to_all x3, blocking collectives: 77.5 us -> 79.4 us  [trade(): lax.all_to_all(whole, 'chord', split_axis=0, concat_axis=0, tiled=True)]
  transfers between devices with their start and end apart: 11 -> 11, of which waited for: 7 -> 6; matrix products, arithmetic and copies ran while one was open for 0% -> 1% of each run, Pallas kernels for 3% -> 2%
where the time goes in v3:
time: 188 us; the launch traced here: 187 us
  blocking collectives  79.4 us (42%)
  starting transfers between devices  67.2 us (36%)
  Pallas kernels  21.7 us (12%)
  waiting for transfers between devices  14.6 us (8%)
    all_to_all x3, blocking collectives, trade(): lax.all_to_all(whole, 'chord', split_axis=0, concat_axis=0, tiled=True)  79.4 us
    ppermute x5, starting transfers between devices, beside(): lax.ppermute(down, 'span', [(i, (i + size - 1) % size) for i in range(siz...  34 us
    all_to_all x1, starting transfers between devices, trade(): lax.all_to_all(whole, 'chord', split_axis=0, concat_axis=0, tiled=True)  22.4 us
    pallas_call x9, Pallas kernels, run(): pl.pallas_call(kernel, name=name, out_shape=shapes, in_specs=[smem if at...  17.2 us
    ppermute x5, starting transfers between devices, beside(): low = lax.ppermute(up, 'span', [(i, (i + 1) % size) for i in range(size)])  10.9 us
    all_to_all x1, waiting for transfers between devices, trade(): lax.all_to_all(whole, 'chord', split_axis=0, concat_axis=0, tiled=True)  7.16 us
    ppermute x5, waiting for transfers between devices, beside(): low = lax.ppermute(up, 'span', [(i, (i + 1) % size) for i in range(size)])  4.83 us
  transfers between devices with their start and end apart: 11, of which 6 were waited for; matrix products, arithmetic and copies ran while one was open for 1% of the time, Pallas kernels for 2%

profile of v3, /device:TPU:1, one launch (start us, length us, event | category | flops | bytes accessed | tf_op | source)
XLA Modules:
  0.0 186.7 jit_solution(4491412311118429297)
XLA Ops:
  0.6 0.0 copy-start.1
  0.6 0.0 copy-start.7
  0.7 0.0 copy-start.16
  0.7 0.0 copy-start.12
  0.7 0.0 copy-start.20
  0.7 0.0 copy-start.19
  0.7 0.0 copy-start.11
  0.7 0.0 copy-start.18
  0.7 2.5 %first_pack.1 = f32[96,4,128]{2,1,0:T(4,128)} custom-call(s32[2,48]{1,0:T(2,128)} %bitcast.30, f32[12,4,1024]{2,1,0:T(4,128)} %bitcast.40, f32[4,4,1024]{2,1,0:T(4,128)} %pressure_ref.1, bf16[1024,128]{1,0:T(8,128)(2,1)} %constant.46.clone.rim_any.edge_ref), custom_call_target="tpu_custom_call" | custom-call | tf_op jit(solution)/shard_map/first_pack/pallas_call | solution.py:846
  3.2 0.0 copy-start.6
  3.2 0.0 copy-start.17
  3.2 22.4 %all-to-all-start = ((f32[48,2,4,128]{3,2,1,0:T(4,128)}), f32[48,2,4,128]{3,2,1,0:T(4,128)S(1)}, u32[]{:S(2)}, u32[]{:S(2)}) async-start(f32[48,2,4,128]{3,2,1,0:T(4,128)} %bitcast.39), calls=%async_computation | async-start | bytes 393216 | tf_op jit(solution)/shard_map/all_to_all | solution.py:806
  25.6 2.0 %routes.1.route_ref = s32[288]{0:T(512)} custom-call(s32[1]{0:T(128)} %bitcast.me_ref, s32[2,48]{1,0:T(2,128)} %bitcast.31, s32[4,4]{1,0:T(4,128)} %recv_ref.1), custom_call_target="tpu_custom_call" | custom-call | tf_op jit(solution)/shard_map/routes/pallas_call | solution.py:864
  27.7 1.0 pad_maximum_fusion
  28.7 0.2 copy.28.own_ref
  28.9 4.7 %collective-permute-start.1 = (f32[4,16,1024]{2,1,0:T(8,128)S(1)}, f32[4,16,1024]{2,1,0:T(8,128)S(1)}, u32[]{:S(2)}, u32[]{:S(2)}) collective-permute-start(f32[4,16,1024]{2,1,0:T(8,128)S(1)} %copy.28.own_ref), channel_id=1, source_target_pairs={{0,15},{1,0},{2,1},{3,2},{4,3},{5,4},{6,5},{7,6},{8,7},{9,8},{10,9... | collective-permute-start | bytes 786440 | tf_op jit(solution)/shard_map/ppermute | solution.py:813
  33.6 1.9 %collective-permute-start = (f32[4,16,1024]{2,1,0:T(8,128)S(1)}, f32[4,16,1024]{2,1,0:T(8,128)S(1)}, u32[]{:S(2)}, u32[]{:S(2)}) collective-permute-start(f32[4,16,1024]{2,1,0:T(8,128)S(1)} %copy.28.own_ref), channel_id=1, source_target_pairs={{0,1},{1,2},{2,3},{3,4},{4,5},{5,6},{6,7},{7,8},{8,9},{9,10},{10,1... | collective-permute-start | bytes 786440 | tf_op jit(solution)/shard_map/ppermute | solution.py:812
  35.5 7.2 %all-to-all-done = f32[48,2,4,128]{3,2,1,0:T(4,128)S(1)} async-done(((f32[48,2,4,128]{3,2,1,0:T(4,128)}), f32[48,2,4,128]{3,2,1,0:T(4,128)S(1)}, u32[]{:S(2)}, u32[]{:S(2)}) %all-to-all-start) | async-done | bytes 196640 | tf_op jit(solution)/shard_map/all_to_all | solution.py:806
  42.7 0.0 copy-done.7
  42.7 0.7 copy-done.14
  43.4 0.7 first_unpack.1
  44.1 3.1 %collective-permute-start.2 = (f32[4,2176]{1,0:T(4,128)S(1)}, f32[4,2176]{1,0:T(4,128)S(1)}, u32[]{:S(2)}, u32[]{:S(2)}) collective-permute-start(f32[4,2176]{1,0:T(4,128)S(1)} %get-tuple-element.49), channel_id=1, source_target_pairs={{0,1},{1,2},{2,3},{3,4},{4,5},{5,6},{6,7},{7,8},{8,9},{9,10},{10,1... | collective-permute-start | bytes 104456 | tf_op jit(solution)/shard_map/ppermute | solution.py:812
  47.2 6.1 %collective-permute-start.3 = (f32[4,2176]{1,0:T(4,128)S(1)}, f32[4,2176]{1,0:T(4,128)S(1)}, u32[]{:S(2)}, u32[]{:S(2)}) collective-permute-start(f32[4,2176]{1,0:T(4,128)S(1)} %get-tuple-element.50), channel_id=1, source_target_pairs={{0,15},{1,0},{2,1},{3,2},{4,3},{5,4},{6,5},{7,6},{8,7},{9,8},{10,9... | collective-permute-start | bytes 104456 | tf_op jit(solution)/shard_map/ppermute | solution.py:813
  53.3 0.1 pad_add_fusion.at_ref
  54.0 0.0 copy-done.16
  54.1 1.1 weigh.1
  55.1 0.0 collective-permute-done.1.high_ref
  55.2 0.0 collective-permute-done.low_ref
  55.2 0.0 copy-start.4
  55.2 0.0 copy-start.5
  55.2 0.0 copy-start.8
  55.2 0.0 copy-start.15
  55.2 0.6 own_layers.1
  55.8 0.0 collective-permute-done.2.rim_low_ref.p_low_ref
  55.8 0.0 collective-permute-done.3.rim_high_ref.p_high_ref
  55.9 2.5 %forcing.1 = (f32[4,16,1024]{2,1,0:T(8,128)S(1)}, f32[48,2,128]{2,1,0:T(2,128)S(1)}, f32[4,1024]{1,0:T(4,128)S(1)}, f32[4,1024]{1,0:T(4,128)S(1)}) custom-call(s32[2,48]{1,0:T(2,128)S(1)} %bitcast.32, s32[1]{0:T(128)S(6)} %copy.29.count_ref, f32[4,16,1024]{2,1,0:T(8,128)S(1)} %copy.28.own_ref, f32[4,16,1024]{2,1,0:T(8,128)S(1)} %collective-permute-done.low_ref, ...), custom_call_target="tpu_custom_call" | custom-call | tf_op jit(solution)/shard_map/forcing/pallas_call | solution.py:791
  58.4 23.2 %all_to_all.20 = f32[48,1,2,128]{3,2,1,0:T(2,128)S(1)} all-to-all(f32[48,1,2,128]{3,2,1,0:T(2,128)S(1)} %bitcast.29), channel_id=1, replica_groups=mesh['chord'=48,'span'=16] {'chord'}, dimensions={0} | all-to-all | bytes 98304 | tf_op jit(solution)/shard_map/all_to_all | solution.py:806
  81.6 1.9 %collective-permute-start.4 = (f32[4,1024]{1,0:T(4,128)S(1)}, f32[4,1024]{1,0:T(4,128)S(1)}, u32[]{:S(2)}, u32[]{:S(2)}) collective-permute-start(f32[4,1024]{1,0:T(4,128)S(1)} %get-tuple-element.57), channel_id=1, source_target_pairs={{0,1},{1,2},{2,3},{3,4},{4,5},{5,6},{6,7},{7,8},{8,9},{9,10},{10,1... | collective-permute-start | bytes 49160 | tf_op jit(solution)/shard_map/ppermute | solution.py:812
  83.5 7.3 %collective-permute-start.5 = (f32[4,1024]{1,0:T(4,128)S(1)}, f32[4,1024]{1,0:T(4,128)S(1)}, u32[]{:S(2)}, u32[]{:S(2)}) collective-permute-start(f32[4,1024]{1,0:T(4,128)S(1)} %get-tuple-element.58), channel_id=1, source_target_pairs={{0,15},{1,0},{2,1},{3,2},{4,3},{5,4},{6,5},{7,6},{8,7},{9,8},{10,9... | collective-permute-start | bytes 49160 | tf_op jit(solution)/shard_map/ppermute | solution.py:813
  90.8 0.0 collective-permute-done.4.low_ref
  90.8 0.8 collective-permute-done.5.high_ref
  91.6 0.0 copy-done.4
  91.7 0.0 copy-start
  91.7 0.0 copy-start.3
  91.7 1.9 first_step.1
  93.6 29.8 %all_to_all.21 = f32[48,5,4,128]{3,2,1,0:T(4,128)S(1)} all-to-all(f32[48,5,4,128]{3,2,1,0:T(4,128)S(1)} %bitcast.26), channel_id=1, replica_groups=mesh['chord'=48,'span'=16] {'chord'}, dimensions={0} | all-to-all | bytes 983040 | tf_op jit(solution)/shard_map/all_to_all | solution.py:806
  123.3 0.0 copy-done
  123.4 0.0 copy-start.10
  123.4 2.3 %middle_unpack.1 = (f32[4,8,1664]{2,1,0:T(8,128)S(1)}, f32[4,8,128]{2,1,0:T(8,128)S(1)}, f32[4,8,1664]{2,1,0:T(8,128)S(1)}, f32[7,4,1920]{2,1,0:T(4,128)S(1)}, f32[7,4,1920]{2,1,0:T(4,128)S(1)}) custom-call(s32[288]{0:T(512)S(1)} %copy-done.15, f32[240,4,128]{2,1,0:T(4,128)S(1)} %bitcast.23, f32[4,4,1024]{2,1,0:T(4,128)S(1)} %get-tuple-element.60.p_ref, ...), custom_call_target="tpu_custom_call" | custom-call | tf_op jit(solution)/shard_map/middle_unpack/pallas_call | solution.py:791
  125.6 0.0 copy-start.13
  125.6 2.1 %collective-permute-start.6 = (f32[7,4,1920]{2,1,0:T(4,128)S(1)}, f32[7,4,1920]{2,1,0:T(4,128)S(1)}, u32[]{:S(2)}, u32[]{:S(2)}) collective-permute-start(f32[7,4,1920]{2,1,0:T(4,128)S(1)} %get-tuple-element.64), channel_id=1, source_target_pairs={{0,1},{1,2},{2,3},{3,4},{4,5},{5,6},{6,7},{7,8},{8,9},{9,10},{10,1... | collective-permute-start | bytes 645128 | tf_op jit(solution)/shard_map/ppermute | solution.py:812
  127.7 7.8 %collective-permute-start.7 = (f32[7,4,1920]{2,1,0:T(4,128)S(1)}, f32[7,4,1920]{2,1,0:T(4,128)S(1)}, u32[]{:S(2)}, u32[]{:S(2)}) collective-permute-start(f32[7,4,1920]{2,1,0:T(4,128)S(1)} %get-tuple-element.65), channel_id=1, source_target_pairs={{0,15},{1,0},{2,1},{3,2},{4,3},{5,4},{6,5},{7,6},{8,7},{9,8},{10,9... | collective-permute-start | bytes 645128 | tf_op jit(solution)/shard_map/ppermute | solution.py:813
  135.5 3.4 %collective-permute-done.6.low_ref = f32[7,4,1920]{2,1,0:T(4,128)S(1)} collective-permute-done((f32[7,4,1920]{2,1,0:T(4,128)S(1)}, f32[7,4,1920]{2,1,0:T(4,128)S(1)}, u32[]{:S(2)}, u32[]{:S(2)}) %collective-permute-start.6) | collective-permute-done | bytes 215072 | tf_op jit(solution)/shard_map/ppermute | solution.py:812
  138.9 0.9 collective-permute-done.7.high_ref
  139.8 0.0 copy-done.2
  139.8 3.5 %middle_sweeps.1 = (f32[4,8,1664]{2,1,0:T(8,128)S(1)}, f32[10,8,1664]{2,1,0:T(8,128)S(1)}, f32[144,4,128]{2,1,0:T(4,128)S(1)}) custom-call(s32[2,48]{1,0:T(2,128)S(1)} %bitcast.34, f32[4,8,1664]{2,1,0:T(8,128)S(1)} %get-tuple-element.62.own_ref, f32[4,8,128]{2,1,0:T(8,128)S(1)} %get-tuple-element.63.fan_ref.old_ref, ...), custom_call_target="tpu_custom_call" | custom-call | tf_op jit(solution)/shard_map/middle_sweeps/pallas_call | solution.py:791
  143.3 26.4 %all_to_all.22 = f32[48,3,4,128]{3,2,1,0:T(4,128)S(1)} all-to-all(f32[48,3,4,128]{3,2,1,0:T(4,128)S(1)} %bitcast.27), channel_id=1, replica_groups=mesh['chord'=48,'span'=16] {'chord'}, dimensions={0} | all-to-all | bytes 589824 | tf_op jit(solution)/shard_map/all_to_all | solution.py:806
  169.7 0.0 copy-done.13
  169.7 1.4 last_unpack.1
  171.1 1.9 %collective-permute-start.8 = (f32[4,4,1920]{2,1,0:T(4,128)S(1)}, f32[4,4,1920]{2,1,0:T(4,128)S(1)}, u32[]{:S(2)}, u32[]{:S(2)}) collective-permute-start(f32[4,4,1920]{2,1,0:T(4,128)S(1)} %get-tuple-element.71), channel_id=1, source_target_pairs={{0,1},{1,2},{2,3},{3,4},{4,5},{5,6},{6,7},{7,8},{8,9},{9,10},{10,1... | collective-permute-start | bytes 368648 | tf_op jit(solution)/shard_map/ppermute | solution.py:812
  173.1 8.0 %collective-permute-start.9 = (f32[4,4,1920]{2,1,0:T(4,128)S(1)}, f32[4,4,1920]{2,1,0:T(4,128)S(1)}, u32[]{:S(2)}, u32[]{:S(2)}) collective-permute-start(f32[4,4,1920]{2,1,0:T(4,128)S(1)} %get-tuple-element.72), channel_id=1, source_target_pairs={{0,15},{1,0},{2,1},{3,2},{4,3},{5,4},{6,5},{7,6},{8,7},{9,8},{10,9... | collective-permute-start | bytes 368648 | tf_op jit(solution)/shard_map/ppermute | solution.py:813
  181.1 1.4 collective-permute-done.8.low_ref
  182.5 0.9 collective-permute-done.9.high_ref
  183.4 3.3 %last_sweeps.1 = (f32[12,4,1024]{2,1,0:T(4,128)}, f32[4,4,1024]{2,1,0:T(4,128)}) custom-call(f32[4,8,1664]{2,1,0:T(8,128)S(1)} %get-tuple-element.69.own_ref, f32[4,8,128]{2,1,0:T(8,128)S(1)} %get-tuple-element.70.fan_ref, f32[4,4,1920]{2,1,0:T(4,128)S(1)} %collective-permute-done.8.low_ref, f32[4,4,1920]{2,1,0:T(4,128)S(1)} %collective-permute-done.9.high_ref, ...), custom_call_target="tpu_custom_call" | custom-call | tf_op jit(solution)/shard_map/last_sweeps/pallas_call | solution.py:791
  (17 shorter events, 0.0 us)
Async XLA Ops:
  0.6 54.5 %copy-start.1 = (bf16[128,1024]{1,0:T(8,128)(2,1)S(1)}, bf16[128,1024]{1,0:T(8,128)(2,1)}, u32[]{:S(2)}) copy-start(bf16[128,1024]{1,0:T(8,128)(2,1)} %constant.47.clone.spread_ref) | copy-start | bytes 786436
  0.6 42.1 %copy-start.7 = (f32[4,4,1024]{2,1,0:T(4,128)S(1)}, f32[4,4,1024]{2,1,0:T(4,128)}, u32[]{:S(2)}) copy-start(f32[4,4,1024]{2,1,0:T(4,128)} %pressure_ref.1) | copy-start | bytes 196612
  0.7 53.4 %copy-start.16 = (f32[3,2048]{1,0:T(4,128)S(1)}, f32[3,2048]{1,0:T(4,128)}, u32[]{:S(2)}) copy-start(f32[3,2048]{1,0:T(4,128)} %target_ref.1) | copy-start | bytes 73732
  0.7 53.4 %copy-start.12 = (f32[16,2048]{1,0:T(8,128)S(1)}, f32[16,2048]{1,0:T(8,128)}, u32[]{:S(2)}) copy-start(f32[16,2048]{1,0:T(8,128)} %weight_ref.1) | copy-start | bytes 393220
  0.7 53.4 %copy-start.20 = (f32[2048]{0:T(1024)S(1)}, f32[2048]{0:T(1024)}, u32[]{:S(2)}) copy-start(f32[2048]{0:T(1024)} %param.31) | copy-start | bytes 24580
  0.7 53.4 %copy-start.19 = (s32[2048]{0:T(1024)S(1)}, s32[2048]{0:T(1024)}, u32[]{:S(2)}) copy-start(s32[2048]{0:T(1024)} %param.30) | copy-start | bytes 24580
  0.7 53.4 %copy-start.11 = (s32[16,2048]{1,0:T(8,128)S(1)}, s32[16,2048]{1,0:T(8,128)}, u32[]{:S(2)}) copy-start(s32[16,2048]{1,0:T(8,128)} %cells_ref.1) | copy-start | bytes 393220
  0.7 53.4 %copy-start.18 = (s32[2048]{0:T(1024)S(1)}, s32[2048]{0:T(1024)}, u32[]{:S(2)}) copy-start(s32[2048]{0:T(1024)} %param.28) | copy-start | bytes 24580
  3.2 52.6 %copy-start.6 = (bf16[1024,128]{1,0:T(8,128)(2,1)S(1)}, bf16[1024,128]{1,0:T(8,128)(2,1)}, u32[]{:S(2)}) copy-start(bf16[1024,128]{1,0:T(8,128)(2,1)} %constant.46.clone.rim_any.edge_ref) | copy-start | bytes 786436
  3.2 52.6 %copy-start.17 = (s32[48,2]{0,1:T(2,128)S(1)}, s32[48,2]{0,1:T(2,128)}, u32[]{:S(2)}) copy-start(s32[48,2]{0,1:T(2,128)} %param.26) | copy-start | bytes 1156
  3.2 39.5 %all-to-all-start = ((f32[48,2,4,128]{3,2,1,0:T(4,128)}), f32[48,2,4,128]{3,2,1,0:T(4,128)S(1)}, u32[]{:S(2)}, u32[]{:S(2)}) async-start(f32[48,2,4,128]{3,2,1,0:T(4,128)} %bitcast.39), calls=%async_computation | async-start | bytes 393216 | tf_op jit(solution)/shard_map/all_to_all | solution.py:806
  28.9 26.3 %collective-permute-start.1 = (f32[4,16,1024]{2,1,0:T(8,128)S(1)}, f32[4,16,1024]{2,1,0:T(8,128)S(1)}, u32[]{:S(2)}, u32[]{:S(2)}) collective-permute-start(f32[4,16,1024]{2,1,0:T(8,128)S(1)} %copy.28.own_ref), channel_id=1, source_target_pairs={{0,15},{1,0},{2,1},{3,2},{4,3},{5,4},{6,5},{7,6},{8,7},{9,8},{10,9... | collective-permute-start | bytes 786440 | tf_op jit(solution)/shard_map/ppermute | solution.py:813
  33.6 21.6 %collective-permute-start = (f32[4,16,1024]{2,1,0:T(8,128)S(1)}, f32[4,16,1024]{2,1,0:T(8,128)S(1)}, u32[]{:S(2)}, u32[]{:S(2)}) collective-permute-start(f32[4,16,1024]{2,1,0:T(8,128)S(1)} %copy.28.own_ref), channel_id=1, source_target_pairs={{0,1},{1,2},{2,3},{3,4},{4,5},{5,6},{6,7},{7,8},{8,9},{9,10},{10,1... | collective-permute-start | bytes 786440 | tf_op jit(solution)/shard_map/ppermute | solution.py:812
  42.7 0.7 copy-start.14
  44.1 11.7 %collective-permute-start.2 = (f32[4,2176]{1,0:T(4,128)S(1)}, f32[4,2176]{1,0:T(4,128)S(1)}, u32[]{:S(2)}, u32[]{:S(2)}) collective-permute-start(f32[4,2176]{1,0:T(4,128)S(1)} %get-tuple-element.49), channel_id=1, source_target_pairs={{0,1},{1,2},{2,3},{3,4},{4,5},{5,6},{6,7},{7,8},{8,9},{9,10},{10,1... | collective-permute-start | bytes 104456 | tf_op jit(solution)/shard_map/ppermute | solution.py:812
  47.2 8.7 %collective-permute-start.3 = (f32[4,2176]{1,0:T(4,128)S(1)}, f32[4,2176]{1,0:T(4,128)S(1)}, u32[]{:S(2)}, u32[]{:S(2)}) collective-permute-start(f32[4,2176]{1,0:T(4,128)S(1)} %get-tuple-element.50), channel_id=1, source_target_pairs={{0,15},{1,0},{2,1},{3,2},{4,3},{5,4},{6,5},{7,6},{8,7},{9,8},{10,9... | collective-permute-start | bytes 104456 | tf_op jit(solution)/shard_map/ppermute | solution.py:813
  55.2 36.5 %copy-start.4 = (bf16[1024,640]{1,0:T(8,128)(2,1)S(1)}, bf16[1024,640]{1,0:T(8,128)(2,1)}, u32[]{:S(2)}) copy-start(bf16[1024,640]{1,0:T(8,128)(2,1)} %constant.49.clone.pack_ref) | copy-start | bytes 3932164
  55.2 36.5 %copy-start.5 = (bf16[1024,512]{1,0:T(8,128)(2,1)S(1)}, bf16[1024,512]{1,0:T(8,128)(2,1)}, u32[]{:S(2)}) copy-start(bf16[1024,512]{1,0:T(8,128)(2,1)} %constant.50.clone.pack_rhs_ref) | copy-start | bytes 3145732
  55.2 36.4 %copy-start.8 = (bf16[128,1024]{1,0:T(8,128)(2,1)S(1)}, bf16[128,1024]{1,0:T(8,128)(2,1)}, u32[]{:S(2)}) copy-start(bf16[128,1024]{1,0:T(8,128)(2,1)} %constant.48.clone.across_ref) | copy-start | bytes 786436
  55.2 36.4 %copy-start.15 = (s32[288]{0:T(512)S(1)}, s32[288]{0:T(512)}, u32[]{:S(2)}) copy-start(s32[288]{0:T(512)} %routes.1.route_ref) | copy-start | bytes 3460
  81.6 9.2 %collective-permute-start.4 = (f32[4,1024]{1,0:T(4,128)S(1)}, f32[4,1024]{1,0:T(4,128)S(1)}, u32[]{:S(2)}, u32[]{:S(2)}) collective-permute-start(f32[4,1024]{1,0:T(4,128)S(1)} %get-tuple-element.57), channel_id=1, source_target_pairs={{0,1},{1,2},{2,3},{3,4},{4,5},{5,6},{6,7},{7,8},{8,9},{9,10},{10,1... | collective-permute-start | bytes 49160 | tf_op jit(solution)/shard_map/ppermute | solution.py:812
  83.5 8.1 %collective-permute-start.5 = (f32[4,1024]{1,0:T(4,128)S(1)}, f32[4,1024]{1,0:T(4,128)S(1)}, u32[]{:S(2)}, u32[]{:S(2)}) collective-permute-start(f32[4,1024]{1,0:T(4,128)S(1)} %get-tuple-element.58), channel_id=1, source_target_pairs={{0,15},{1,0},{2,1},{3,2},{4,3},{5,4},{6,5},{7,6},{8,7},{9,8},{10,9... | collective-permute-start | bytes 49160 | tf_op jit(solution)/shard_map/ppermute | solution.py:813
  91.7 31.7 %copy-start = (bf16[640,1664]{1,0:T(8,128)(2,1)S(1)}, bf16[640,1664]{1,0:T(8,128)(2,1)}, u32[]{:S(2)}) copy-start(bf16[640,1664]{1,0:T(8,128)(2,1)} %constant.52.clone.place_ref) | copy-start | bytes 6389764
  91.7 31.7 %copy-start.3 = (bf16[512,1664]{1,0:T(8,128)(2,1)S(1)}, bf16[512,1664]{1,0:T(8,128)(2,1)}, u32[]{:S(2)}) copy-start(bf16[512,1664]{1,0:T(8,128)(2,1)} %constant.53.clone.place_rhs_ref) | copy-start | bytes 5111812
  123.3 16.5 %copy-start.2 = (bf16[1664,640]{1,0:T(8,128)(2,1)S(1)}, bf16[1664,640]{1,0:T(8,128)(2,1)}, u32[]{:S(2)}) copy-start(bf16[1664,640]{1,0:T(8,128)(2,1)} %constant.51.clone.pack_ref) | copy-start | bytes 6389764
  123.3 16.5 %copy-start.9 = (f32[8,1664]{1,0:T(8,128)S(1)}, f32[8,1664]{1,0:T(8,128)}, u32[]{:S(2)}) copy-start(f32[8,1664]{1,0:T(8,128)} %constant.55.clone.mask_ref) | copy-start | bytes 159748
  123.4 16.5 %copy-start.10 = (f32[8,1664]{1,0:T(8,128)S(1)}, f32[8,1664]{1,0:T(8,128)}, u32[]{:S(2)}) copy-start(f32[8,1664]{1,0:T(8,128)} %constant.54.clone.codes_ref) | copy-start | bytes 159748
  125.6 44.1 %copy-start.13 = (f32[8,1664]{1,0:T(8,128)S(1)}, f32[8,1664]{1,0:T(8,128)}, u32[]{:S(2)}) copy-start(f32[8,1664]{1,0:T(8,128)} %constant.56.clone.block_ref) | copy-start | bytes 159748
  125.6 13.3 %collective-permute-start.6 = (f32[7,4,1920]{2,1,0:T(4,128)S(1)}, f32[7,4,1920]{2,1,0:T(4,128)S(1)}, u32[]{:S(2)}, u32[]{:S(2)}) collective-permute-start(f32[7,4,1920]{2,1,0:T(4,128)S(1)} %get-tuple-element.64), channel_id=1, source_target_pairs={{0,1},{1,2},{2,3},{3,4},{4,5},{5,6},{6,7},{7,8},{8,9},{9,10},{10,1... | collective-permute-start | bytes 645128 | tf_op jit(solution)/shard_map/ppermute | solution.py:812
  127.7 12.1 %collective-permute-start.7 = (f32[7,4,1920]{2,1,0:T(4,128)S(1)}, f32[7,4,1920]{2,1,0:T(4,128)S(1)}, u32[]{:S(2)}, u32[]{:S(2)}) collective-permute-start(f32[7,4,1920]{2,1,0:T(4,128)S(1)} %get-tuple-element.65), channel_id=1, source_target_pairs={{0,15},{1,0},{2,1},{3,2},{4,3},{5,4},{6,5},{7,6},{8,7},{9,8},{10,9... | collective-permute-start | bytes 645128 | tf_op jit(solution)/shard_map/ppermute | solution.py:813
  171.1 11.4 %collective-permute-start.8 = (f32[4,4,1920]{2,1,0:T(4,128)S(1)}, f32[4,4,1920]{2,1,0:T(4,128)S(1)}, u32[]{:S(2)}, u32[]{:S(2)}) collective-permute-start(f32[4,4,1920]{2,1,0:T(4,128)S(1)} %get-tuple-element.71), channel_id=1, source_target_pairs={{0,1},{1,2},{2,3},{3,4},{4,5},{5,6},{6,7},{7,8},{8,9},{9,10},{10,1... | collective-permute-start | bytes 368648 | tf_op jit(solution)/shard_map/ppermute | solution.py:812
  173.1 10.3 %collective-permute-start.9 = (f32[4,4,1920]{2,1,0:T(4,128)S(1)}, f32[4,4,1920]{2,1,0:T(4,128)S(1)}, u32[]{:S(2)}, u32[]{:S(2)}) collective-permute-start(f32[4,4,1920]{2,1,0:T(4,128)S(1)} %get-tuple-element.72), channel_id=1, source_target_pairs={{0,15},{1,0},{2,1},{3,2},{4,3},{5,4},{6,5},{7,6},{8,7},{9,8},{10,9... | collective-permute-start | bytes 368648 | tf_op jit(solution)/shard_map/ppermute | solution.py:813

commit v4 on v3

--- a/solution.py
+++ b/solution.py
@@ -412,10 +412,10 @@
     return jnp.concatenate([x, x], axis=0)
 
 
-def first_unpack(route_ref, got_ref, p_ref, rim_ref, up_ref, down_ref):
+def first_unpack(recv_ref, got_ref, p_ref, rim_ref, up_ref, down_ref):
     lane = lane_ids(SZ)
     for block in range(NB):
-        strips = [strip_of(got_ref, route_ref, block, side, 0, 2) for side in range(4)]
+        strips = [got_ref[recv_ref[block, side]] for side in range(4)]
         for comp in range(4):
             value = jnp.zeros((SZ, LANES), F32)
             for side in range(4):
@@ -654,7 +654,7 @@
 
 
 def first_step(
-    route_ref, send_ref, got_ref, star_ref, pressure_ref, p_low_ref, p_high_ref, rim_ref, spread_ref,
+    recv_ref, send_ref, got_ref, star_ref, pressure_ref, p_low_ref, p_high_ref, rim_ref, spread_ref,
     low_ref, high_ref, across_ref, pack_ref, pack_rhs_ref,
     p_ref, rhs_ref, out_ref, half_ref, near_ref, table_ref, corner_ref, rhs_table_ref,
 ):
@@ -662,9 +662,9 @@
     lane = lane_ids(NB)
     for side in range(4):
         for block in range(NB):
-            edge = block * 4 + side
-            rows = got_ref[route_ref[2 * edge]]
-            near_ref[side, block : block + 1, :] = jnp.where(route_ref[2 * edge + 1] == 1, rows[1:2], rows[0:1])
+            entry = recv_ref[block, side]
+            rows = got_ref[entry // 2]
+            near_ref[side, block : block + 1, :] = jnp.where(entry % 2 == 1, rows[1:2], rows[0:1])
     beyond = []
     for layer in range(SZ):
         value = jnp.zeros((NB, LANES), F32)
@@ -884,7 +884,7 @@
     )
 
     edge = (NB, RIMS + CELLS)
-    rims, up, down = call(first_unpack, "first_unpack", [(SZ, 16, LANES), edge, edge], [], 1)(route, got, pressure)
+    rims, up, down = call(first_unpack, "first_unpack", [(SZ, 16, LANES), edge, edge], [], 1)(recv_slot, got, pressure)
     low, high = beside(up, down)
     tilde, total = call(own_layers, "own_layers", [flat, (16, 2 * group)], [], 0)(
         cells, cells_low, cells_high, rims, spread, weights_high, weights_low, spans
@@ -902,7 +902,7 @@
         first_step, "first_step", [rows, rows, (5 * count, SZ, LANES)],
         [vmem(SZ, 8, CELLS), vmem(4, NB, LANES), table, vmem(1, SZ, LANES), vmem(32, SZ, LANES)], 2,
     )(
-        route, send, got, star, pressure, low, high, rims, spread, star_low, star_high, across, pack_flat, pack_rhs
+        recv_slot, send, got, star, pressure, low, high, rims, spread, star_low, star_high, across, pack_flat, pack_rhs
     )
     got = trade(messages, count)
     edge = (SZ + REACH, NB, WIDTH + 2 * LANES)

time: 188 us -> 187 us (level)
  no operation moved by 1% of the time
where the time goes in v4:
time: 187 us; the launch traced here: 186 us
  blocking collectives  79.4 us (42%)
  starting transfers between devices  67.2 us (36%)
  Pallas kernels  21.8 us (12%)
  waiting for transfers between devices  14.6 us (8%)
    all_to_all x3, blocking collectives, trade(): lax.all_to_all(whole, 'chord', split_axis=0, concat_axis=0, tiled=True)  79.4 us
    ppermute x5, starting transfers between devices, beside(): lax.ppermute(down, 'span', [(i, (i + size - 1) % size) for i in range(siz...  34 us
    all_to_all x1, starting transfers between devices, trade(): lax.all_to_all(whole, 'chord', split_axis=0, concat_axis=0, tiled=True)  22.4 us
    pallas_call x9, Pallas kernels, run(): pl.pallas_call(kernel, name=name, out_shape=shapes, in_specs=[smem if at...  17.3 us
    ppermute x5, starting transfers between devices, beside(): low = lax.ppermute(up, 'span', [(i, (i + 1) % size) for i in range(size)])  10.9 us
    all_to_all x1, waiting for transfers between devices, trade(): lax.all_to_all(whole, 'chord', split_axis=0, concat_axis=0, tiled=True)  7.16 us
    ppermute x5, waiting for transfers between devices, beside(): low = lax.ppermute(up, 'span', [(i, (i + 1) % size) for i in range(size)])  4.83 us
  transfers between devices with their start and end apart: 11, of which 6 were waited for; matrix products, arithmetic and copies ran while one was open for 1% of the time, Pallas kernels for 2%

profile of v4, /device:TPU:1, one launch (start us, length us, event | category | flops | bytes accessed | tf_op | source)
XLA Modules:
  0.0 186.2 jit_solution(6478243357042690552)
XLA Ops:
  0.6 0.0 copy-start.1
  0.6 0.0 copy-start.7
  0.7 0.0 copy-start.17
  0.7 0.0 copy-start.14
  0.7 0.0 copy-start.12
  0.7 0.0 copy-start.20
  0.7 0.0 copy-start.19
  0.7 0.0 copy-start.11
  0.7 0.0 copy-start.18
  0.7 2.5 %first_pack.1 = f32[96,4,128]{2,1,0:T(4,128)} custom-call(s32[2,48]{1,0:T(2,128)} %bitcast.30, f32[12,4,1024]{2,1,0:T(4,128)} %bitcast.40, f32[4,4,1024]{2,1,0:T(4,128)} %pressure_ref.1, bf16[1024,128]{1,0:T(8,128)(2,1)} %constant.46.clone.rim_any.edge_ref), custom_call_target="tpu_custom_call" | custom-call | tf_op jit(solution)/shard_map/first_pack/pallas_call | solution.py:846
  3.3 0.0 copy-start.6
  3.3 0.0 copy-start.15
  3.3 22.4 %all-to-all-start = ((f32[48,2,4,128]{3,2,1,0:T(4,128)}), f32[48,2,4,128]{3,2,1,0:T(4,128)S(1)}, u32[]{:S(2)}, u32[]{:S(2)}) async-start(f32[48,2,4,128]{3,2,1,0:T(4,128)} %bitcast.39), calls=%async_computation | async-start | bytes 393216 | tf_op jit(solution)/shard_map/all_to_all | solution.py:806
  25.7 2.0 %routes.1.route_ref = s32[288]{0:T(512)} custom-call(s32[1]{0:T(128)} %bitcast.me_ref, s32[2,48]{1,0:T(2,128)} %bitcast.31, s32[4,4]{1,0:T(4,128)} %recv_ref.5), custom_call_target="tpu_custom_call" | custom-call | tf_op jit(solution)/shard_map/routes/pallas_call | solution.py:864
  27.7 1.0 pad_maximum_fusion
  28.8 0.2 copy.28.own_ref
  28.9 4.7 %collective-permute-start.1 = (f32[4,16,1024]{2,1,0:T(8,128)S(1)}, f32[4,16,1024]{2,1,0:T(8,128)S(1)}, u32[]{:S(2)}, u32[]{:S(2)}) collective-permute-start(f32[4,16,1024]{2,1,0:T(8,128)S(1)} %copy.28.own_ref), channel_id=1, source_target_pairs={{0,15},{1,0},{2,1},{3,2},{4,3},{5,4},{6,5},{7,6},{8,7},{9,8},{10,9... | collective-permute-start | bytes 786440 | tf_op jit(solution)/shard_map/ppermute | solution.py:813
  33.7 1.9 %collective-permute-start = (f32[4,16,1024]{2,1,0:T(8,128)S(1)}, f32[4,16,1024]{2,1,0:T(8,128)S(1)}, u32[]{:S(2)}, u32[]{:S(2)}) collective-permute-start(f32[4,16,1024]{2,1,0:T(8,128)S(1)} %copy.28.own_ref), channel_id=1, source_target_pairs={{0,1},{1,2},{2,3},{3,4},{4,5},{5,6},{6,7},{7,8},{8,9},{9,10},{10,1... | collective-permute-start | bytes 786440 | tf_op jit(solution)/shard_map/ppermute | solution.py:812
  35.6 7.2 %all-to-all-done = f32[48,2,4,128]{3,2,1,0:T(4,128)S(1)} async-done(((f32[48,2,4,128]{3,2,1,0:T(4,128)}), f32[48,2,4,128]{3,2,1,0:T(4,128)S(1)}, u32[]{:S(2)}, u32[]{:S(2)}) %all-to-all-start) | async-done | bytes 196640 | tf_op jit(solution)/shard_map/all_to_all | solution.py:806
  42.8 0.0 copy-done.7
  42.8 0.0 copy-done.17
  42.8 0.7 first_unpack.1
  43.5 3.1 %collective-permute-start.2 = (f32[4,2176]{1,0:T(4,128)S(1)}, f32[4,2176]{1,0:T(4,128)S(1)}, u32[]{:S(2)}, u32[]{:S(2)}) collective-permute-start(f32[4,2176]{1,0:T(4,128)S(1)} %get-tuple-element.49), channel_id=1, source_target_pairs={{0,1},{1,2},{2,3},{3,4},{4,5},{5,6},{6,7},{7,8},{8,9},{9,10},{10,1... | collective-permute-start | bytes 104456 | tf_op jit(solution)/shard_map/ppermute | solution.py:812
  46.5 6.1 %collective-permute-start.3 = (f32[4,2176]{1,0:T(4,128)S(1)}, f32[4,2176]{1,0:T(4,128)S(1)}, u32[]{:S(2)}, u32[]{:S(2)}) collective-permute-start(f32[4,2176]{1,0:T(4,128)S(1)} %get-tuple-element.50), channel_id=1, source_target_pairs={{0,15},{1,0},{2,1},{3,2},{4,3},{5,4},{6,5},{7,6},{8,7},{9,8},{10,9... | collective-permute-start | bytes 104456 | tf_op jit(solution)/shard_map/ppermute | solution.py:813
  52.7 0.1 pad_add_fusion.at_ref
  53.5 1.1 weigh.1
  54.5 0.0 collective-permute-done.1.high_ref
  54.5 0.0 collective-permute-done.low_ref
  54.6 0.0 copy-done.1
  54.6 0.0 copy-start.4
  54.6 0.0 copy-start.5
  54.6 0.0 copy-start.8
  54.6 0.6 own_layers.1
  55.2 0.0 collective-permute-done.2.rim_low_ref.p_low_ref
  55.2 0.0 collective-permute-done.3.rim_high_ref.p_high_ref
  55.2 2.5 %forcing.1 = (f32[4,16,1024]{2,1,0:T(8,128)S(1)}, f32[48,2,128]{2,1,0:T(2,128)S(1)}, f32[4,1024]{1,0:T(4,128)S(1)}, f32[4,1024]{1,0:T(4,128)S(1)}) custom-call(s32[2,48]{1,0:T(2,128)S(1)} %bitcast.32, s32[1]{0:T(128)S(6)} %copy.29.count_ref, f32[4,16,1024]{2,1,0:T(8,128)S(1)} %copy.28.own_ref, f32[4,16,1024]{2,1,0:T(8,128)S(1)} %collective-permute-done.low_ref, ...), custom_call_target="tpu_custom_call" | custom-call | tf_op jit(solution)/shard_map/forcing/pallas_call | solution.py:791
  57.7 23.2 %all_to_all.20 = f32[48,1,2,128]{3,2,1,0:T(2,128)S(1)} all-to-all(f32[48,1,2,128]{3,2,1,0:T(2,128)S(1)} %bitcast.29), channel_id=1, replica_groups=mesh['chord'=48,'span'=16] {'chord'}, dimensions={0} | all-to-all | bytes 98304 | tf_op jit(solution)/shard_map/all_to_all | solution.py:806
  80.9 1.9 %collective-permute-start.4 = (f32[4,1024]{1,0:T(4,128)S(1)}, f32[4,1024]{1,0:T(4,128)S(1)}, u32[]{:S(2)}, u32[]{:S(2)}) collective-permute-start(f32[4,1024]{1,0:T(4,128)S(1)} %get-tuple-element.57), channel_id=1, source_target_pairs={{0,1},{1,2},{2,3},{3,4},{4,5},{5,6},{6,7},{7,8},{8,9},{9,10},{10,1... | collective-permute-start | bytes 49160 | tf_op jit(solution)/shard_map/ppermute | solution.py:812
  82.9 7.3 %collective-permute-start.5 = (f32[4,1024]{1,0:T(4,128)S(1)}, f32[4,1024]{1,0:T(4,128)S(1)}, u32[]{:S(2)}, u32[]{:S(2)}) collective-permute-start(f32[4,1024]{1,0:T(4,128)S(1)} %get-tuple-element.58), channel_id=1, source_target_pairs={{0,15},{1,0},{2,1},{3,2},{4,3},{5,4},{6,5},{7,6},{8,7},{9,8},{10,9... | collective-permute-start | bytes 49160 | tf_op jit(solution)/shard_map/ppermute | solution.py:813
  90.1 0.0 collective-permute-done.4.low_ref
  90.1 0.8 collective-permute-done.5.high_ref
  91.0 0.0 copy-start.3
  91.0 0.0 copy-start.16
  91.0 1.9 %first_step.1 = (f32[4,4,1024]{2,1,0:T(4,128)S(1)}, f32[4,4,1024]{2,1,0:T(4,128)S(1)}, f32[240,4,128]{2,1,0:T(4,128)S(1)}) custom-call(s32[4,4]{1,0:T(4,128)S(1)} %copy-done.17, s32[2,48]{1,0:T(2,128)S(1)} %bitcast.33, f32[48,2,128]{2,1,0:T(2,128)S(1)} %bitcast.28, f32[4,16,1024]{2,1,0:T(8,128)S(1)} %get-tuple-element.56.star_ref, ...), custom_call_target="tpu_custom_call" | custom-call | tf_op jit(solution)/shard_map/first_step/pallas_call | solution.py:791
  93.0 29.8 %all_to_all.21 = f32[48,5,4,128]{3,2,1,0:T(4,128)S(1)} all-to-all(f32[48,5,4,128]{3,2,1,0:T(4,128)S(1)} %bitcast.26), channel_id=1, replica_groups=mesh['chord'=48,'span'=16] {'chord'}, dimensions={0} | all-to-all | bytes 983040 | tf_op jit(solution)/shard_map/all_to_all | solution.py:806
  122.8 0.0 copy-done
  122.8 0.0 copy-start.2
  122.8 0.0 copy-start.9
  122.8 0.0 copy-start.10
  122.8 2.3 %middle_unpack.1 = (f32[4,8,1664]{2,1,0:T(8,128)S(1)}, f32[4,8,128]{2,1,0:T(8,128)S(1)}, f32[4,8,1664]{2,1,0:T(8,128)S(1)}, f32[7,4,1920]{2,1,0:T(4,128)S(1)}, f32[7,4,1920]{2,1,0:T(4,128)S(1)}) custom-call(s32[288]{0:T(512)S(1)} %copy-done.16, f32[240,4,128]{2,1,0:T(4,128)S(1)} %bitcast.23, f32[4,4,1024]{2,1,0:T(4,128)S(1)} %get-tuple-element.60.p_ref, ...), custom_call_target="tpu_custom_call" | custom-call | tf_op jit(solution)/shard_map/middle_unpack/pallas_call | solution.py:791
  125.1 0.0 copy-start.13
  125.1 2.1 %collective-permute-start.6 = (f32[7,4,1920]{2,1,0:T(4,128)S(1)}, f32[7,4,1920]{2,1,0:T(4,128)S(1)}, u32[]{:S(2)}, u32[]{:S(2)}) collective-permute-start(f32[7,4,1920]{2,1,0:T(4,128)S(1)} %get-tuple-element.64), channel_id=1, source_target_pairs={{0,1},{1,2},{2,3},{3,4},{4,5},{5,6},{6,7},{7,8},{8,9},{9,10},{10,1... | collective-permute-start | bytes 645128 | tf_op jit(solution)/shard_map/ppermute | solution.py:812
  127.1 7.8 %collective-permute-start.7 = (f32[7,4,1920]{2,1,0:T(4,128)S(1)}, f32[7,4,1920]{2,1,0:T(4,128)S(1)}, u32[]{:S(2)}, u32[]{:S(2)}) collective-permute-start(f32[7,4,1920]{2,1,0:T(4,128)S(1)} %get-tuple-element.65), channel_id=1, source_target_pairs={{0,15},{1,0},{2,1},{3,2},{4,3},{5,4},{6,5},{7,6},{8,7},{9,8},{10,9... | collective-permute-start | bytes 645128 | tf_op jit(solution)/shard_map/ppermute | solution.py:813
  135.0 3.4 %collective-permute-done.6.low_ref = f32[7,4,1920]{2,1,0:T(4,128)S(1)} collective-permute-done((f32[7,4,1920]{2,1,0:T(4,128)S(1)}, f32[7,4,1920]{2,1,0:T(4,128)S(1)}, u32[]{:S(2)}, u32[]{:S(2)}) %collective-permute-start.6) | collective-permute-done | bytes 215072 | tf_op jit(solution)/shard_map/ppermute | solution.py:812
  138.4 0.9 collective-permute-done.7.high_ref
  139.2 0.0 copy-done.9
  139.3 3.5 %middle_sweeps.1 = (f32[4,8,1664]{2,1,0:T(8,128)S(1)}, f32[10,8,1664]{2,1,0:T(8,128)S(1)}, f32[144,4,128]{2,1,0:T(4,128)S(1)}) custom-call(s32[2,48]{1,0:T(2,128)S(1)} %bitcast.34, f32[4,8,1664]{2,1,0:T(8,128)S(1)} %get-tuple-element.62.own_ref, f32[4,8,128]{2,1,0:T(8,128)S(1)} %get-tuple-element.63.fan_ref.old_ref, ...), custom_call_target="tpu_custom_call" | custom-call | tf_op jit(solution)/shard_map/middle_sweeps/pallas_call | solution.py:791
  142.7 26.4 %all_to_all.22 = f32[48,3,4,128]{3,2,1,0:T(4,128)S(1)} all-to-all(f32[48,3,4,128]{3,2,1,0:T(4,128)S(1)} %bitcast.27), channel_id=1, replica_groups=mesh['chord'=48,'span'=16] {'chord'}, dimensions={0} | all-to-all | bytes 589824 | tf_op jit(solution)/shard_map/all_to_all | solution.py:806
  169.2 1.4 last_unpack.1
  170.6 1.9 %collective-permute-start.8 = (f32[4,4,1920]{2,1,0:T(4,128)S(1)}, f32[4,4,1920]{2,1,0:T(4,128)S(1)}, u32[]{:S(2)}, u32[]{:S(2)}) collective-permute-start(f32[4,4,1920]{2,1,0:T(4,128)S(1)} %get-tuple-element.71), channel_id=1, source_target_pairs={{0,1},{1,2},{2,3},{3,4},{4,5},{5,6},{6,7},{7,8},{8,9},{9,10},{10,1... | collective-permute-start | bytes 368648 | tf_op jit(solution)/shard_map/ppermute | solution.py:812
  172.5 8.0 %collective-permute-start.9 = (f32[4,4,1920]{2,1,0:T(4,128)S(1)}, f32[4,4,1920]{2,1,0:T(4,128)S(1)}, u32[]{:S(2)}, u32[]{:S(2)}) collective-permute-start(f32[4,4,1920]{2,1,0:T(4,128)S(1)} %get-tuple-element.72), channel_id=1, source_target_pairs={{0,15},{1,0},{2,1},{3,2},{4,3},{5,4},{6,5},{7,6},{8,7},{9,8},{10,9... | collective-permute-start | bytes 368648 | tf_op jit(solution)/shard_map/ppermute | solution.py:813
  180.5 1.4 collective-permute-done.8.low_ref
  182.0 0.9 collective-permute-done.9.high_ref
  182.8 3.3 %last_sweeps.1 = (f32[12,4,1024]{2,1,0:T(4,128)}, f32[4,4,1024]{2,1,0:T(4,128)}) custom-call(f32[4,8,1664]{2,1,0:T(8,128)S(1)} %get-tuple-element.69.own_ref, f32[4,8,128]{2,1,0:T(8,128)S(1)} %get-tuple-element.70.fan_ref, f32[4,4,1920]{2,1,0:T(4,128)S(1)} %collective-permute-done.8.low_ref, f32[4,4,1920]{2,1,0:T(4,128)S(1)} %collective-permute-done.9.high_ref, ...), custom_call_target="tpu_custom_call" | custom-call | tf_op jit(solution)/shard_map/last_sweeps/pallas_call | solution.py:791
  (17 shorter events, 0.0 us)
Async XLA Ops:
  0.6 53.9 %copy-start.1 = (bf16[128,1024]{1,0:T(8,128)(2,1)S(1)}, bf16[128,1024]{1,0:T(8,128)(2,1)}, u32[]{:S(2)}) copy-start(bf16[128,1024]{1,0:T(8,128)(2,1)} %constant.47.clone.spread_ref) | copy-start | bytes 786436
  0.6 42.1 %copy-start.7 = (f32[4,4,1024]{2,1,0:T(4,128)S(1)}, f32[4,4,1024]{2,1,0:T(4,128)}, u32[]{:S(2)}) copy-start(f32[4,4,1024]{2,1,0:T(4,128)} %pressure_ref.1) | copy-start | bytes 196612
  0.7 42.1 %copy-start.17 = (s32[4,4]{1,0:T(4,128)S(1)}, s32[4,4]{1,0:T(4,128)}, u32[]{:S(2)}) copy-start(s32[4,4]{1,0:T(4,128)} %recv_ref.5) | copy-start | bytes 196
  0.7 52.7 %copy-start.14 = (f32[3,2048]{1,0:T(4,128)S(1)}, f32[3,2048]{1,0:T(4,128)}, u32[]{:S(2)}) copy-start(f32[3,2048]{1,0:T(4,128)} %target_ref.1) | copy-start | bytes 73732
  0.7 52.7 %copy-start.12 = (f32[16,2048]{1,0:T(8,128)S(1)}, f32[16,2048]{1,0:T(8,128)}, u32[]{:S(2)}) copy-start(f32[16,2048]{1,0:T(8,128)} %weight_ref.1) | copy-start | bytes 393220
  0.7 52.7 %copy-start.20 = (f32[2048]{0:T(1024)S(1)}, f32[2048]{0:T(1024)}, u32[]{:S(2)}) copy-start(f32[2048]{0:T(1024)} %param.31) | copy-start | bytes 24580
  0.7 52.7 %copy-start.19 = (s32[2048]{0:T(1024)S(1)}, s32[2048]{0:T(1024)}, u32[]{:S(2)}) copy-start(s32[2048]{0:T(1024)} %param.30) | copy-start | bytes 24580
  0.7 52.7 %copy-start.11 = (s32[16,2048]{1,0:T(8,128)S(1)}, s32[16,2048]{1,0:T(8,128)}, u32[]{:S(2)}) copy-start(s32[16,2048]{1,0:T(8,128)} %cells_ref.1) | copy-start | bytes 393220
  0.7 52.7 %copy-start.18 = (s32[2048]{0:T(1024)S(1)}, s32[2048]{0:T(1024)}, u32[]{:S(2)}) copy-start(s32[2048]{0:T(1024)} %param.28) | copy-start | bytes 24580
  3.3 51.9 %copy-start.6 = (bf16[1024,128]{1,0:T(8,128)(2,1)S(1)}, bf16[1024,128]{1,0:T(8,128)(2,1)}, u32[]{:S(2)}) copy-start(bf16[1024,128]{1,0:T(8,128)(2,1)} %constant.46.clone.rim_any.edge_ref) | copy-start | bytes 786436
  3.3 51.9 %copy-start.15 = (s32[48,2]{0,1:T(2,128)S(1)}, s32[48,2]{0,1:T(2,128)}, u32[]{:S(2)}) copy-start(s32[48,2]{0,1:T(2,128)} %param.26) | copy-start | bytes 1156
  3.3 39.5 %all-to-all-start = ((f32[48,2,4,128]{3,2,1,0:T(4,128)}), f32[48,2,4,128]{3,2,1,0:T(4,128)S(1)}, u32[]{:S(2)}, u32[]{:S(2)}) async-start(f32[48,2,4,128]{3,2,1,0:T(4,128)} %bitcast.39), calls=%async_computation | async-start | bytes 393216 | tf_op jit(solution)/shard_map/all_to_all | solution.py:806
  28.9 25.6 %collective-permute-start.1 = (f32[4,16,1024]{2,1,0:T(8,128)S(1)}, f32[4,16,1024]{2,1,0:T(8,128)S(1)}, u32[]{:S(2)}, u32[]{:S(2)}) collective-permute-start(f32[4,16,1024]{2,1,0:T(8,128)S(1)} %copy.28.own_ref), channel_id=1, source_target_pairs={{0,15},{1,0},{2,1},{3,2},{4,3},{5,4},{6,5},{7,6},{8,7},{9,8},{10,9... | collective-permute-start | bytes 786440 | tf_op jit(solution)/shard_map/ppermute | solution.py:813
  33.7 20.9 %collective-permute-start = (f32[4,16,1024]{2,1,0:T(8,128)S(1)}, f32[4,16,1024]{2,1,0:T(8,128)S(1)}, u32[]{:S(2)}, u32[]{:S(2)}) collective-permute-start(f32[4,16,1024]{2,1,0:T(8,128)S(1)} %copy.28.own_ref), channel_id=1, source_target_pairs={{0,1},{1,2},{2,3},{3,4},{4,5},{5,6},{6,7},{7,8},{8,9},{9,10},{10,1... | collective-permute-start | bytes 786440 | tf_op jit(solution)/shard_map/ppermute | solution.py:812
  43.5 11.7 %collective-permute-start.2 = (f32[4,2176]{1,0:T(4,128)S(1)}, f32[4,2176]{1,0:T(4,128)S(1)}, u32[]{:S(2)}, u32[]{:S(2)}) collective-permute-start(f32[4,2176]{1,0:T(4,128)S(1)} %get-tuple-element.49), channel_id=1, source_target_pairs={{0,1},{1,2},{2,3},{3,4},{4,5},{5,6},{6,7},{7,8},{8,9},{9,10},{10,1... | collective-permute-start | bytes 104456 | tf_op jit(solution)/shard_map/ppermute | solution.py:812
  46.5 8.7 %collective-permute-start.3 = (f32[4,2176]{1,0:T(4,128)S(1)}, f32[4,2176]{1,0:T(4,128)S(1)}, u32[]{:S(2)}, u32[]{:S(2)}) collective-permute-start(f32[4,2176]{1,0:T(4,128)S(1)} %get-tuple-element.50), channel_id=1, source_target_pairs={{0,15},{1,0},{2,1},{3,2},{4,3},{5,4},{6,5},{7,6},{8,7},{9,8},{10,9... | collective-permute-start | bytes 104456 | tf_op jit(solution)/shard_map/ppermute | solution.py:813
  54.6 36.4 %copy-start.4 = (bf16[1024,640]{1,0:T(8,128)(2,1)S(1)}, bf16[1024,640]{1,0:T(8,128)(2,1)}, u32[]{:S(2)}) copy-start(bf16[1024,640]{1,0:T(8,128)(2,1)} %constant.49.clone.pack_ref) | copy-start | bytes 3932164
  54.6 36.4 %copy-start.5 = (bf16[1024,512]{1,0:T(8,128)(2,1)S(1)}, bf16[1024,512]{1,0:T(8,128)(2,1)}, u32[]{:S(2)}) copy-start(bf16[1024,512]{1,0:T(8,128)(2,1)} %constant.50.clone.pack_rhs_ref) | copy-start | bytes 3145732
  54.6 36.4 %copy-start.8 = (bf16[128,1024]{1,0:T(8,128)(2,1)S(1)}, bf16[128,1024]{1,0:T(8,128)(2,1)}, u32[]{:S(2)}) copy-start(bf16[128,1024]{1,0:T(8,128)(2,1)} %constant.48.clone.across_ref) | copy-start | bytes 786436
  80.9 9.2 %collective-permute-start.4 = (f32[4,1024]{1,0:T(4,128)S(1)}, f32[4,1024]{1,0:T(4,128)S(1)}, u32[]{:S(2)}, u32[]{:S(2)}) collective-permute-start(f32[4,1024]{1,0:T(4,128)S(1)} %get-tuple-element.57), channel_id=1, source_target_pairs={{0,1},{1,2},{2,3},{3,4},{4,5},{5,6},{6,7},{7,8},{8,9},{9,10},{10,1... | collective-permute-start | bytes 49160 | tf_op jit(solution)/shard_map/ppermute | solution.py:812
  82.9 8.1 %collective-permute-start.5 = (f32[4,1024]{1,0:T(4,128)S(1)}, f32[4,1024]{1,0:T(4,128)S(1)}, u32[]{:S(2)}, u32[]{:S(2)}) collective-permute-start(f32[4,1024]{1,0:T(4,128)S(1)} %get-tuple-element.58), channel_id=1, source_target_pairs={{0,15},{1,0},{2,1},{3,2},{4,3},{5,4},{6,5},{7,6},{8,7},{9,8},{10,9... | collective-permute-start | bytes 49160 | tf_op jit(solution)/shard_map/ppermute | solution.py:813
  91.0 31.8 %copy-start = (bf16[640,1664]{1,0:T(8,128)(2,1)S(1)}, bf16[640,1664]{1,0:T(8,128)(2,1)}, u32[]{:S(2)}) copy-start(bf16[640,1664]{1,0:T(8,128)(2,1)} %constant.52.clone.place_ref) | copy-start | bytes 6389764
  91.0 31.8 %copy-start.3 = (bf16[512,1664]{1,0:T(8,128)(2,1)S(1)}, bf16[512,1664]{1,0:T(8,128)(2,1)}, u32[]{:S(2)}) copy-start(bf16[512,1664]{1,0:T(8,128)(2,1)} %constant.53.clone.place_rhs_ref) | copy-start | bytes 5111812
  91.0 31.7 %copy-start.16 = (s32[288]{0:T(512)S(1)}, s32[288]{0:T(512)}, u32[]{:S(2)}) copy-start(s32[288]{0:T(512)} %routes.1.route_ref) | copy-start | bytes 3460
  122.8 16.5 %copy-start.2 = (bf16[1664,640]{1,0:T(8,128)(2,1)S(1)}, bf16[1664,640]{1,0:T(8,128)(2,1)}, u32[]{:S(2)}) copy-start(bf16[1664,640]{1,0:T(8,128)(2,1)} %constant.51.clone.pack_ref) | copy-start | bytes 6389764
  122.8 16.5 %copy-start.9 = (f32[8,1664]{1,0:T(8,128)S(1)}, f32[8,1664]{1,0:T(8,128)}, u32[]{:S(2)}) copy-start(f32[8,1664]{1,0:T(8,128)} %constant.55.clone.mask_ref) | copy-start | bytes 159748
  122.8 16.5 %copy-start.10 = (f32[8,1664]{1,0:T(8,128)S(1)}, f32[8,1664]{1,0:T(8,128)}, u32[]{:S(2)}) copy-start(f32[8,1664]{1,0:T(8,128)} %constant.54.clone.codes_ref) | copy-start | bytes 159748
  125.1 44.1 %copy-start.13 = (f32[8,1664]{1,0:T(8,128)S(1)}, f32[8,1664]{1,0:T(8,128)}, u32[]{:S(2)}) copy-start(f32[8,1664]{1,0:T(8,128)} %constant.56.clone.block_ref) | copy-start | bytes 159748
  125.1 13.3 %collective-permute-start.6 = (f32[7,4,1920]{2,1,0:T(4,128)S(1)}, f32[7,4,1920]{2,1,0:T(4,128)S(1)}, u32[]{:S(2)}, u32[]{:S(2)}) collective-permute-start(f32[7,4,1920]{2,1,0:T(4,128)S(1)} %get-tuple-element.64), channel_id=1, source_target_pairs={{0,1},{1,2},{2,3},{3,4},{4,5},{5,6},{6,7},{7,8},{8,9},{9,10},{10,1... | collective-permute-start | bytes 645128 | tf_op jit(solution)/shard_map/ppermute | solution.py:812
  127.1 12.1 %collective-permute-start.7 = (f32[7,4,1920]{2,1,0:T(4,128)S(1)}, f32[7,4,1920]{2,1,0:T(4,128)S(1)}, u32[]{:S(2)}, u32[]{:S(2)}) collective-permute-start(f32[7,4,1920]{2,1,0:T(4,128)S(1)} %get-tuple-element.65), channel_id=1, source_target_pairs={{0,15},{1,0},{2,1},{3,2},{4,3},{5,4},{6,5},{7,6},{8,7},{9,8},{10,9... | collective-permute-start | bytes 645128 | tf_op jit(solution)/shard_map/ppermute | solution.py:813
  170.6 11.4 %collective-permute-start.8 = (f32[4,4,1920]{2,1,0:T(4,128)S(1)}, f32[4,4,1920]{2,1,0:T(4,128)S(1)}, u32[]{:S(2)}, u32[]{:S(2)}) collective-permute-start(f32[4,4,1920]{2,1,0:T(4,128)S(1)} %get-tuple-element.71), channel_id=1, source_target_pairs={{0,1},{1,2},{2,3},{3,4},{4,5},{5,6},{6,7},{7,8},{8,9},{9,10},{10,1... | collective-permute-start | bytes 368648 | tf_op jit(solution)/shard_map/ppermute | solution.py:812
  172.5 10.3 %collective-permute-start.9 = (f32[4,4,1920]{2,1,0:T(4,128)S(1)}, f32[4,4,1920]{2,1,0:T(4,128)S(1)}, u32[]{:S(2)}, u32[]{:S(2)}) collective-permute-start(f32[4,4,1920]{2,1,0:T(4,128)S(1)} %get-tuple-element.72), channel_id=1, source_target_pairs={{0,15},{1,0},{2,1},{3,2},{4,3},{5,4},{6,5},{7,6},{8,7},{9,8},{10,9... | collective-permute-start | bytes 368648 | tf_op jit(solution)/shard_map/ppermute | solution.py:813
